TPU v7x, 1024 devices: a whole 8x8x8 slice. The times are simulated.
1024 devices in a mesh: lon: 128 (over y, x_lo, z), lat: 8 (over x_hi, core).
Axes of the slice: x: 8 (x_hi: 4, x_lo: 2; x = x_hi * 2 + x_lo), y: 8, z: 8, core: 2. Of those that a mesh axis runs over, the one named last changes fastest.
Arguments:
- zonal_flow_speed: float32 [62, 1024, 1024], P(None, 'lon', 'lat'), may hold values from -6 to 6
- meridional_flow_speed: float32 [62, 1024, 1024], P(None, 'lon', 'lat'), may hold values from -6 to 6
- first_scalar_concentration: float32 [62, 1024, 1024], P(None, 'lon', 'lat'), may hold values from -6 to 6
- second_scalar_concentration: float32 [62, 1024, 1024], P(None, 'lon', 'lat'), may hold values from -6 to 6
- water_point_indicator: int32 [1024, 1024], P('lon', 'lat'), may hold values 0 or 1
- water_layers_per_point: int32 [1024, 1024], P('lon', 'lat'), may hold values from 1 to 62
- elevation_operator_main_entry: float32 [1024, 1024], P('lon', 'lat'), may hold values from 0.02 to 0.2
- earlier_free_elevation: float32 [1024, 1024], P('lon', 'lat'), may hold values from -6 to 6
Outputs:
- zonal_next: float32 [62, 1024, 1024], P(None, 'lon', 'lat')
- meridional_next: float32 [62, 1024, 1024], P(None, 'lon', 'lat')
- temperature_next: float32 [62, 1024, 1024], P(None, 'lon', 'lat')
- salinity_next: float32 [62, 1024, 1024], P(None, 'lon', 'lat')
- surface_height: float32 [1024, 1024], P('lon', 'lat')
Inputs may be any that keep to these rules, and one draw needn't show every extreme that they name: `water_layers_per_point`: every column has at least one and at most 62 levels.
All inputs are finite; a program needn't handle non-finite values. No bound on the sum of `water_point_indicator` on one device may be relied on, other than what follows from the above.
Results may differ from a plain program's by a relative error of at most 0.000026.
Values sent between devices are 32-bit elements; how exact they have to be, the bound alone decides.
No kernel may reach another device: no remote copies, remote signals or barrier semaphores. Data moves between devices by JAX's collectives and lax.ppermute only.
A program may use at most 32 MiB of HBM per device.

v0:
```python
import jax
import jax.numpy as jnp
from jax import lax
from jax.sharding import PartitionSpec as P

ITERS = 8


spectrum_mid = 1.0
spectrum_half = 0.995


def extended_2(array, sides, width):
    for axis, dim in sides:
        size, length = (lax.axis_size(axis), array.shape[dim])
        up = [(i, (i + 1) % size) for i in range(size)]
        down = [(j, i) for i, j in up]
        last = lax.slice_in_dim(array, length - width, length, axis=dim)
        initial = lax.slice_in_dim(array, 0, width, axis=dim)
        before = lax.ppermute(last, axis, up)
        after = lax.ppermute(initial, axis, down)
        array = jnp.concatenate([before, array, after], axis=dim)
    return array


def keep_inner(length, margin):
    position = lax.axis_index("lat")
    last_index = lax.axis_size("lat") - 1
    column = lax.broadcasted_iota(jnp.int32, (length,), 0)
    outside = (column < margin) & (position == 0) | (column >= length - margin) & (
        position == last_index
    )
    return jnp.where(outside, 0.0, 1.0).astype(jnp.float32)


def chebyshev(summed_fn, rhs, start, damping, shade):
    sigma = spectrum_mid / spectrum_half
    ratio = 1.0 / sigma
    diagonal = damping + 4.0
    inverse = 1.0 / diagonal
    residual = rhs
    previous = start
    iterate = start
    for step in range(ITERS):
        residual = residual - (diagonal * previous - shade * summed_fn(shade * previous))
        if step == 0:
            direction = residual * inverse / spectrum_mid
        else:
            following = 1.0 / (2.0 * sigma - ratio)
            direction = (
                following * ratio * previous + 2.0 * following / spectrum_half * residual * inverse
            )
            ratio = following
        iterate = iterate + direction
        previous = direction
    return iterate


def on_device(
    zonal_flow_speed,
    meridional_flow_speed,
    first_scalar_concentration,
    second_scalar_concentration,
    water_point_indicator,
    water_layers_per_point,
    elevation_operator_main_entry,
    earlier_free_elevation,
):
    shade = water_point_indicator.astype(jnp.float32)
    depth = lax.broadcasted_iota(jnp.int32, zonal_flow_speed.shape, 0)
    ocean_cell_mask = shade[None] * (depth < water_layers_per_point[None]).astype(jnp.float32)
    stacked_fields = (
        jnp.stack(
            [
                zonal_flow_speed,
                meridional_flow_speed,
                first_scalar_concentration,
                second_scalar_concentration,
            ]
        )
        * ocean_cell_mask[None]
    )
    padded = extended_2(stacked_fields, (("lon", 2), ("lat", 3)), 2)
    padded = padded * keep_inner(padded.shape[3], 2)
    rows = stacked_fields.shape[2]
    columns = stacked_fields.shape[3]
    center = padded[:, :, 2 : 2 + rows, 2 : 2 + columns]

    def along_lon(shift):
        return padded[:, :, 2 + shift : 2 + shift + rows, 2 : 2 + columns]

    def along_lat(shift):
        return padded[:, :, 2 : 2 + rows, 2 + shift : 2 + shift + columns]

    grad_lon = (8.0 * (along_lon(1) - along_lon(-1)) - (along_lon(2) - along_lon(-2))) / 12.0
    grad_lat = (8.0 * (along_lat(1) - along_lat(-1)) - (along_lat(2) - along_lat(-2))) / 12.0
    laplace = along_lon(1) + along_lon(-1) + along_lat(1) + along_lat(-1) - 4.0 * center
    vertical_pad = jnp.pad(center, ((0, 0), (1, 1), (0, 0), (0, 0)))
    vertical = vertical_pad[:, 2:] + vertical_pad[:, :-2] - 2.0 * center
    tendency = -(center[0:1] * grad_lon + center[1:2] * grad_lat) + 0.05 * laplace + 0.2 * vertical
    fresh = ocean_cell_mask[None] * (center + 0.1 * tendency)
    forcing = 0.1 * jnp.sum(0.7 * fresh[2] - 0.5 * fresh[3], axis=0)
    rhs = earlier_free_elevation + forcing

    def summed_tile(shaded):
        extended = extended_2(shaded, (("lon", 0), ("lat", 1)), 1)
        extended = extended * keep_inner(extended.shape[1], 1)
        return extended[2:, 1:-1] + extended[:-2, 1:-1] + extended[1:-1, 2:] + extended[1:-1, :-2]

    height = chebyshev(
        summed_tile, rhs, earlier_free_elevation, elevation_operator_main_entry, shade
    )
    return (fresh[0], fresh[1], fresh[2], fresh[3], height)


def solution(mesh):
    return jax.shard_map(
        on_device,
        mesh=mesh,
        in_specs=(
            P(None, "lon", "lat"),
            P(None, "lon", "lat"),
            P(None, "lon", "lat"),
            P(None, "lon", "lat"),
            P("lon", "lat"),
            P("lon", "lat"),
            P("lon", "lat"),
            P("lon", "lat"),
        ),
        out_specs=(
            P(None, "lon", "lat"),
            P(None, "lon", "lat"),
            P(None, "lon", "lat"),
            P(None, "lon", "lat"),
            P("lon", "lat"),
        ),
        check_vma=False,
    )
```

profile of v0, /device:TPU:5, one launch (start us, length us, event | category | flops | bytes accessed | tf_op | source)
XLA Modules:
  0.0 226.6 jit_solution(994118661007671205)
XLA Ops:
  3.7 4.9 %collective-permute-start = (f32[4,62,2,128]{3,2,1,0:T(2,128)S(1)}, f32[4,62,2,128]{3,2,1,0:T(2,128)S(1)}, u32[]{:S(2)}, u32[]{:S(2)}) collective-permute-start(f32[4,62,2,128]{3,2,1,0:T(2,128)S(1)} %get-tuple-element.30), channel_id=1, source_target_pairs={{0,8},{8,16},{16,24},{24,32},{32,40},{40,48},{48,56},{56,64},{64,7... | collective-permute-start | bytes 761864 | tf_op jit(solution)/shard_map/ppermute | solution.py:20
  8.6 18.7 %collective-permute-start.1 = (f32[4,62,2,128]{3,2,1,0:T(2,128)S(1)}, f32[4,62,2,128]{3,2,1,0:T(2,128)S(1)}, u32[]{:S(2)}, u32[]{:S(2)}) collective-permute-start(f32[4,62,2,128]{3,2,1,0:T(2,128)S(1)} %get-tuple-element.31), channel_id=1, source_target_pairs={{8,0},{16,8},{24,16},{32,24},{40,32},{48,40},{56,48},{64,56},{72,6... | collective-permute-start | bytes 761864 | tf_op jit(solution)/shard_map/ppermute | solution.py:21
  29.3 7.6 %collective-permute-start.5 = (f32[1,128]{1,0:T(1,128)S(1)}, f32[1,128]{1,0:T(1,128)S(1)}, u32[]{:S(2)}, u32[]{:S(2)}) collective-permute-start(f32[1,128]{1,0:T(1,128)S(1)} %get-tuple-element.63), channel_id=1, source_target_pairs={{8,0},{16,8},{24,16},{32,24},{40,32},{48,40},{56,48},{64,56},{72,6... | collective-permute-start | bytes 1544 | tf_op jit(solution)/shard_map/ppermute | solution.py:21
  38.7 5.9 %collective-permute-start.6 = (f32[10,1]{1,0:T(8,128)}, f32[10,1]{1,0:T(8,128)}, u32[]{:S(2)}, u32[]{:S(2)}) collective-permute-start(f32[10,1]{1,0:T(8,128)} %get-tuple-element.46), channel_id=1, source_target_pairs={{0,1},{1,2},{2,3},{3,4},{4,5},{5,6},{6,7},{7,0},{8,9},{9,10},{10,1... | collective-permute-start | bytes 128 | tf_op jit(solution)/shard_map/ppermute | solution.py:20
  49.6 3.0 %copy.36 = f32[4,62,12,2]{1,0,3,2:T(4,128)} copy(f32[4,62,12,2]{3,2,1,0:T(8,128)} %get-tuple-element.26) | data formatting | bytes 47616 | tf_op jit(solution)/shard_map/slice | solution.py:18
  52.6 5.7 %collective-permute-start.2 = (f32[4,62,12,2]{1,0,3,2:T(4,128)}, f32[4,62,12,2]{1,0,3,2:T(4,128)}, u32[]{:S(2)}, u32[]{:S(2)}) collective-permute-start(f32[4,62,12,2]{1,0,3,2:T(4,128)} %copy.36), channel_id=1, source_target_pairs={{0,1},{1,2},{2,3},{3,4},{4,5},{5,6},{6,7},{7,0},{8,9},{9,10},{10,1... | collective-permute-start | bytes 71432 | tf_op jit(solution)/shard_map/ppermute | solution.py:20
  67.7 3.0 %copy.39 = f32[4,62,12,2]{3,2,1,0:T(8,128)} copy(f32[4,62,12,2]{1,0,3,2:T(4,128)} %collective-permute-done.3) | data formatting | bytes 47616 | tf_op jit(solution)/shard_map/ppermute | solution.py:21
  70.6 4.5 %maximum_multiply_fusion = f32[4,62,12,132]{3,2,1,0:T(8,128)S(1)} fusion(f32[4,62,12,2]{3,2,1,0:T(8,128)} %copy.39, f32[4,62,2,128]{3,2,1,0:T(2,128)} %copy-done, f32[4,62,8,128]{3,2,1,0:T(8,128)S(1)} %maximum_multiply_fusion.1, f32[4,62,2,128]{3,2,1,0:T(2,128)S(1)} %collective-permute-done, f32[4,62,12,2]{3,2,1,0:T(8,128)S(1)} %copy.38, f32[132]{0:T(256)} %or_select_fusion.1), kind=kLoop, calls=%fused_computation | loop fusion | flops 1964160 | bytes 3143184 | tf_op jit(solution)/shard_map/mul | solution.py:84
  80.7 8.1 %collective-permute-start.9 = (f32[1,128]{1,0:T(1,128)S(1)}, f32[1,128]{1,0:T(1,128)S(1)}, u32[]{:S(2)}, u32[]{:S(2)}) collective-permute-start(f32[1,128]{1,0:T(1,128)S(1)} %get-tuple-element.61), channel_id=1, source_target_pairs={{8,0},{16,8},{24,16},{32,24},{40,32},{48,40},{56,48},{64,56},{72,6... | collective-permute-start | bytes 1544 | tf_op jit(solution)/shard_map/ppermute | solution.py:21
  89.6 3.9 %collective-permute-start.10 = (f32[10,1]{1,0:T(8,128)S(1)}, f32[10,1]{1,0:T(8,128)S(1)}, u32[]{:S(2)}, u32[]{:S(2)}) collective-permute-start(f32[10,1]{1,0:T(8,128)S(1)} %get-tuple-element.44), channel_id=1, source_target_pairs={{0,1},{1,2},{2,3},{3,4},{4,5},{5,6},{6,7},{7,0},{8,9},{9,10},{10,1... | collective-permute-start | bytes 128 | tf_op jit(solution)/shard_map/ppermute | solution.py:20
  95.4 5.1 %collective-permute-done.11 = f32[10,1]{1,0:T(8,128)S(1)} collective-permute-done((f32[10,1]{1,0:T(8,128)S(1)}, f32[10,1]{1,0:T(8,128)S(1)}, u32[]{:S(2)}, u32[]{:S(2)}) %collective-permute-start.11) | collective-permute-done | bytes 72 | tf_op jit(solution)/shard_map/ppermute | solution.py:21
  102.7 8.1 %collective-permute-start.13 = (f32[1,128]{1,0:T(1,128)S(1)}, f32[1,128]{1,0:T(1,128)S(1)}, u32[]{:S(2)}, u32[]{:S(2)}) collective-permute-start(f32[1,128]{1,0:T(1,128)S(1)} %get-tuple-element.59), channel_id=1, source_target_pairs={{8,0},{16,8},{24,16},{32,24},{40,32},{48,40},{56,48},{64,56},{72,6... | collective-permute-start | bytes 1544 | tf_op jit(solution)/shard_map/ppermute | solution.py:21
  111.6 2.8 %collective-permute-start.14 = (f32[10,1]{1,0:T(8,128)S(1)}, f32[10,1]{1,0:T(8,128)S(1)}, u32[]{:S(2)}, u32[]{:S(2)}) collective-permute-start(f32[10,1]{1,0:T(8,128)S(1)} %get-tuple-element.42), channel_id=1, source_target_pairs={{0,1},{1,2},{2,3},{3,4},{4,5},{5,6},{6,7},{7,0},{8,9},{9,10},{10,1... | collective-permute-start | bytes 128 | tf_op jit(solution)/shard_map/ppermute | solution.py:20
  116.3 5.1 %collective-permute-done.15 = f32[10,1]{1,0:T(8,128)S(1)} collective-permute-done((f32[10,1]{1,0:T(8,128)S(1)}, f32[10,1]{1,0:T(8,128)S(1)}, u32[]{:S(2)}, u32[]{:S(2)}) %collective-permute-start.15) | collective-permute-done | bytes 72 | tf_op jit(solution)/shard_map/ppermute | solution.py:21
  123.5 8.1 %collective-permute-start.17 = (f32[1,128]{1,0:T(1,128)S(1)}, f32[1,128]{1,0:T(1,128)S(1)}, u32[]{:S(2)}, u32[]{:S(2)}) collective-permute-start(f32[1,128]{1,0:T(1,128)S(1)} %get-tuple-element.57), channel_id=1, source_target_pairs={{8,0},{16,8},{24,16},{32,24},{40,32},{48,40},{56,48},{64,56},{72,6... | collective-permute-start | bytes 1544 | tf_op jit(solution)/shard_map/ppermute | solution.py:21
  137.2 5.1 %collective-permute-done.19 = f32[10,1]{1,0:T(8,128)S(1)} collective-permute-done((f32[10,1]{1,0:T(8,128)S(1)}, f32[10,1]{1,0:T(8,128)S(1)}, u32[]{:S(2)}, u32[]{:S(2)}) %collective-permute-start.19) | collective-permute-done | bytes 72 | tf_op jit(solution)/shard_map/ppermute | solution.py:21
  144.4 8.1 %collective-permute-start.21 = (f32[1,128]{1,0:T(1,128)S(1)}, f32[1,128]{1,0:T(1,128)S(1)}, u32[]{:S(2)}, u32[]{:S(2)}) collective-permute-start(f32[1,128]{1,0:T(1,128)S(1)} %get-tuple-element.55), channel_id=1, source_target_pairs={{8,0},{16,8},{24,16},{32,24},{40,32},{48,40},{56,48},{64,56},{72,6... | collective-permute-start | bytes 1544 | tf_op jit(solution)/shard_map/ppermute | solution.py:21
  158.0 5.1 %collective-permute-done.23 = f32[10,1]{1,0:T(8,128)S(1)} collective-permute-done((f32[10,1]{1,0:T(8,128)S(1)}, f32[10,1]{1,0:T(8,128)S(1)}, u32[]{:S(2)}, u32[]{:S(2)}) %collective-permute-start.23) | collective-permute-done | bytes 72 | tf_op jit(solution)/shard_map/ppermute | solution.py:21
  165.3 8.1 %collective-permute-start.25 = (f32[1,128]{1,0:T(1,128)S(1)}, f32[1,128]{1,0:T(1,128)S(1)}, u32[]{:S(2)}, u32[]{:S(2)}) collective-permute-start(f32[1,128]{1,0:T(1,128)S(1)} %get-tuple-element.53), channel_id=1, source_target_pairs={{8,0},{16,8},{24,16},{32,24},{40,32},{48,40},{56,48},{64,56},{72,6... | collective-permute-start | bytes 1544 | tf_op jit(solution)/shard_map/ppermute | solution.py:21
  178.9 5.1 %collective-permute-done.27 = f32[10,1]{1,0:T(8,128)S(1)} collective-permute-done((f32[10,1]{1,0:T(8,128)S(1)}, f32[10,1]{1,0:T(8,128)S(1)}, u32[]{:S(2)}, u32[]{:S(2)}) %collective-permute-start.27) | collective-permute-done | bytes 72 | tf_op jit(solution)/shard_map/ppermute | solution.py:21
  186.1 8.1 %collective-permute-start.29 = (f32[1,128]{1,0:T(1,128)S(1)}, f32[1,128]{1,0:T(1,128)S(1)}, u32[]{:S(2)}, u32[]{:S(2)}) collective-permute-start(f32[1,128]{1,0:T(1,128)S(1)} %get-tuple-element.51), channel_id=1, source_target_pairs={{8,0},{16,8},{24,16},{32,24},{40,32},{48,40},{56,48},{64,56},{72,6... | collective-permute-start | bytes 1544 | tf_op jit(solution)/shard_map/ppermute | solution.py:21
  199.8 5.1 %collective-permute-done.31 = f32[10,1]{1,0:T(8,128)S(1)} collective-permute-done((f32[10,1]{1,0:T(8,128)S(1)}, f32[10,1]{1,0:T(8,128)S(1)}, u32[]{:S(2)}, u32[]{:S(2)}) %collective-permute-start.31) | collective-permute-done | bytes 72 | tf_op jit(solution)/shard_map/ppermute | solution.py:21
  207.0 8.1 %collective-permute-start.33 = (f32[1,128]{1,0:T(1,128)S(1)}, f32[1,128]{1,0:T(1,128)S(1)}, u32[]{:S(2)}, u32[]{:S(2)}) collective-permute-start(f32[1,128]{1,0:T(1,128)S(1)} %get-tuple-element.49), channel_id=1, source_target_pairs={{8,0},{16,8},{24,16},{32,24},{40,32},{48,40},{56,48},{64,56},{72,6... | collective-permute-start | bytes 1544 | tf_op jit(solution)/shard_map/ppermute | solution.py:21
  220.6 5.1 %collective-permute-done.35 = f32[10,1]{1,0:T(8,128)S(1)} collective-permute-done((f32[10,1]{1,0:T(8,128)S(1)}, f32[10,1]{1,0:T(8,128)S(1)}, u32[]{:S(2)}, u32[]{:S(2)}) %collective-permute-start.35) | collective-permute-done | bytes 72 | tf_op jit(solution)/shard_map/ppermute | solution.py:21
  (129 shorter events, 72.7 us)
Async XLA Ops:
  3.7 42.8 %collective-permute-start = (f32[4,62,2,128]{3,2,1,0:T(2,128)S(1)}, f32[4,62,2,128]{3,2,1,0:T(2,128)S(1)}, u32[]{:S(2)}, u32[]{:S(2)}) collective-permute-start(f32[4,62,2,128]{3,2,1,0:T(2,128)S(1)} %get-tuple-element.30), channel_id=1, source_target_pairs={{0,8},{8,16},{16,24},{24,32},{32,40},{40,48},{48,56},{56,64},{64,7... | collective-permute-start | bytes 761864 | tf_op jit(solution)/shard_map/ppermute | solution.py:20
  8.6 37.9 %collective-permute-start.1 = (f32[4,62,2,128]{3,2,1,0:T(2,128)S(1)}, f32[4,62,2,128]{3,2,1,0:T(2,128)S(1)}, u32[]{:S(2)}, u32[]{:S(2)}) collective-permute-start(f32[4,62,2,128]{3,2,1,0:T(2,128)S(1)} %get-tuple-element.31), channel_id=1, source_target_pairs={{8,0},{16,8},{24,16},{32,24},{40,32},{48,40},{56,48},{64,56},{72,6... | collective-permute-start | bytes 761864 | tf_op jit(solution)/shard_map/ppermute | solution.py:21
  27.3 10.7 %collective-permute-start.4 = (f32[1,128]{1,0:T(1,128)S(1)}, f32[1,128]{1,0:T(1,128)S(1)}, u32[]{:S(2)}, u32[]{:S(2)}) collective-permute-start(f32[1,128]{1,0:T(1,128)S(1)} %get-tuple-element.62), channel_id=1, source_target_pairs={{0,8},{8,16},{16,24},{24,32},{32,40},{40,48},{48,56},{56,64},{64,7... | collective-permute-start | bytes 1544 | tf_op jit(solution)/shard_map/ppermute | solution.py:20
  29.3 8.7 %collective-permute-start.5 = (f32[1,128]{1,0:T(1,128)S(1)}, f32[1,128]{1,0:T(1,128)S(1)}, u32[]{:S(2)}, u32[]{:S(2)}) collective-permute-start(f32[1,128]{1,0:T(1,128)S(1)} %get-tuple-element.63), channel_id=1, source_target_pairs={{8,0},{16,8},{24,16},{32,24},{40,32},{48,40},{56,48},{64,56},{72,6... | collective-permute-start | bytes 1544 | tf_op jit(solution)/shard_map/ppermute | solution.py:21
  38.7 23.1 %collective-permute-start.6 = (f32[10,1]{1,0:T(8,128)}, f32[10,1]{1,0:T(8,128)}, u32[]{:S(2)}, u32[]{:S(2)}) collective-permute-start(f32[10,1]{1,0:T(8,128)} %get-tuple-element.46), channel_id=1, source_target_pairs={{0,1},{1,2},{2,3},{3,4},{4,5},{5,6},{6,7},{7,0},{8,9},{9,10},{10,1... | collective-permute-start | bytes 128 | tf_op jit(solution)/shard_map/ppermute | solution.py:20
  44.6 17.2 %collective-permute-start.7 = (f32[10,1]{1,0:T(8,128)}, f32[10,1]{1,0:T(8,128)}, u32[]{:S(2)}, u32[]{:S(2)}) collective-permute-start(f32[10,1]{1,0:T(8,128)} %get-tuple-element.47), channel_id=1, source_target_pairs={{1,0},{2,1},{3,2},{4,3},{5,4},{6,5},{7,6},{0,7},{9,8},{10,9},{11,1... | collective-permute-start | bytes 128 | tf_op jit(solution)/shard_map/ppermute | solution.py:21
  52.6 10.6 %collective-permute-start.2 = (f32[4,62,12,2]{1,0,3,2:T(4,128)}, f32[4,62,12,2]{1,0,3,2:T(4,128)}, u32[]{:S(2)}, u32[]{:S(2)}) collective-permute-start(f32[4,62,12,2]{1,0,3,2:T(4,128)} %copy.36), channel_id=1, source_target_pairs={{0,1},{1,2},{2,3},{3,4},{4,5},{5,6},{6,7},{7,0},{8,9},{9,10},{10,1... | collective-permute-start | bytes 71432 | tf_op jit(solution)/shard_map/ppermute | solution.py:20
  59.9 7.8 %collective-permute-start.3 = (f32[4,62,12,2]{1,0,3,2:T(4,128)}, f32[4,62,12,2]{1,0,3,2:T(4,128)}, u32[]{:S(2)}, u32[]{:S(2)}) collective-permute-start(f32[4,62,12,2]{1,0,3,2:T(4,128)} %copy.37), channel_id=1, source_target_pairs={{1,0},{2,1},{3,2},{4,3},{5,4},{6,5},{7,6},{0,7},{9,8},{10,9},{11,1... | collective-permute-start | bytes 71432 | tf_op jit(solution)/shard_map/ppermute | solution.py:21
  78.7 10.0 %collective-permute-start.8 = (f32[1,128]{1,0:T(1,128)S(1)}, f32[1,128]{1,0:T(1,128)S(1)}, u32[]{:S(2)}, u32[]{:S(2)}) collective-permute-start(f32[1,128]{1,0:T(1,128)S(1)} %get-tuple-element.60), channel_id=1, source_target_pairs={{0,8},{8,16},{16,24},{24,32},{32,40},{40,48},{48,56},{56,64},{64,7... | collective-permute-start | bytes 1544 | tf_op jit(solution)/shard_map/ppermute | solution.py:20
  80.7 8.8 %collective-permute-start.9 = (f32[1,128]{1,0:T(1,128)S(1)}, f32[1,128]{1,0:T(1,128)S(1)}, u32[]{:S(2)}, u32[]{:S(2)}) collective-permute-start(f32[1,128]{1,0:T(1,128)S(1)} %get-tuple-element.61), channel_id=1, source_target_pairs={{8,0},{16,8},{24,16},{32,24},{40,32},{48,40},{56,48},{64,56},{72,6... | collective-permute-start | bytes 1544 | tf_op jit(solution)/shard_map/ppermute | solution.py:21
  100.7 10.0 %collective-permute-start.12 = (f32[1,128]{1,0:T(1,128)S(1)}, f32[1,128]{1,0:T(1,128)S(1)}, u32[]{:S(2)}, u32[]{:S(2)}) collective-permute-start(f32[1,128]{1,0:T(1,128)S(1)} %get-tuple-element.58), channel_id=1, source_target_pairs={{0,8},{8,16},{16,24},{24,32},{32,40},{40,48},{48,56},{56,64},{64,7... | collective-permute-start | bytes 1544 | tf_op jit(solution)/shard_map/ppermute | solution.py:20
  102.7 8.8 %collective-permute-start.13 = (f32[1,128]{1,0:T(1,128)S(1)}, f32[1,128]{1,0:T(1,128)S(1)}, u32[]{:S(2)}, u32[]{:S(2)}) collective-permute-start(f32[1,128]{1,0:T(1,128)S(1)} %get-tuple-element.59), channel_id=1, source_target_pairs={{8,0},{16,8},{24,16},{32,24},{40,32},{48,40},{56,48},{64,56},{72,6... | collective-permute-start | bytes 1544 | tf_op jit(solution)/shard_map/ppermute | solution.py:21
  114.3 7.1 %collective-permute-start.15 = (f32[10,1]{1,0:T(8,128)S(1)}, f32[10,1]{1,0:T(8,128)S(1)}, u32[]{:S(2)}, u32[]{:S(2)}) collective-permute-start(f32[10,1]{1,0:T(8,128)S(1)} %get-tuple-element.43), channel_id=1, source_target_pairs={{1,0},{2,1},{3,2},{4,3},{5,4},{6,5},{7,6},{0,7},{9,8},{10,9},{11,1... | collective-permute-start | bytes 128 | tf_op jit(solution)/shard_map/ppermute | solution.py:21
  121.6 10.0 %collective-permute-start.16 = (f32[1,128]{1,0:T(1,128)S(1)}, f32[1,128]{1,0:T(1,128)S(1)}, u32[]{:S(2)}, u32[]{:S(2)}) collective-permute-start(f32[1,128]{1,0:T(1,128)S(1)} %get-tuple-element.56), channel_id=1, source_target_pairs={{0,8},{8,16},{16,24},{24,32},{32,40},{40,48},{48,56},{56,64},{64,7... | collective-permute-start | bytes 1544 | tf_op jit(solution)/shard_map/ppermute | solution.py:20
  123.5 8.8 %collective-permute-start.17 = (f32[1,128]{1,0:T(1,128)S(1)}, f32[1,128]{1,0:T(1,128)S(1)}, u32[]{:S(2)}, u32[]{:S(2)}) collective-permute-start(f32[1,128]{1,0:T(1,128)S(1)} %get-tuple-element.57), channel_id=1, source_target_pairs={{8,0},{16,8},{24,16},{32,24},{40,32},{48,40},{56,48},{64,56},{72,6... | collective-permute-start | bytes 1544 | tf_op jit(solution)/shard_map/ppermute | solution.py:21
  135.2 7.1 %collective-permute-start.19 = (f32[10,1]{1,0:T(8,128)S(1)}, f32[10,1]{1,0:T(8,128)S(1)}, u32[]{:S(2)}, u32[]{:S(2)}) collective-permute-start(f32[10,1]{1,0:T(8,128)S(1)} %get-tuple-element.41), channel_id=1, source_target_pairs={{1,0},{2,1},{3,2},{4,3},{5,4},{6,5},{7,6},{0,7},{9,8},{10,9},{11,1... | collective-permute-start | bytes 128 | tf_op jit(solution)/shard_map/ppermute | solution.py:21
  142.5 10.0 %collective-permute-start.20 = (f32[1,128]{1,0:T(1,128)S(1)}, f32[1,128]{1,0:T(1,128)S(1)}, u32[]{:S(2)}, u32[]{:S(2)}) collective-permute-start(f32[1,128]{1,0:T(1,128)S(1)} %get-tuple-element.54), channel_id=1, source_target_pairs={{0,8},{8,16},{16,24},{24,32},{32,40},{40,48},{48,56},{56,64},{64,7... | collective-permute-start | bytes 1544 | tf_op jit(solution)/shard_map/ppermute | solution.py:20
  144.4 8.8 %collective-permute-start.21 = (f32[1,128]{1,0:T(1,128)S(1)}, f32[1,128]{1,0:T(1,128)S(1)}, u32[]{:S(2)}, u32[]{:S(2)}) collective-permute-start(f32[1,128]{1,0:T(1,128)S(1)} %get-tuple-element.55), channel_id=1, source_target_pairs={{8,0},{16,8},{24,16},{32,24},{40,32},{48,40},{56,48},{64,56},{72,6... | collective-permute-start | bytes 1544 | tf_op jit(solution)/shard_map/ppermute | solution.py:21
  163.3 10.0 %collective-permute-start.24 = (f32[1,128]{1,0:T(1,128)S(1)}, f32[1,128]{1,0:T(1,128)S(1)}, u32[]{:S(2)}, u32[]{:S(2)}) collective-permute-start(f32[1,128]{1,0:T(1,128)S(1)} %get-tuple-element.52), channel_id=1, source_target_pairs={{0,8},{8,16},{16,24},{24,32},{32,40},{40,48},{48,56},{56,64},{64,7... | collective-permute-start | bytes 1544 | tf_op jit(solution)/shard_map/ppermute | solution.py:20
  165.3 8.8 %collective-permute-start.25 = (f32[1,128]{1,0:T(1,128)S(1)}, f32[1,128]{1,0:T(1,128)S(1)}, u32[]{:S(2)}, u32[]{:S(2)}) collective-permute-start(f32[1,128]{1,0:T(1,128)S(1)} %get-tuple-element.53), channel_id=1, source_target_pairs={{8,0},{16,8},{24,16},{32,24},{40,32},{48,40},{56,48},{64,56},{72,6... | collective-permute-start | bytes 1544 | tf_op jit(solution)/shard_map/ppermute | solution.py:21
  184.2 10.0 %collective-permute-start.28 = (f32[1,128]{1,0:T(1,128)S(1)}, f32[1,128]{1,0:T(1,128)S(1)}, u32[]{:S(2)}, u32[]{:S(2)}) collective-permute-start(f32[1,128]{1,0:T(1,128)S(1)} %get-tuple-element.50), channel_id=1, source_target_pairs={{0,8},{8,16},{16,24},{24,32},{32,40},{40,48},{48,56},{56,64},{64,7... | collective-permute-start | bytes 1544 | tf_op jit(solution)/shard_map/ppermute | solution.py:20
  186.1 8.8 %collective-permute-start.29 = (f32[1,128]{1,0:T(1,128)S(1)}, f32[1,128]{1,0:T(1,128)S(1)}, u32[]{:S(2)}, u32[]{:S(2)}) collective-permute-start(f32[1,128]{1,0:T(1,128)S(1)} %get-tuple-element.51), channel_id=1, source_target_pairs={{8,0},{16,8},{24,16},{32,24},{40,32},{48,40},{56,48},{64,56},{72,6... | collective-permute-start | bytes 1544 | tf_op jit(solution)/shard_map/ppermute | solution.py:21
  205.1 10.8 %collective-permute-start.32 = (f32[1,128]{1,0:T(1,128)S(1)}, f32[1,128]{1,0:T(1,128)S(1)}, u32[]{:S(2)}, u32[]{:S(2)}) collective-permute-start(f32[1,128]{1,0:T(1,128)S(1)} %get-tuple-element.48), channel_id=1, source_target_pairs={{0,8},{8,16},{16,24},{24,32},{32,40},{40,48},{48,56},{56,64},{64,7... | collective-permute-start | bytes 1544 | tf_op jit(solution)/shard_map/ppermute | solution.py:20
  207.0 8.9 %collective-permute-start.33 = (f32[1,128]{1,0:T(1,128)S(1)}, f32[1,128]{1,0:T(1,128)S(1)}, u32[]{:S(2)}, u32[]{:S(2)}) collective-permute-start(f32[1,128]{1,0:T(1,128)S(1)} %get-tuple-element.49), channel_id=1, source_target_pairs={{8,0},{16,8},{24,16},{32,24},{40,32},{48,40},{56,48},{64,56},{72,6... | collective-permute-start | bytes 1544 | tf_op jit(solution)/shard_map/ppermute | solution.py:21
  (23 other events, 196.3 us)
where the time goes:
time: 228 us; the launch traced here: 227 us
  starting transfers between devices  153 us (67%)
  waiting for transfers between devices  42.9 us (19%)
  other arithmetic  15.3 us (7%)
  local copies, waits for them, and re-layouts  14.5 us (6%)
    ppermute x18, starting transfers between devices, extended_2(): after = lax.ppermute(initial, axis, down)  100 us
    ppermute x18, starting transfers between devices, extended_2(): before = lax.ppermute(last, axis, up)  52.4 us
    ppermute x18, waiting for transfers between devices, extended_2(): after = lax.ppermute(initial, axis, down)  42.8 us
    slice x19, local copies, waits for them, and re-layouts, extended_2(): last = lax.slice_in_dim(array, length - width, length, axis=dim)  6.37 us
  transfers between devices with their start and end apart: 36, of which 14 were waited for; matrix products, arithmetic and copies ran while one was open for 6% of the time, Pallas kernels for 0%

commit v1 on v0

v1 whole, which is shorter than its diff:
```python
import jax
import jax.numpy as jnp
from jax import lax
from jax.experimental import pallas as pl
from jax.experimental.pallas import tpu as pltpu
from jax.sharding import PartitionSpec as P

ITERS = 8
LEVELS = 62
SPECTRUM_MID = 1.0
SPECTRUM_HALF = 0.995

ROWS = 8
LANES = 128
STRIP = 128
LON_ROWS = 4 * STRIP + 3 * ROWS
LAT_ROWS = 17 * ROWS
SOLVE_ROWS = 5 * ROWS + 32 + 8
VMEM = 12 * 1024 * 1024

F32 = jnp.float32
ADV = 0.1 / 12.0


def rows_of(shape=(ROWS, LANES)):
    return lax.broadcasted_iota(jnp.int32, shape, 0)


def lanes_of(shape=(ROWS, LANES)):
    return lax.broadcasted_iota(jnp.int32, shape, 1)


def by_rows(x, d):
    d %= ROWS
    return pltpu.roll(x, d, 0) if d else x


def by_lanes(x, d):
    d %= LANES
    return pltpu.roll(x, d, 1) if d else x


def scalar_mix(t, s):
    return 0.7 * t - 0.5 * s


def even(axis):
    return lax.axis_index(axis) % 2 == 0


def pack_lon(u, v, t, s, water, layers, diag, elev, parity, up_first, low_first):
    row = rows_of()
    group = row >> 1
    depth = water[...] * layers[...]
    is_even = parity[0] == 0

    def body(g, carry):
        for f, ref in enumerate((u, v, t, s)):
            top = None
            for i in range(4):
                k = 4 * g + i
                m = jnp.where(k < depth, ref[jnp.minimum(k, LEVELS - 1)], 0.0)
                a, b = by_rows(m, 2 * i), by_rows(m, 2 * i - 6)
                if top is None:
                    top, bottom = a, b
                else:
                    top, bottom = jnp.where(group == i, a, top), jnp.where(group == i, b, bottom)
            at = pl.ds(pl.multiple_of(f * STRIP + 8 * g, 8), 8)
            up_first[at, :] = jnp.where(is_even, top, bottom)
            low_first[at, :] = jnp.where(is_even, bottom, top)
        return carry

    lax.fori_loop(0, 16, body, 0)
    for ref in (up_first, low_first):
        ref[4 * STRIP : 4 * STRIP + 8, :] = elev[...]
        ref[4 * STRIP + 8 : 4 * STRIP + 16, :] = diag[...]
        ref[4 * STRIP + 16 : 4 * STRIP + 24, :] = depth.astype(F32)


def pack_lat(u, v, t, s, water, layers, diag, elev, parity, odd_out, even_out, partial):
    row, lane = rows_of(), lanes_of()
    slot = lane >> 3
    depth = water[...] * layers[...]
    is_even = parity[1] == 0

    def body(a, acc):
        left = [None] * 4
        right = [None] * 4
        for i in range(16):
            k = 16 * a + i
            wet = k < depth
            at = jnp.minimum(k, LEVELS - 1)
            m = [jnp.where(wet, ref[at], 0.0) for ref in (u, v, t, s)]
            for f in range(4):
                x, y = by_lanes(m[f], 8 * i), by_lanes(m[f], 8 * i - 120)
                left[f] = x if i == 0 else jnp.where(slot == i, x, left[f])
                right[f] = y if i == 0 else jnp.where(slot == i, y, right[f])
            w = scalar_mix(m[2], m[3])
            n1 = jnp.where(row < 7, by_rows(w, -1), 0.0)
            p1 = jnp.where(row > 0, by_rows(w, 1), 0.0)
            n2 = jnp.where(row < 6, by_rows(w, -2), 0.0)
            p2 = jnp.where(row > 1, by_rows(w, 2), 0.0)
            e1 = jnp.where(lane < 127, by_lanes(w, -1), 0.0)
            q1 = jnp.where(lane > 0, by_lanes(w, 1), 0.0)
            e2 = jnp.where(lane < 126, by_lanes(w, -2), 0.0)
            q2 = jnp.where(lane > 1, by_lanes(w, 2), 0.0)
            gx = 8.0 * (n1 - p1) - (n2 - p2)
            gy = 8.0 * (e1 - q1) - (e2 - q2)
            around = jnp.where(wet, (n1 + p1) + (e1 + q1), 0.0)
            column = jnp.where(k > 0, w, 0.0) + jnp.where(k + 1 < depth, w, 0.0)
            acc = acc + (
                0.94 * w + 0.02 * column + 0.005 * around - ADV * (m[0] * gx + m[1] * gy)
            )
        for f in range(4):
            where = pl.ds(pl.multiple_of(f * 32 + 8 * a, 8), 8)
            odd_out[where, :] = jnp.where(is_even, left[f], right[f])
            even_out[where, :] = jnp.where(is_even, right[f], left[f])
        return acc

    acc = 0.1 * lax.fori_loop(0, 4, body, jnp.zeros((ROWS, LANES), F32))
    partial[...] = acc
    flat = (acc, elev[...], diag[...], depth.astype(F32))
    left = right = None
    for i, x in enumerate(flat):
        a, b = by_lanes(x, 8 * i), by_lanes(x, 8 * i - 120)
        left = a if i == 0 else jnp.where(slot == i, a, left)
        right = b if i == 0 else jnp.where(slot == i, b, right)
    odd_out[128:136, :] = jnp.where(is_even, left, right)
    even_out[128:136, :] = jnp.where(is_even, right, left)


def tile_lanes(x):
    x = jnp.where(lanes_of() < 8, x, 0.0)
    for d in (8, 16, 32, 64):
        x = x + by_lanes(x, d)
    return x


def sum_slots(x):
    for d in (8, 16, 32, 64):
        x = x + by_lanes(x, d)
    return x


def wet_pack(depth, a):
    return (16 * a + (lanes_of() >> 3)).astype(F32) < depth


def lat_rims(a_v, a_w, a_depth, b_v, b_w, b_depth):
    column = lanes_of() & 7
    a_sum = b_sum = jnp.zeros((ROWS, LANES), F32)
    for i in range(4):
        y1, y2 = by_lanes(b_w[i], 7), by_lanes(b_w[i], 6)
        y1 = jnp.where(column == 7, y1, 0.0)
        y2 = jnp.where(column >= 6, y2, 0.0)
        a_sum = a_sum - ADV * a_v[i] * (8.0 * y1 - y2)
        a_sum = a_sum + 0.005 * jnp.where(wet_pack(a_depth, i), y1, 0.0)
        z1, z2 = by_lanes(a_w[i], -7), by_lanes(a_w[i], -6)
        z1 = jnp.where(column == 0, z1, 0.0)
        z2 = jnp.where(column <= 1, z2, 0.0)
        b_sum = b_sum - ADV * b_v[i] * (z2 - 8.0 * z1)
        b_sum = b_sum + 0.005 * jnp.where(wet_pack(b_depth, i), z1, 0.0)
    return 0.1 * sum_slots(a_sum), 0.1 * sum_slots(b_sum)


def pick(flag, a, b):
    return jnp.where(flag, a, b)


def four(ref, base, flag, other):
    at = [slice(base + 8 * i, base + 8 * i + 8) for i in range(4)]
    return [jnp.where(flag, ref[x, :], other[x, :]) for x in at]


def forcing(
    parity, own_odd_u, own_even_u, got_odd_ts, got_even_ts, flat2d,
    own_odd_lat, own_even_lat, got_odd_lat, got_even_lat, partial,
    odd_out, even_out,
):
    row, lane = rows_of(), lanes_of()
    lon_even, lat_even = parity[0] == 0, parity[1] == 0
    elev, diag, depth = (flat2d[8 * i : 8 * i + 8, :] for i in range(3))
    total = elev + partial[...]

    r = row & 1
    for lower in (True, False):
        rim = row < 2 if lower else row >= 6
        tiled = jnp.where(rim, depth, 0.0)
        tiled = tiled + by_rows(tiled, 2)
        tiled = tiled + by_rows(tiled, 4)
        acc = jnp.zeros((ROWS, LANES), F32)
        own_first = lon_even if lower else jnp.logical_not(lon_even)
        for g in range(16):
            at = slice(8 * g, 8 * g + 8)
            also = slice(STRIP + 8 * g, STRIP + 8 * g + 8)
            vel = jnp.where(own_first, own_odd_u[at, :], own_even_u[at, :])
            w = jnp.where(
                own_first,
                scalar_mix(got_odd_ts[at, :], got_odd_ts[also, :]),
                scalar_mix(got_even_ts[at, :], got_even_ts[also, :]),
            )
            wet = (4 * g + (row >> 1)).astype(F32) < tiled
            if lower:
                near = jnp.where(r == 0, by_rows(w, -1), 0.0)
                slope = w - 8.0 * near
            else:
                near = jnp.where(r == 1, by_rows(w, 1), 0.0)
                slope = 8.0 * near - w
            acc = acc + (0.005 * jnp.where(wet, near, 0.0) - ADV * vel * slope)
        acc = acc + by_rows(acc, 2)
        acc = acc + by_rows(acc, 4)
        total = total + jnp.where(rim, 0.1 * acc, 0.0)

    own_r = [four(own_even_lat, f * 32, lat_even, own_odd_lat) for f in range(1, 4)]
    own_l = [four(own_odd_lat, f * 32, lat_even, own_even_lat) for f in range(1, 4)]
    ext_r = [four(got_even_lat, f * 32, lat_even, got_odd_lat) for f in range(4)]
    ext_l = [four(got_odd_lat, f * 32, lat_even, got_even_lat) for f in range(4)]
    flat_r = jnp.where(lat_even, got_even_lat[128:136, :], got_odd_lat[128:136, :])
    flat_l = jnp.where(lat_even, got_odd_lat[128:136, :], got_even_lat[128:136, :])

    def mixed(pair):
        return [scalar_mix(x, y) for x, y in zip(*pair, strict=True)]

    w_r, w_l = mixed(ext_r[2:]), mixed(ext_l[2:])
    miss_own_r, miss_ext_r = lat_rims(
        own_r[0], mixed(own_r[1:]), tile_lanes(by_lanes(depth, 8)),
        ext_r[1], w_r, tile_lanes(by_lanes(flat_r, -24)),
    )
    miss_ext_l, miss_own_l = lat_rims(
        ext_l[1], w_l, tile_lanes(by_lanes(flat_l, -24)),
        own_l[0], mixed(own_l[1:]), tile_lanes(depth),
    )
    total = total + jnp.where(lane >= 126, miss_own_r, 0.0) + jnp.where(lane < 2, miss_own_l, 0.0)

    def side(i):
        return jnp.where(
            lane < 8,
            by_lanes(flat_r, -8 * i),
            jnp.where(lane >= 120, by_lanes(flat_l, 120 - 8 * i), 0.0),
        )

    elev_side = side(1)
    total_side = side(0) + elev_side
    total_side = total_side + jnp.where(lane < 2, miss_ext_r, 0.0)
    total_side = total_side + jnp.where(lane >= 126, miss_ext_l, 0.0)
    for ref in (odd_out, even_out):
        for i, x in enumerate((total, total_side, elev_side, side(2), side(3))):
            ref[8 * i : 8 * i + 8, :] = x
        ref[SOLVE_ROWS - 8 : SOLVE_ROWS, :] = jnp.zeros((8, LANES), F32)
    packs = ext_r[0] + ext_l[0] + w_r + w_l
    group = row >> 1
    for i in range(4):
        top = bottom = None
        for j in range(4):
            x = packs[4 * i + j]
            a, b = by_rows(x, 2 * j), by_rows(x, 2 * j - 6)
            top = a if j == 0 else jnp.where(group == j, a, top)
            bottom = b if j == 0 else jnp.where(group == j, b, bottom)
        at = slice(40 + 8 * i, 48 + 8 * i)
        odd_out[at, :] = jnp.where(lon_even, top, bottom)
        even_out[at, :] = jnp.where(lon_even, bottom, top)


def fields(
    parity, u, v, t, s, water, layers, odd_lon, even_lon, odd_lat, even_lat, *outs
):
    row, lane = rows_of(), lanes_of()
    depth = water[...] * layers[...]
    lon_even, lat_even = parity[0] == 0, parity[1] == 0
    refs = (u, v, t, s)

    def level(a, i, strips, packs):
        k = 16 * a + i
        wet = k < depth
        wet_below = k + 1 < depth
        below, above = jnp.minimum(k + 1, LEVELS - 1), jnp.maximum(k - 1, 0)
        center = [jnp.where(wet, ref[k], 0.0) for ref in refs]
        j = i % 4
        for f in range(4):
            m = center[f]
            upper, lower = strips[f]
            rim = jnp.where(row < 4, by_rows(upper, -2 * j), by_rows(lower, 6 - 2 * j))
            n1 = by_rows(jnp.where(row < 1, rim, m), -1)
            n2 = by_rows(jnp.where(row < 2, rim, m), -2)
            p1 = by_rows(jnp.where(row > 6, rim, m), 1)
            p2 = by_rows(jnp.where(row > 5, rim, m), 2)
            west, east = packs[f]
            beside = jnp.where(lane < 64, by_lanes(east, -8 * i), by_lanes(west, 120 - 8 * i))
            e1 = by_lanes(jnp.where(lane < 1, beside, m), -1)
            e2 = by_lanes(jnp.where(lane < 2, beside, m), -2)
            q1 = by_lanes(jnp.where(lane > 126, beside, m), 1)
            q2 = by_lanes(jnp.where(lane > 125, beside, m), 2)
            gx = 8.0 * (n1 - p1) - (n2 - p2)
            gy = 8.0 * (e1 - q1) - (e2 - q2)
            around = (n1 + p1) + (e1 + q1)
            column = jnp.where(wet_below, refs[f][below], 0.0) + jnp.where(
                k > 0, refs[f][above], 0.0
            )
            fresh = (
                0.94 * m
                + 0.02 * column
                + 0.005 * around
                - ADV * (center[0] * gx + center[1] * gy)
            )
            outs[f][k] = jnp.where(wet, fresh, 0.0)

    def body(a, carry):
        packs = []
        for f in range(4):
            at = pl.ds(pl.multiple_of(f * 32 + 8 * a, 8), 8)
            x, y = odd_lat[at, :], even_lat[at, :]
            packs.append((jnp.where(lat_even, x, y), jnp.where(lat_even, y, x)))
        for b in range(4):
            strips = []
            for f in range(4):
                at = pl.ds(pl.multiple_of(f * STRIP + 32 * a + 8 * b, 8), 8)
                x, y = odd_lon[at, :], even_lon[at, :]
                strips.append((jnp.where(lon_even, y, x), jnp.where(lon_even, x, y)))
            for i in range(4 * b, 4 * b + 4):
                if i < 14:
                    level(a, i, strips, packs)
                else:
                    pl.when(16 * a + i < LEVELS)(lambda i=i, s=strips: level(a, i, s, packs))
        return carry

    lax.fori_loop(0, 4, body, 0)


def solve(
    parity, own2d, odd2d, even2d, odd_lat, even_lat, own_b, odd_b, even_b, height
):
    row, lane = rows_of(), lanes_of()
    lon_even, lat_even = parity[0] == 0, parity[1] == 0
    lower = [jnp.where(lon_even, odd_b[8 * i : 8 * i + 8, :], even_b[8 * i : 8 * i + 8, :]) for i in range(10)]
    upper = [jnp.where(lon_even, even_b[8 * i : 8 * i + 8, :], odd_b[8 * i : 8 * i + 8, :]) for i in range(10)]
    own = [own_b[8 * i : 8 * i + 8, :] for i in range(5)]

    ext_r = [four(even_lat, f * 32, lat_even, odd_lat) for f in (0, 2, 3)]
    ext_l = [four(odd_lat, f * 32, lat_even, even_lat) for f in (0, 2, 3)]

    def lon_part(vel, wet, x1, x2):
        slope = jnp.where(row == 0, -8.0 * x1, jnp.where(row == 7, 8.0 * x1, 0.0))
        slope = slope + jnp.where(row < 2, x2, jnp.where(row >= 6, -x2, 0.0))
        near = jnp.where((row == 0) | (row == 7), x1, 0.0)
        return 0.005 * jnp.where(wet, near, 0.0) - ADV * vel * slope

    def rim_rows(tile, q, first):
        return by_rows(tile[5 + q // 4], first - 2 * (q % 4))

    def side_parts(ext, base, own_depth, near_depth):
        mine = theirs = jnp.zeros((ROWS, LANES), F32)
        for i in range(4):
            vel, w = ext[0][i], scalar_mix(ext[1][i], ext[2][i])
            qu, qw = base + i, 8 + base + i
            x2 = jnp.where(row < 4, rim_rows(lower, qw, 0), rim_rows(upper, qw, 6))
            x1 = jnp.where(row < 4, rim_rows(lower, qw, -1), rim_rows(upper, qw, 7))
            mine = mine + lon_part(vel, wet_pack(own_depth, i), x1, x2)
            y2 = jnp.where(row < 4, by_rows(w, 2), by_rows(w, -2))
            y1 = jnp.where(row < 4, by_rows(w, 1), by_rows(w, -1))
            other = jnp.where(row < 4, rim_rows(upper, qu, 0), rim_rows(lower, qu, 6))
            theirs = theirs + lon_part(other, wet_pack(near_depth, i), y1, y2)
        return 0.1 * sum_slots(mine), 0.1 * sum_slots(theirs)

    near_side = jnp.where(row < 4, upper[4], lower[4])
    mine_r, theirs_r = side_parts(ext_r, 0, tile_lanes(own[4]), tile_lanes(near_side))
    mine_l, theirs_l = side_parts(
        ext_l, 4, tile_lanes(by_lanes(own[4], 8)), tile_lanes(by_lanes(near_side, 8))
    )
    in_r, in_l = lane < 8, lane >= 120
    mine = jnp.where(in_r, mine_r, jnp.where(in_l, mine_l, 0.0))
    theirs = jnp.where(in_r, theirs_r, jnp.where(in_l, theirs_l, 0.0))

    flat_own = [own2d[8 * i : 8 * i + 8, :] for i in range(3)]
    flat_low = [jnp.where(lon_even, odd2d[8 * i : 8 * i + 8, :], even2d[8 * i : 8 * i + 8, :]) for i in range(3)]
    flat_up = [jnp.where(lon_even, even2d[8 * i : 8 * i + 8, :], odd2d[8 * i : 8 * i + 8, :]) for i in range(3)]

    rhs = [
        lower[0], own[0], upper[0],
        lower[1] + jnp.where(row >= 6, theirs, 0.0),
        own[1] + mine,
        upper[1] + jnp.where(row < 2, theirs, 0.0),
    ]
    elev = [flat_low[0], flat_own[0], flat_up[0], lower[2], own[2], upper[2]]
    diag = [flat_low[1], flat_own[1], flat_up[1], lower[3], own[3], upper[3]]
    wet = [x > 0.0 for x in (flat_low[2], flat_own[2], flat_up[2], lower[4], own[4], upper[4])]
    diag = [x + 4.0 for x in diag]
    inverse = [1.0 / x for x in diag]

    def neighbours(x):
        out = []
        up = [by_rows(y, -1) for y in x]
        down = [by_rows(y, 1) for y in x]
        east = [by_lanes(y, -1) for y in x]
        west = [by_lanes(y, 1) for y in x]
        for i in range(6):
            h, c = divmod(i, 3)
            base = 3 * h
            other = 3 * (1 - h) + c
            n = jnp.where(row < 7, up[i], up[base + (c + 1) % 3])
            p = jnp.where(row > 0, down[i], down[base + (c + 2) % 3])
            e = jnp.where(lane < 127, east[i], east[other])
            w = jnp.where(lane > 0, west[i], west[other])
            out.append((n + p) + (e + w))
        return out

    sigma = SPECTRUM_MID / SPECTRUM_HALF
    ratio = 1.0 / sigma
    residual = rhs
    previous = elev
    iterate = elev[1]
    for step in range(ITERS):
        around = neighbours([jnp.where(a, x, 0.0) for a, x in zip(wet, previous, strict=True)])
        residual = [
            res - (d * x - jnp.where(a, n, 0.0))
            for res, d, x, a, n in zip(residual, diag, previous, wet, around, strict=True)
        ]
        if step == 0:
            previous = [res * inv / SPECTRUM_MID for res, inv in zip(residual, inverse, strict=True)]
        else:
            following = 1.0 / (2.0 * sigma - ratio)
            keep, gain = following * ratio, 2.0 * following / SPECTRUM_HALF
            previous = [
                keep * x + gain * res * inv
                for x, res, inv in zip(previous, residual, inverse, strict=True)
            ]
            ratio = following
        iterate = iterate + previous[1]
    height[...] = iterate


def shaped(*shape):
    return jax.ShapeDtypeStruct(shape, F32)


def part(rows, index=0):
    return pl.BlockSpec((rows, LANES), lambda i: (index, 0))


def call(kernel, outs, ins, flops, moved, grid=()):
    return pl.pallas_call(
        kernel,
        grid=grid,
        out_shape=outs,
        in_specs=ins,
        compiler_params=pltpu.CompilerParams(vmem_limit_bytes=VMEM),
        cost_estimate=pl.CostEstimate(flops=flops, bytes_accessed=moved, transcendentals=0),
    )


def on_device(u, v, t, s, water, layers, diag, elev):
    lon, lat = lax.axis_size("lon"), lax.axis_size("lat")
    lon_even = [(i, i ^ 1) for i in range(lon)]
    lon_odd = [(i, (((i + 1) ^ 1) - 1) % lon) for i in range(lon)]
    lat_even = [(i, i ^ 1) for i in range(lat)]
    lat_odd = [(i, ((i + 1) ^ 1) - 1) for i in range(1, lat - 1)]
    parity = jnp.stack([lax.axis_index("lon") % 2, lax.axis_index("lat") % 2]).astype(jnp.int32)

    smem = pl.BlockSpec(memory_space=pltpu.SMEM)
    whole = pl.BlockSpec(memory_space=pltpu.VMEM)
    block = 4 * LEVELS * ROWS * LANES * 4
    raw = (u, v, t, s, water, layers, diag, elev)

    own_odd, own_even = call(
        pack_lon, (shaped(LON_ROWS, LANES),) * 2, [whole] * 8 + [smem], 10**6, 2 * block
    )(*raw, parity)
    got_odd = lax.ppermute(own_odd, "lon", lon_odd)
    got_even = lax.ppermute(own_even, "lon", lon_even)
    lat_own_odd, lat_own_even, partial = call(
        pack_lat,
        (shaped(LAT_ROWS, LANES), shaped(LAT_ROWS, LANES), shaped(ROWS, LANES)),
        [whole] * 8 + [smem], 4 * 10**6, block,
    )(*raw, parity)
    lat_got_odd = lax.ppermute(lat_own_odd, "lat", lat_odd)
    lat_got_even = lax.ppermute(lat_own_even, "lat", lat_even)

    own2d, odd2d, even2d = (x[4 * STRIP :] for x in (own_odd, got_odd, got_even))
    b_odd, b_even = call(
        forcing, (shaped(SOLVE_ROWS, LANES),) * 2,
        [smem, part(STRIP), part(STRIP), part(2 * STRIP, 1), part(2 * STRIP, 1)] + [whole] * 6,
        10**6, 10**6, grid=(1,),
    )(
        parity, own_odd, own_even, got_odd, got_even, own2d,
        lat_own_odd, lat_own_even, lat_got_odd, lat_got_even, partial,
    )
    b_got_odd = lax.ppermute(b_odd, "lon", lon_odd)
    b_got_even = lax.ppermute(b_even, "lon", lon_even)

    fresh = call(
        fields, (shaped(LEVELS, ROWS, LANES),) * 4, [smem] + [whole] * 10, 10**7, 3 * block
    )(parity, u, v, t, s, water, layers, got_odd, got_even, lat_got_odd, lat_got_even)

    height = call(solve, shaped(ROWS, LANES), [smem] + [whole] * 8, 10**6, 10**6)(
        parity, own2d, odd2d, even2d, lat_got_odd, lat_got_even, b_odd, b_got_odd, b_got_even
    )
    return (*fresh, height)


def solution(mesh):
    field, flat = P(None, "lon", "lat"), P("lon", "lat")
    return jax.shard_map(
        on_device,
        mesh=mesh,
        in_specs=(field,) * 4 + (flat,) * 4,
        out_specs=(field,) * 4 + (flat,),
        check_vma=False,
    )
```

time: 228 us -> 63.7 us (0.28)
  the two profiles are of different devices: /device:TPU:5 before, /device:TPU:4 now
where the time goes in v1:
time: 63.7 us; the launch traced here: 63.3 us
  starting transfers between devices  38.3 us (60%)
  Pallas kernels  18.8 us (30%)
  local copies, waits for them, and re-layouts  4.43 us (7%)
  waiting for transfers between devices  0.88 us (1%)
  between operations  0.83 us (1%)
    ppermute x1, starting transfers between devices, on_device(): got_odd = lax.ppermute(own_odd, 'lon', lon_odd)  18.7 us
    pallas_call x1, Pallas kernels, on_device(): call(fields, (shaped(LEVELS, ROWS, LANES),) * 4, [smem] + [whole] * 10, 1...  12.8 us
    ppermute x1, starting transfers between devices, on_device(): b_got_odd = lax.ppermute(b_odd, 'lon', lon_odd)  5.89 us
    ppermute x1, starting transfers between devices, on_device(): got_even = lax.ppermute(own_even, 'lon', lon_even)  5.19 us
    ppermute x1, starting transfers between devices, on_device(): lat_got_even = lax.ppermute(lat_own_even, 'lat', lat_even)  4.74 us
    unnamed x24, local copies, waits for them, and re-layouts  4.42 us
    pallas_call x1, Pallas kernels, on_device(): call(solve, shaped(ROWS, LANES), [smem] + [whole] * 8, 10 ** 6, 10 ** 6)  2.32 us
    ppermute x1, starting transfers between devices, on_device(): lat_got_odd = lax.ppermute(lat_own_odd, 'lat', lat_odd)  1.94 us
  transfers between devices with their start and end apart: 6, of which 1 were waited for; matrix products, arithmetic and copies ran while one was open for 0% of the time, Pallas kernels for 23%

profile of v1, /device:TPU:4, one launch (start us, length us, event | category | flops | bytes accessed | tf_op | source)
XLA Modules:
  0.0 63.3 jit_solution(10226473077239569712)
XLA Ops:
  0.7 0.1 pad_add_fusion.parity
  0.8 0.6 copy-done.11
  1.3 0.0 copy-done.10
  1.3 0.0 copy-done.9
  1.4 0.0 copy-done.8
  1.4 0.9 %copy-done = f32[62,8,128]{2,1,0:T(8,128)S(1)} copy-done((f32[62,8,128]{2,1,0:T(8,128)S(1)}, f32[62,8,128]{2,1,0:T(8,128)}, u32[]{:S(2)}) %copy-start) | copy-done | bytes 253976
  2.3 0.9 %copy-done.2 = f32[62,8,128]{2,1,0:T(8,128)S(1)} copy-done((f32[62,8,128]{2,1,0:T(8,128)S(1)}, f32[62,8,128]{2,1,0:T(8,128)}, u32[]{:S(2)}) %copy-start.2) | copy-done | bytes 253976
  3.3 0.9 %copy-done.4 = f32[62,8,128]{2,1,0:T(8,128)S(1)} copy-done((f32[62,8,128]{2,1,0:T(8,128)S(1)}, f32[62,8,128]{2,1,0:T(8,128)}, u32[]{:S(2)}) %copy-start.4) | copy-done | bytes 253976
  4.2 0.9 %copy-done.6 = f32[62,8,128]{2,1,0:T(8,128)S(1)} copy-done((f32[62,8,128]{2,1,0:T(8,128)S(1)}, f32[62,8,128]{2,1,0:T(8,128)}, u32[]{:S(2)}) %copy-start.6) | copy-done | bytes 253976
  5.2 0.8 %shard_map.119 = (f32[536,128]{1,0:T(8,128)S(1)}, f32[536,128]{1,0:T(8,128)S(1)}) custom-call(f32[62,8,128]{2,1,0:T(8,128)S(1)} %copy-done, f32[62,8,128]{2,1,0:T(8,128)S(1)} %copy-done.2, f32[62,8,128]{2,1,0:T(8,128)S(1)} %copy-done.4, f32[62,8,128]{2,1,0:T(8,128)S(1)} %copy-done.6, s32[8,128]{1,0:T(8,128)S(1)} %copy-done.8, s32[8,128]{1,0:T(8,128)S(1)} %copy-done.9, ...), custom_call_target="tpu_custom_call" | custom-call | flops 1000000 | bytes 2031616 | tf_op jit(solution)/shard_map/pallas_call | solution.py:463
  6.0 5.2 %collective-permute-start.1 = (f32[536,128]{1,0:T(8,128)S(1)}, f32[536,128]{1,0:T(8,128)S(1)}, u32[]{:S(2)}, u32[]{:S(2)}) collective-permute-start(f32[536,128]{1,0:T(8,128)S(1)} %get-tuple-element.17.own_even_u), channel_id=1, source_target_pairs={{0,8},{8,0},{16,24},{24,16},{32,40},{40,32},{48,56},{56,48},{64,72... | collective-permute-start | bytes 823304 | tf_op jit(solution)/shard_map/ppermute | solution.py:467
  11.2 18.7 %collective-permute-start = (f32[536,128]{1,0:T(8,128)S(1)}, f32[536,128]{1,0:T(8,128)S(1)}, u32[]{:S(2)}, u32[]{:S(2)}) collective-permute-start(f32[536,128]{1,0:T(8,128)S(1)} %get-tuple-element.16.own_odd_u), channel_id=1, source_target_pairs={{0,1016},{8,16},{16,8},{24,32},{32,24},{40,48},{48,40},{56,64},{64... | collective-permute-start | bytes 823304 | tf_op jit(solution)/shard_map/ppermute | solution.py:466
  29.9 1.7 %shard_map.120 = (f32[136,128]{1,0:T(8,128)S(1)}, f32[136,128]{1,0:T(8,128)S(1)}, f32[8,128]{1,0:T(8,128)S(1)}) custom-call(f32[62,8,128]{2,1,0:T(8,128)S(1)} %copy-done, f32[62,8,128]{2,1,0:T(8,128)S(1)} %copy-done.2, f32[62,8,128]{2,1,0:T(8,128)S(1)} %copy-done.4, f32[62,8,128]{2,1,0:T(8,128)S(1)} %copy-done.6, s32[8,128]{1,0:T(8,128)S(1)} %copy-done.8, ...), custom_call_target="tpu_custom_call" | custom-call | flops 4000000 | bytes 1015808 | tf_op jit(solution)/shard_map/pallas_call | solution.py:468
  31.5 1.9 %collective-permute-start.2 = (f32[136,128]{1,0:T(8,128)S(1)}, f32[136,128]{1,0:T(8,128)S(1)}, u32[]{:S(2)}, u32[]{:S(2)}) collective-permute-start(f32[136,128]{1,0:T(8,128)S(1)} %get-tuple-element.18.own_odd_lat), channel_id=1, source_target_pairs={{1,2},{2,1},{3,4},{4,3},{5,6},{6,5},{9,10},{10,9},{11,12},{12,11},... | collective-permute-start | bytes 208904 | tf_op jit(solution)/shard_map/ppermute | solution.py:473
  33.5 4.7 %collective-permute-start.3 = (f32[136,128]{1,0:T(8,128)S(1)}, f32[136,128]{1,0:T(8,128)S(1)}, u32[]{:S(2)}, u32[]{:S(2)}) collective-permute-start(f32[136,128]{1,0:T(8,128)S(1)} %get-tuple-element.19.own_even_lat), channel_id=1, source_target_pairs={{0,1},{1,0},{2,3},{3,2},{4,5},{5,4},{6,7},{7,6},{8,9},{9,8},{10,11... | collective-permute-start | bytes 208904 | tf_op jit(solution)/shard_map/ppermute | solution.py:474
  38.3 0.9 %collective-permute-done.3.even_lat.got_even_lat = f32[136,128]{1,0:T(8,128)S(1)} collective-permute-done((f32[136,128]{1,0:T(8,128)S(1)}, f32[136,128]{1,0:T(8,128)S(1)}, u32[]{:S(2)}, u32[]{:S(2)}) %collective-permute-start.3) | collective-permute-done | bytes 69664 | tf_op jit(solution)/shard_map/ppermute | solution.py:474
  39.1 0.0 collective-permute-done.1.even_lon.got_even_ts
  39.1 0.0 copy-start.5
  39.2 0.0 copy-start.7
  39.2 1.2 %shard_map.122 = (f32[80,128]{1,0:T(8,128)S(1)}, f32[80,128]{1,0:T(8,128)S(1)}) custom-call(s32[2]{0:T(128)S(1)} %pad_add_fusion.parity, f32[536,128]{1,0:T(8,128)S(1)} %get-tuple-element.16.own_odd_u, f32[536,128]{1,0:T(8,128)S(1)} %get-tuple-element.17.own_even_u, f32[536,128]{1,0:T(8,128)S(1)} %collective-permute-done.odd_lon.got_odd_ts, ...), custom_call_target="tpu_custom_call" | custom-call | flops 1000000 | bytes 1000000 | tf_op jit(solution)/shard_map/pallas_call | solution.py:477
  40.4 1.9 %collective-permute-start.5 = (f32[80,128]{1,0:T(8,128)S(1)}, f32[80,128]{1,0:T(8,128)S(1)}, u32[]{:S(2)}, u32[]{:S(2)}) collective-permute-start(f32[80,128]{1,0:T(8,128)S(1)} %get-tuple-element.26), channel_id=1, source_target_pairs={{0,8},{8,0},{16,24},{24,16},{32,40},{40,32},{48,56},{56,48},{64,72... | collective-permute-start | bytes 122888 | tf_op jit(solution)/shard_map/ppermute | solution.py:486
  42.3 5.9 %collective-permute-start.4 = (f32[80,128]{1,0:T(8,128)S(1)}, f32[80,128]{1,0:T(8,128)S(1)}, u32[]{:S(2)}, u32[]{:S(2)}) collective-permute-start(f32[80,128]{1,0:T(8,128)S(1)} %get-tuple-element.25.own_b), channel_id=1, source_target_pairs={{0,1016},{8,16},{16,8},{24,32},{32,24},{40,48},{48,40},{56,64},{64... | collective-permute-start | bytes 122888 | tf_op jit(solution)/shard_map/ppermute | solution.py:485
  48.2 12.8 %shard_map.121 = (f32[62,8,128]{2,1,0:T(8,128)}, f32[62,8,128]{2,1,0:T(8,128)}, f32[62,8,128]{2,1,0:T(8,128)}, f32[62,8,128]{2,1,0:T(8,128)}) custom-call(s32[2]{0:T(128)S(1)} %pad_add_fusion.parity, f32[62,8,128]{2,1,0:T(8,128)S(1)} %copy-done.1, f32[62,8,128]{2,1,0:T(8,128)S(1)} %copy-done.3, f32[62,8,128]{2,1,0:T(8,128)S(1)} %copy-done.5, ...), custom_call_target="tpu_custom_call" | custom-call | flops 10000000 | bytes 3047424 | tf_op jit(solution)/shard_map/pallas_call | solution.py:488
  61.0 2.3 %shard_map.123 = f32[8,128]{1,0:T(8,128)} custom-call(s32[2]{0:T(128)S(1)} %pad_add_fusion.parity, f32[24,128]{1,0:T(8,128)S(1)} %slice.9.flat2d.own2d, f32[24,128]{1,0:T(8,128)S(1)} %slice.12.odd2d, f32[24,128]{1,0:T(8,128)S(1)} %slice.13.even2d, f32[136,128]{1,0:T(8,128)S(1)} %collective-permute-done.2.odd_lat.got_odd_lat, ...), custom_call_target="tpu_custom_call" | custom-call | flops 1000000 | bytes 1000000 | tf_op jit(solution)/shard_map/pallas_call | solution.py:492
  (21 shorter events, 0.0 us)
Async XLA Ops:
  0.6 0.7 %copy-start.11 = (f32[8,128]{1,0:T(8,128)S(1)}, f32[8,128]{1,0:T(8,128)}, u32[]{:S(2)}) copy-start(f32[8,128]{1,0:T(8,128)} %elev.3) | copy-start | bytes 12292
  0.7 0.7 %copy-start.10 = (f32[8,128]{1,0:T(8,128)S(1)}, f32[8,128]{1,0:T(8,128)}, u32[]{:S(2)}) copy-start(f32[8,128]{1,0:T(8,128)} %diag.3) | copy-start | bytes 12292
  0.7 0.7 %copy-start.9 = (s32[8,128]{1,0:T(8,128)S(1)}, s32[8,128]{1,0:T(8,128)}, u32[]{:S(2)}) copy-start(s32[8,128]{1,0:T(8,128)} %layers.5) | copy-start | bytes 12292
  0.7 0.7 %copy-start.8 = (s32[8,128]{1,0:T(8,128)S(1)}, s32[8,128]{1,0:T(8,128)}, u32[]{:S(2)}) copy-start(s32[8,128]{1,0:T(8,128)} %water.5) | copy-start | bytes 12292
  1.4 0.9 %copy-start = (f32[62,8,128]{2,1,0:T(8,128)S(1)}, f32[62,8,128]{2,1,0:T(8,128)}, u32[]{:S(2)}) copy-start(f32[62,8,128]{2,1,0:T(8,128)} %u.5) | copy-start | bytes 761860
  2.3 0.9 %copy-start.2 = (f32[62,8,128]{2,1,0:T(8,128)S(1)}, f32[62,8,128]{2,1,0:T(8,128)}, u32[]{:S(2)}) copy-start(f32[62,8,128]{2,1,0:T(8,128)} %v.5) | copy-start | bytes 761860
  3.3 0.9 %copy-start.4 = (f32[62,8,128]{2,1,0:T(8,128)S(1)}, f32[62,8,128]{2,1,0:T(8,128)}, u32[]{:S(2)}) copy-start(f32[62,8,128]{2,1,0:T(8,128)} %t.5) | copy-start | bytes 761860
  4.2 0.9 %copy-start.6 = (f32[62,8,128]{2,1,0:T(8,128)S(1)}, f32[62,8,128]{2,1,0:T(8,128)}, u32[]{:S(2)}) copy-start(f32[62,8,128]{2,1,0:T(8,128)} %s.5) | copy-start | bytes 761860
  6.0 33.1 %collective-permute-start.1 = (f32[536,128]{1,0:T(8,128)S(1)}, f32[536,128]{1,0:T(8,128)S(1)}, u32[]{:S(2)}, u32[]{:S(2)}) collective-permute-start(f32[536,128]{1,0:T(8,128)S(1)} %get-tuple-element.17.own_even_u), channel_id=1, source_target_pairs={{0,8},{8,0},{16,24},{24,16},{32,40},{40,32},{48,56},{56,48},{64,72... | collective-permute-start | bytes 823304 | tf_op jit(solution)/shard_map/ppermute | solution.py:467
  11.2 27.9 %collective-permute-start = (f32[536,128]{1,0:T(8,128)S(1)}, f32[536,128]{1,0:T(8,128)S(1)}, u32[]{:S(2)}, u32[]{:S(2)}) collective-permute-start(f32[536,128]{1,0:T(8,128)S(1)} %get-tuple-element.16.own_odd_u), channel_id=1, source_target_pairs={{0,1016},{8,16},{16,8},{24,32},{32,24},{40,48},{48,40},{56,64},{64... | collective-permute-start | bytes 823304 | tf_op jit(solution)/shard_map/ppermute | solution.py:466
  31.5 6.7 %collective-permute-start.2 = (f32[136,128]{1,0:T(8,128)S(1)}, f32[136,128]{1,0:T(8,128)S(1)}, u32[]{:S(2)}, u32[]{:S(2)}) collective-permute-start(f32[136,128]{1,0:T(8,128)S(1)} %get-tuple-element.18.own_odd_lat), channel_id=1, source_target_pairs={{1,2},{2,1},{3,4},{4,3},{5,6},{6,5},{9,10},{10,9},{11,12},{12,11},... | collective-permute-start | bytes 208904 | tf_op jit(solution)/shard_map/ppermute | solution.py:473
  33.5 5.6 %collective-permute-start.3 = (f32[136,128]{1,0:T(8,128)S(1)}, f32[136,128]{1,0:T(8,128)S(1)}, u32[]{:S(2)}, u32[]{:S(2)}) collective-permute-start(f32[136,128]{1,0:T(8,128)S(1)} %get-tuple-element.19.own_even_lat), channel_id=1, source_target_pairs={{0,1},{1,0},{2,3},{3,2},{4,5},{5,4},{6,7},{7,6},{8,9},{9,8},{10,11... | collective-permute-start | bytes 208904 | tf_op jit(solution)/shard_map/ppermute | solution.py:474
  39.1 9.1 %copy-start.1 = (f32[62,8,128]{2,1,0:T(8,128)S(1)}, f32[62,8,128]{2,1,0:T(8,128)}, u32[]{:S(2)}) copy-start(f32[62,8,128]{2,1,0:T(8,128)} %u.5) | copy-start | bytes 761860
  39.1 9.1 %copy-start.3 = (f32[62,8,128]{2,1,0:T(8,128)S(1)}, f32[62,8,128]{2,1,0:T(8,128)}, u32[]{:S(2)}) copy-start(f32[62,8,128]{2,1,0:T(8,128)} %v.5) | copy-start | bytes 761860
  39.1 9.1 %copy-start.5 = (f32[62,8,128]{2,1,0:T(8,128)S(1)}, f32[62,8,128]{2,1,0:T(8,128)}, u32[]{:S(2)}) copy-start(f32[62,8,128]{2,1,0:T(8,128)} %t.5) | copy-start | bytes 761860
  39.2 9.1 %copy-start.7 = (f32[62,8,128]{2,1,0:T(8,128)S(1)}, f32[62,8,128]{2,1,0:T(8,128)}, u32[]{:S(2)}) copy-start(f32[62,8,128]{2,1,0:T(8,128)} %s.5) | copy-start | bytes 761860
  40.4 20.6 %collective-permute-start.5 = (f32[80,128]{1,0:T(8,128)S(1)}, f32[80,128]{1,0:T(8,128)S(1)}, u32[]{:S(2)}, u32[]{:S(2)}) collective-permute-start(f32[80,128]{1,0:T(8,128)S(1)} %get-tuple-element.26), channel_id=1, source_target_pairs={{0,8},{8,0},{16,24},{24,16},{32,40},{40,32},{48,56},{56,48},{64,72... | collective-permute-start | bytes 122888 | tf_op jit(solution)/shard_map/ppermute | solution.py:486
  42.3 18.7 %collective-permute-start.4 = (f32[80,128]{1,0:T(8,128)S(1)}, f32[80,128]{1,0:T(8,128)S(1)}, u32[]{:S(2)}, u32[]{:S(2)}) collective-permute-start(f32[80,128]{1,0:T(8,128)S(1)} %get-tuple-element.25.own_b), channel_id=1, source_target_pairs={{0,1016},{8,16},{16,8},{24,32},{32,24},{40,48},{48,40},{56,64},{64... | collective-permute-start | bytes 122888 | tf_op jit(solution)/shard_map/ppermute | solution.py:485

commit v2 on v1

--- a/solution.py
+++ b/solution.py
@@ -13,7 +13,8 @@
 ROWS = 8
 LANES = 128
 STRIP = 128
-LON_ROWS = 4 * STRIP + 3 * ROWS
+FLAT = 4 * STRIP
+LON_ROWS = FLAT + 3 * ROWS
 LAT_ROWS = 17 * ROWS
 SOLVE_ROWS = 5 * ROWS + 32 + 8
 VMEM = 12 * 1024 * 1024
@@ -48,39 +49,62 @@
     return lax.axis_index(axis) % 2 == 0
 
 
-def pack_lon(u, v, t, s, water, layers, diag, elev, parity, up_first, low_first):
+def pack_lon(
+    u, v, t, s, water, layers, diag, elev, parity, masked, up_first, low_first, held, held_int, held_flat, sems
+):
+    copies = [
+        pltpu.make_async_copy(src, held.at[i], sems.at[i]) for i, src in enumerate((u, v, t, s))
+    ]
+    small = [
+        pltpu.make_async_copy(water, held_int.at[0], sems.at[4]),
+        pltpu.make_async_copy(layers, held_int.at[1], sems.at[5]),
+        pltpu.make_async_copy(elev, held_flat.at[0], sems.at[6]),
+        pltpu.make_async_copy(diag, held_flat.at[1], sems.at[7]),
+    ]
+    for copy in small + copies:
+        copy.start()
+    for copy in small:
+        copy.wait()
     row = rows_of()
     group = row >> 1
-    depth = water[...] * layers[...]
+    depth = held_int[0] * held_int[1]
     is_even = parity[0] == 0
-
-    def body(g, carry):
-        for f, ref in enumerate((u, v, t, s)):
-            top = None
+    for ref in (up_first, low_first):
+        ref[FLAT : FLAT + 8, :] = held_flat[0]
+        ref[FLAT + 8 : FLAT + 16, :] = held_flat[1]
+        ref[FLAT + 16 : FLAT + 24, :] = depth.astype(F32)
+
+    for f in range(4):
+        masked[f, 0] = jnp.zeros((ROWS, LANES), F32)
+        masked[f, LEVELS + 3] = jnp.zeros((ROWS, LANES), F32)
+        copies[f].wait()
+
+        def body(g, carry, f=f):
+            top = bottom = None
             for i in range(4):
                 k = 4 * g + i
-                m = jnp.where(k < depth, ref[jnp.minimum(k, LEVELS - 1)], 0.0)
+                m = jnp.where(k < depth, held[f, jnp.minimum(k, LEVELS - 1)], 0.0)
+                masked[f, k + 1] = m
                 a, b = by_rows(m, 2 * i), by_rows(m, 2 * i - 6)
-                if top is None:
-                    top, bottom = a, b
-                else:
-                    top, bottom = jnp.where(group == i, a, top), jnp.where(group == i, b, bottom)
+                top = a if i == 0 else jnp.where(group == i, a, top)
+                bottom = b if i == 0 else jnp.where(group == i, b, bottom)
             at = pl.ds(pl.multiple_of(f * STRIP + 8 * g, 8), 8)
             up_first[at, :] = jnp.where(is_even, top, bottom)
             low_first[at, :] = jnp.where(is_even, bottom, top)
-        return carry
-
-    lax.fori_loop(0, 16, body, 0)
-    for ref in (up_first, low_first):
-        ref[4 * STRIP : 4 * STRIP + 8, :] = elev[...]
-        ref[4 * STRIP + 8 : 4 * STRIP + 16, :] = diag[...]
-        ref[4 * STRIP + 16 : 4 * STRIP + 24, :] = depth.astype(F32)
-
-
-def pack_lat(u, v, t, s, water, layers, diag, elev, parity, odd_out, even_out, partial):
+            return carry
+
+        lax.fori_loop(0, 16, body, 0, unroll=4)
+
+
+def flat_of(ref):
+    return [ref[FLAT + 8 * i : FLAT + 8 * i + 8, :] for i in range(3)]
+
+
+def pack_lat(masked, own_lon, parity, odd_out, even_out, partial):
     row, lane = rows_of(), lanes_of()
     slot = lane >> 3
-    depth = water[...] * layers[...]
+    elev, diag, depth = flat_of(own_lon)
+    levels = depth.astype(jnp.int32)
     is_even = parity[1] == 0
 
     def body(a, acc):
@@ -88,9 +112,8 @@
         right = [None] * 4
         for i in range(16):
             k = 16 * a + i
-            wet = k < depth
-            at = jnp.minimum(k, LEVELS - 1)
-            m = [jnp.where(wet, ref[at], 0.0) for ref in (u, v, t, s)]
+            wet = k < levels
+            m = [masked[f, k + 1] for f in range(4)]
             for f in range(4):
                 x, y = by_lanes(m[f], 8 * i), by_lanes(m[f], 8 * i - 120)
                 left[f] = x if i == 0 else jnp.where(slot == i, x, left[f])
@@ -107,7 +130,7 @@
             gx = 8.0 * (n1 - p1) - (n2 - p2)
             gy = 8.0 * (e1 - q1) - (e2 - q2)
             around = jnp.where(wet, (n1 + p1) + (e1 + q1), 0.0)
-            column = jnp.where(k > 0, w, 0.0) + jnp.where(k + 1 < depth, w, 0.0)
+            column = jnp.where(k > 0, w, 0.0) + jnp.where(k + 1 < levels, w, 0.0)
             acc = acc + (
                 0.94 * w + 0.02 * column + 0.005 * around - ADV * (m[0] * gx + m[1] * gy)
             )
@@ -119,7 +142,7 @@
 
     acc = 0.1 * lax.fori_loop(0, 4, body, jnp.zeros((ROWS, LANES), F32))
     partial[...] = acc
-    flat = (acc, elev[...], diag[...], depth.astype(F32))
+    flat = (acc, elev, diag, depth)
     left = right = None
     for i, x in enumerate(flat):
         a, b = by_lanes(x, 8 * i), by_lanes(x, 8 * i - 120)
@@ -173,13 +196,13 @@
 
 
 def forcing(
-    parity, own_odd_u, own_even_u, got_odd_ts, got_even_ts, flat2d,
+    parity, got_even, got_odd, own_odd, own_even,
     own_odd_lat, own_even_lat, got_odd_lat, got_even_lat, partial,
     odd_out, even_out,
 ):
     row, lane = rows_of(), lanes_of()
     lon_even, lat_even = parity[0] == 0, parity[1] == 0
-    elev, diag, depth = (flat2d[8 * i : 8 * i + 8, :] for i in range(3))
+    elev, diag, depth = flat_of(own_odd)
     total = elev + partial[...]
 
     r = row & 1
@@ -192,12 +215,12 @@
         own_first = lon_even if lower else jnp.logical_not(lon_even)
         for g in range(16):
             at = slice(8 * g, 8 * g + 8)
-            also = slice(STRIP + 8 * g, STRIP + 8 * g + 8)
-            vel = jnp.where(own_first, own_odd_u[at, :], own_even_u[at, :])
-            w = jnp.where(
-                own_first,
-                scalar_mix(got_odd_ts[at, :], got_odd_ts[also, :]),
-                scalar_mix(got_even_ts[at, :], got_even_ts[also, :]),
+            at_t = slice(2 * STRIP + 8 * g, 2 * STRIP + 8 * g + 8)
+            at_s = slice(3 * STRIP + 8 * g, 3 * STRIP + 8 * g + 8)
+            vel = jnp.where(own_first, own_odd[at, :], own_even[at, :])
+            w = scalar_mix(
+                jnp.where(own_first, got_odd[at_t, :], got_even[at_t, :]),
+                jnp.where(own_first, got_odd[at_s, :], got_even[at_s, :]),
             )
             wet = (4 * g + (row >> 1)).astype(F32) < tiled
             if lower:
@@ -261,73 +284,87 @@
         even_out[at, :] = jnp.where(lon_even, bottom, top)
 
 
+CHUNKS = ((0, 5), (5, 10), (10, 15))
+
+
 def fields(
-    parity, u, v, t, s, water, layers, odd_lon, even_lon, odd_lat, even_lat, *outs
+    parity, masked, own_lon, odd_lon, even_lon, odd_lat, even_lat, o1, o2, o3, o4, rims, fresh, sems
 ):
     row, lane = rows_of(), lanes_of()
-    depth = water[...] * layers[...]
+    levels = flat_of(own_lon)[2].astype(jnp.int32)
     lon_even, lat_even = parity[0] == 0, parity[1] == 0
-    refs = (u, v, t, s)
-
-    def level(a, i, strips, packs):
-        k = 16 * a + i
-        wet = k < depth
-        wet_below = k + 1 < depth
-        below, above = jnp.minimum(k + 1, LEVELS - 1), jnp.maximum(k - 1, 0)
-        center = [jnp.where(wet, ref[k], 0.0) for ref in refs]
-        j = i % 4
-        for f in range(4):
-            m = center[f]
-            upper, lower = strips[f]
-            rim = jnp.where(row < 4, by_rows(upper, -2 * j), by_rows(lower, 6 - 2 * j))
-            n1 = by_rows(jnp.where(row < 1, rim, m), -1)
-            n2 = by_rows(jnp.where(row < 2, rim, m), -2)
-            p1 = by_rows(jnp.where(row > 6, rim, m), 1)
-            p2 = by_rows(jnp.where(row > 5, rim, m), 2)
-            west, east = packs[f]
-            beside = jnp.where(lane < 64, by_lanes(east, -8 * i), by_lanes(west, 120 - 8 * i))
-            e1 = by_lanes(jnp.where(lane < 1, beside, m), -1)
-            e2 = by_lanes(jnp.where(lane < 2, beside, m), -2)
-            q1 = by_lanes(jnp.where(lane > 126, beside, m), 1)
-            q2 = by_lanes(jnp.where(lane > 125, beside, m), 2)
-            gx = 8.0 * (n1 - p1) - (n2 - p2)
-            gy = 8.0 * (e1 - q1) - (e2 - q2)
-            around = (n1 + p1) + (e1 + q1)
-            column = jnp.where(wet_below, refs[f][below], 0.0) + jnp.where(
-                k > 0, refs[f][above], 0.0
-            )
-            fresh = (
-                0.94 * m
-                + 0.02 * column
-                + 0.005 * around
-                - ADV * (center[0] * gx + center[1] * gy)
-            )
-            outs[f][k] = jnp.where(wet, fresh, 0.0)
-
-    def body(a, carry):
-        packs = []
+    outs = (o1, o2, o3, o4)
+
+    def unpack(a, carry):
         for f in range(4):
             at = pl.ds(pl.multiple_of(f * 32 + 8 * a, 8), 8)
             x, y = odd_lat[at, :], even_lat[at, :]
-            packs.append((jnp.where(lat_even, x, y), jnp.where(lat_even, y, x)))
-        for b in range(4):
-            strips = []
+            west, east = jnp.where(lat_even, x, y), jnp.where(lat_even, y, x)
+            for i in range(16):
+                rims[f, 16 * a + i] = jnp.where(
+                    lane < 64, by_lanes(east, -8 * i), by_lanes(west, 120 - 8 * i)
+                )
+        return carry
+
+    lax.fori_loop(0, 4, unpack, 0)
+
+    def group(g, count):
+        strips = []
+        for f in range(4):
+            at = pl.ds(pl.multiple_of(f * STRIP + 8 * g, 8), 8)
+            x, y = odd_lon[at, :], even_lon[at, :]
+            strips.append((jnp.where(lon_even, y, x), jnp.where(lon_even, x, y)))
+        for j in range(count):
+            k = 4 * g + j
+            wet = k < levels
+            center = [masked[f, k + 1] for f in range(4)]
+            zonal, merid = ADV * center[0], ADV * center[1]
             for f in range(4):
-                at = pl.ds(pl.multiple_of(f * STRIP + 32 * a + 8 * b, 8), 8)
-                x, y = odd_lon[at, :], even_lon[at, :]
-                strips.append((jnp.where(lon_even, y, x), jnp.where(lon_even, x, y)))
-            for i in range(4 * b, 4 * b + 4):
-                if i < 14:
-                    level(a, i, strips, packs)
-                else:
-                    pl.when(16 * a + i < LEVELS)(lambda i=i, s=strips: level(a, i, s, packs))
+                m = center[f]
+                upper, lower = strips[f]
+                rim = jnp.where(row < 4, by_rows(upper, -2 * j), by_rows(lower, 6 - 2 * j))
+                n1 = by_rows(jnp.where(row < 1, rim, m), -1)
+                n2 = by_rows(jnp.where(row < 2, rim, m), -2)
+                p1 = by_rows(jnp.where(row > 6, rim, m), 1)
+                p2 = by_rows(jnp.where(row > 5, rim, m), 2)
+                beside = rims[f, k]
+                e1 = by_lanes(jnp.where(lane < 1, beside, m), -1)
+                e2 = by_lanes(jnp.where(lane < 2, beside, m), -2)
+                q1 = by_lanes(jnp.where(lane > 126, beside, m), 1)
+                q2 = by_lanes(jnp.where(lane > 125, beside, m), 2)
+                gx = 8.0 * (n1 - p1) - (n2 - p2)
+                gy = 8.0 * (e1 - q1) - (e2 - q2)
+                around = (n1 + p1) + (e1 + q1)
+                column = masked[f, k] + masked[f, k + 2]
+                value = 0.94 * m + 0.02 * column + 0.005 * around - (zonal * gx + merid * gy)
+                fresh[f, k] = jnp.where(wet, value, 0.0)
+
+    def body(g, carry):
+        group(g, 4)
         return carry
 
-    lax.fori_loop(0, 4, body, 0)
+    copies = []
+
+    def send(first, last):
+        for f in range(4):
+            copies.append(
+                pltpu.make_async_copy(
+                    fresh.at[f, first:last], outs[f].at[first:last], sems.at[len(copies)]
+                )
+            )
+            copies[-1].start()
+
+    for first, last in CHUNKS:
+        lax.fori_loop(first, last, body, 0)
+        send(4 * first, 4 * last)
+    group(15, LEVELS - 60)
+    send(60, LEVELS)
+    for copy in copies:
+        copy.wait()
 
 
 def solve(
-    parity, own2d, odd2d, even2d, odd_lat, even_lat, own_b, odd_b, even_b, height
+    parity, odd_b, even_b, own_b, own_lon, odd_lon, even_lon, odd_lat, even_lat, height
 ):
     row, lane = rows_of(), lanes_of()
     lon_even, lat_even = parity[0] == 0, parity[1] == 0
@@ -370,9 +407,10 @@
     mine = jnp.where(in_r, mine_r, jnp.where(in_l, mine_l, 0.0))
     theirs = jnp.where(in_r, theirs_r, jnp.where(in_l, theirs_l, 0.0))
 
-    flat_own = [own2d[8 * i : 8 * i + 8, :] for i in range(3)]
-    flat_low = [jnp.where(lon_even, odd2d[8 * i : 8 * i + 8, :], even2d[8 * i : 8 * i + 8, :]) for i in range(3)]
-    flat_up = [jnp.where(lon_even, even2d[8 * i : 8 * i + 8, :], odd2d[8 * i : 8 * i + 8, :]) for i in range(3)]
+    flat_own = flat_of(own_lon)
+    flat_odd, flat_even = flat_of(odd_lon), flat_of(even_lon)
+    flat_low = [jnp.where(lon_even, x, y) for x, y in zip(flat_odd, flat_even, strict=True)]
+    flat_up = [jnp.where(lon_even, y, x) for x, y in zip(flat_odd, flat_even, strict=True)]
 
     rhs = [
         lower[0], own[0], upper[0],
@@ -385,6 +423,7 @@
     wet = [x > 0.0 for x in (flat_low[2], flat_own[2], flat_up[2], lower[4], own[4], upper[4])]
     diag = [x + 4.0 for x in diag]
     inverse = [1.0 / x for x in diag]
+    coupled = [jnp.where(a, x, 0.0) for a, x in zip(wet, inverse, strict=True)]
 
     def neighbours(x):
         out = []
@@ -405,24 +444,21 @@
 
     sigma = SPECTRUM_MID / SPECTRUM_HALF
     ratio = 1.0 / sigma
-    residual = rhs
+    scaled = [x * y for x, y in zip(rhs, inverse, strict=True)]
     previous = elev
     iterate = elev[1]
     for step in range(ITERS):
         around = neighbours([jnp.where(a, x, 0.0) for a, x in zip(wet, previous, strict=True)])
-        residual = [
-            res - (d * x - jnp.where(a, n, 0.0))
-            for res, d, x, a, n in zip(residual, diag, previous, wet, around, strict=True)
+        scaled = [
+            (res - x) + c * n
+            for res, x, c, n in zip(scaled, previous, coupled, around, strict=True)
         ]
         if step == 0:
-            previous = [res * inv / SPECTRUM_MID for res, inv in zip(residual, inverse, strict=True)]
+            previous = [res / SPECTRUM_MID for res in scaled]
         else:
             following = 1.0 / (2.0 * sigma - ratio)
             keep, gain = following * ratio, 2.0 * following / SPECTRUM_HALF
-            previous = [
-                keep * x + gain * res * inv
-                for x, res, inv in zip(previous, residual, inverse, strict=True)
-            ]
+            previous = [keep * x + gain * res for x, res in zip(previous, scaled, strict=True)]
             ratio = following
         iterate = iterate + previous[1]
     height[...] = iterate
@@ -432,19 +468,65 @@
     return jax.ShapeDtypeStruct(shape, F32)
 
 
-def part(rows, index=0):
-    return pl.BlockSpec((rows, LANES), lambda i: (index, 0))
-
-
-def call(kernel, outs, ins, flops, moved, grid=()):
+def call(kernel, outs, ins, flops, moved, **kw):
     return pl.pallas_call(
         kernel,
-        grid=grid,
         out_shape=outs,
         in_specs=ins,
         compiler_params=pltpu.CompilerParams(vmem_limit_bytes=VMEM),
         cost_estimate=pl.CostEstimate(flops=flops, bytes_accessed=moved, transcendentals=0),
-    )
+        **kw,
+    )
+
+
+SMEM = pl.BlockSpec(memory_space=pltpu.SMEM)
+WHOLE = pl.BlockSpec(memory_space=pltpu.VMEM)
+HERE = pl.BlockSpec(memory_space=pltpu.HBM)
+BLOCK = 4 * LEVELS * ROWS * LANES * 4
+
+
+def call_pack_lon(*args):
+    return call(
+        pack_lon,
+        (shaped(4, LEVELS + 4, ROWS, LANES), shaped(LON_ROWS, LANES), shaped(LON_ROWS, LANES)),
+        [HERE] * 8 + [SMEM], 10**6, 2 * BLOCK,
+        out_specs=(WHOLE,) * 3,
+        scratch_shapes=[
+            pltpu.VMEM((4, LEVELS, ROWS, LANES), F32),
+            pltpu.VMEM((2, ROWS, LANES), jnp.int32),
+            pltpu.VMEM((2, ROWS, LANES), F32),
+            pltpu.SemaphoreType.DMA((8,)),
+        ],
+    )(*args)
+
+
+def call_pack_lat(*args):
+    return call(
+        pack_lat, (shaped(LAT_ROWS, LANES), shaped(LAT_ROWS, LANES), shaped(ROWS, LANES)),
+        [WHOLE] * 2 + [SMEM], 4 * 10**6, BLOCK,
+    )(*args)
+
+
+def call_forcing(*args):
+    return call(
+        forcing, (shaped(SOLVE_ROWS, LANES),) * 2, [SMEM] + [WHOLE] * 9, 10**6, 10**6
+    )(*args)
+
+
+def call_fields(*args):
+    return call(
+        fields, (shaped(LEVELS, ROWS, LANES),) * 4, [SMEM] + [WHOLE] * 6, 10**7, 3 * BLOCK,
+        out_specs=(HERE,) * 4,
+        scratch_shapes=[
+            pltpu.VMEM((4, LEVELS + 2, ROWS, LANES), F32),
+            pltpu.VMEM((4, LEVELS, ROWS, LANES), F32),
+            pltpu.SemaphoreType.DMA((16,)),
+        ],
+    )(*args)
+
+
+def call_solve(*args):
+    return call(solve, shaped(ROWS, LANES), [SMEM] + [WHOLE] * 8, 10**6, 10**6)(*args)
 
 
 def on_device(u, v, t, s, water, layers, diag, elev):
@@ -453,44 +535,29 @@
     lon_odd = [(i, (((i + 1) ^ 1) - 1) % lon) for i in range(lon)]
     lat_even = [(i, i ^ 1) for i in range(lat)]
     lat_odd = [(i, ((i + 1) ^ 1) - 1) for i in range(1, lat - 1)]
-    parity = jnp.stack([lax.axis_index("lon") % 2, lax.axis_index("lat") % 2]).astype(jnp.int32)
-
-    smem = pl.BlockSpec(memory_space=pltpu.SMEM)
-    whole = pl.BlockSpec(memory_space=pltpu.VMEM)
-    block = 4 * LEVELS * ROWS * LANES * 4
-    raw = (u, v, t, s, water, layers, diag, elev)
-
-    own_odd, own_even = call(
-        pack_lon, (shaped(LON_ROWS, LANES),) * 2, [whole] * 8 + [smem], 10**6, 2 * block
-    )(*raw, parity)
+    parity = jnp.stack([lax.axis_index("lon") & 1, lax.axis_index("lat") & 1]).astype(jnp.int32)
+
+    raw = [
+        pltpu.with_memory_space_constraint(x, pltpu.HBM)
+        for x in (u, v, t, s, water, layers, diag, elev)
+    ]
+    masked, own_odd, own_even = call_pack_lon(*raw, parity)
+    got_even = lax.ppermute(own_even, "lon", lon_even)
     got_odd = lax.ppermute(own_odd, "lon", lon_odd)
-    got_even = lax.ppermute(own_even, "lon", lon_even)
-    lat_own_odd, lat_own_even, partial = call(
-        pack_lat,
-        (shaped(LAT_ROWS, LANES), shaped(LAT_ROWS, LANES), shaped(ROWS, LANES)),
-        [whole] * 8 + [smem], 4 * 10**6, block,
-    )(*raw, parity)
+    lat_own_odd, lat_own_even, partial = call_pack_lat(masked, own_odd, parity)
     lat_got_odd = lax.ppermute(lat_own_odd, "lat", lat_odd)
     lat_got_even = lax.ppermute(lat_own_even, "lat", lat_even)
 
-    own2d, odd2d, even2d = (x[4 * STRIP :] for x in (own_odd, got_odd, got_even))
-    b_odd, b_even = call(
-        forcing, (shaped(SOLVE_ROWS, LANES),) * 2,
-        [smem, part(STRIP), part(STRIP), part(2 * STRIP, 1), part(2 * STRIP, 1)] + [whole] * 6,
-        10**6, 10**6, grid=(1,),
-    )(
-        parity, own_odd, own_even, got_odd, got_even, own2d,
+    b_odd, b_even = call_forcing(
+        parity, got_even, got_odd, own_odd, own_even,
         lat_own_odd, lat_own_even, lat_got_odd, lat_got_even, partial,
     )
     b_got_odd = lax.ppermute(b_odd, "lon", lon_odd)
     b_got_even = lax.ppermute(b_even, "lon", lon_even)
 
-    fresh = call(
-        fields, (shaped(LEVELS, ROWS, LANES),) * 4, [smem] + [whole] * 10, 10**7, 3 * block
-    )(parity, u, v, t, s, water, layers, got_odd, got_even, lat_got_odd, lat_got_even)
-
-    height = call(solve, shaped(ROWS, LANES), [smem] + [whole] * 8, 10**6, 10**6)(
-        parity, own2d, odd2d, even2d, lat_got_odd, lat_got_even, b_odd, b_got_odd, b_got_even
+    fresh = call_fields(parity, masked, own_odd, got_odd, got_even, lat_got_odd, lat_got_even)
+    height = call_solve(
+        parity, b_got_odd, b_got_even, b_odd, own_odd, got_odd, got_even, lat_got_odd, lat_got_even
     )
     return (*fresh, height)
 

time: 63.7 us -> 50.7 us (0.80)
  the two profiles are of different devices: /device:TPU:4 before, /device:TPU:1 now
where the time goes in v2:
time: 50.7 us; the launch traced here: 50.4 us
  starting transfers between devices  36.8 us (73%)
  Pallas kernels  11.6 us (23%)
  waiting for transfers between devices  1.24 us (2%)
  between operations  0.72 us (1%)
    ppermute x1, starting transfers between devices, on_device(): got_odd = lax.ppermute(own_odd, 'lon', lon_odd)  22.5 us
    ppermute x1, starting transfers between devices, on_device(): lat_got_odd = lax.ppermute(lat_own_odd, 'lat', lat_odd)  4.88 us
    pallas_call x1, Pallas kernels, call_fields(): call(fields, (shaped(LEVELS, ROWS, LANES),) * 4, [SMEM] + [WHOLE] * 6, 10...  4.34 us
    ppermute x1, starting transfers between devices, on_device(): b_got_even = lax.ppermute(b_even, 'lon', lon_even)  3.64 us
    pallas_call x1, Pallas kernels, call_solve(): call(solve, shaped(ROWS, LANES), [SMEM] + [WHOLE] * 8, 10 ** 6, 10 ** 6)  2.31 us
    pallas_call x1, Pallas kernels, call_pack_lon(): call(pack_lon, (shaped(4, LEVELS + 4, ROWS, LANES), shaped(LON_ROWS, LANE...  2.09 us
    ppermute x1, starting transfers between devices, on_device(): lat_got_even = lax.ppermute(lat_own_even, 'lat', lat_even)  1.92 us
    ppermute x1, starting transfers between devices, on_device(): got_even = lax.ppermute(own_even, 'lon', lon_even)  1.92 us
  transfers between devices with their start and end apart: 6, of which 1 were waited for; matrix products, arithmetic and copies ran while one was open for 0% of the time, Pallas kernels for 12%

profile of v2, /device:TPU:1, one launch (start us, length us, event | category | flops | bytes accessed | tf_op | source)
XLA Modules:
  0.0 50.4 jit_solution(10469479886179576744)
XLA Ops:
  0.6 0.1 pad_add_fusion.parity
  0.7 2.1 %shard_map.119 = (f32[4,66,8,128]{3,2,1,0:T(8,128)S(1)}, f32[536,128]{1,0:T(8,128)S(1)}, f32[536,128]{1,0:T(8,128)S(1)}) custom-call(f32[62,8,128]{2,1,0:T(8,128)} %u.1, f32[62,8,128]{2,1,0:T(8,128)} %v.1, f32[62,8,128]{2,1,0:T(8,128)} %t.1, f32[62,8,128]{2,1,0:T(8,128)} %s.1, s32[8,128]{1,0:T(8,128)} %water.1, s32[8,128]{1,0:T(8,128)} %layers.1, ...), custom_call_target="tpu_custom_call" | custom-call | flops 1000000 | bytes 2031616 | tf_op jit(solution)/shard_map/pallas_call | solution.py:489
  2.8 22.5 %collective-permute-start = (f32[536,128]{1,0:T(8,128)S(1)}, f32[536,128]{1,0:T(8,128)S(1)}, u32[]{:S(2)}, u32[]{:S(2)}) collective-permute-start(f32[536,128]{1,0:T(8,128)S(1)} %get-tuple-element.18.own_lon.own_odd), channel_id=1, source_target_pairs={{0,1016},{8,16},{16,8},{24,32},{32,24},{40,48},{48,40},{56,64},{64... | collective-permute-start | bytes 823304 | tf_op jit(solution)/shard_map/ppermute | solution.py:546
  25.3 1.9 %collective-permute-start.1 = (f32[536,128]{1,0:T(8,128)S(1)}, f32[536,128]{1,0:T(8,128)S(1)}, u32[]{:S(2)}, u32[]{:S(2)}) collective-permute-start(f32[536,128]{1,0:T(8,128)S(1)} %get-tuple-element.19.own_even), channel_id=1, source_target_pairs={{0,8},{8,0},{16,24},{24,16},{32,40},{40,32},{48,56},{56,48},{64,72... | collective-permute-start | bytes 823304 | tf_op jit(solution)/shard_map/ppermute | solution.py:545
  27.2 1.7 %shard_map.120 = (f32[136,128]{1,0:T(8,128)S(1)}, f32[136,128]{1,0:T(8,128)S(1)}, f32[8,128]{1,0:T(8,128)S(1)}) custom-call(f32[4,66,8,128]{3,2,1,0:T(8,128)S(1)} %get-tuple-element.17.masked, f32[536,128]{1,0:T(8,128)S(1)} %get-tuple-element.18.own_lon.own_odd, s32[2]{0:T(128)S(1)} %pad_add_fusion.parity), custom_call_target="tpu_custom_call" | custom-call | flops 4000000 | bytes 1015808 | tf_op jit(solution)/shard_map/pallas_call | solution.py:504
  28.9 4.9 %collective-permute-start.2 = (f32[136,128]{1,0:T(8,128)S(1)}, f32[136,128]{1,0:T(8,128)S(1)}, u32[]{:S(2)}, u32[]{:S(2)}) collective-permute-start(f32[136,128]{1,0:T(8,128)S(1)} %get-tuple-element.20.own_odd_lat), channel_id=1, source_target_pairs={{1,2},{2,1},{3,4},{4,3},{5,6},{6,5},{9,10},{10,9},{11,12},{12,11},... | collective-permute-start | bytes 208904 | tf_op jit(solution)/shard_map/ppermute | solution.py:548
  33.8 1.9 %collective-permute-start.3 = (f32[136,128]{1,0:T(8,128)S(1)}, f32[136,128]{1,0:T(8,128)S(1)}, u32[]{:S(2)}, u32[]{:S(2)}) collective-permute-start(f32[136,128]{1,0:T(8,128)S(1)} %get-tuple-element.21.own_even_lat), channel_id=1, source_target_pairs={{0,1},{1,0},{2,3},{3,2},{4,5},{5,4},{6,7},{7,6},{8,9},{9,8},{10,11... | collective-permute-start | bytes 208904 | tf_op jit(solution)/shard_map/ppermute | solution.py:549
  35.7 0.1 collective-permute-done.2.odd_lat.got_odd_lat
  35.8 1.2 %collective-permute-done.3.even_lat.got_even_lat = f32[136,128]{1,0:T(8,128)S(1)} collective-permute-done((f32[136,128]{1,0:T(8,128)S(1)}, f32[136,128]{1,0:T(8,128)S(1)}, u32[]{:S(2)}, u32[]{:S(2)}) %collective-permute-start.3) | collective-permute-done | bytes 69664 | tf_op jit(solution)/shard_map/ppermute | solution.py:549
  36.9 0.0 collective-permute-done.odd_lon.got_odd
  36.9 0.0 collective-permute-done.1.even_lon.got_even
  37.0 1.2 %shard_map.122 = (f32[80,128]{1,0:T(8,128)S(1)}, f32[80,128]{1,0:T(8,128)S(1)}) custom-call(s32[2]{0:T(128)S(1)} %pad_add_fusion.parity, f32[536,128]{1,0:T(8,128)S(1)} %collective-permute-done.1.even_lon.got_even, f32[536,128]{1,0:T(8,128)S(1)} %collective-permute-done.odd_lon.got_odd, f32[536,128]{1,0:T(8,128)S(1)} %get-tuple-element.18.own_lon.own_odd, ...), custom_call_target="tpu_custom_call" | custom-call | flops 1000000 | bytes 1000000 | tf_op jit(solution)/shard_map/pallas_call | solution.py:511
  38.1 1.9 %collective-permute-start.4 = (f32[80,128]{1,0:T(8,128)S(1)}, f32[80,128]{1,0:T(8,128)S(1)}, u32[]{:S(2)}, u32[]{:S(2)}) collective-permute-start(f32[80,128]{1,0:T(8,128)S(1)} %get-tuple-element.27.own_b), channel_id=1, source_target_pairs={{0,1016},{8,16},{16,8},{24,32},{32,24},{40,48},{48,40},{56,64},{64... | collective-permute-start | bytes 122888 | tf_op jit(solution)/shard_map/ppermute | solution.py:555
  40.1 3.6 %collective-permute-start.5 = (f32[80,128]{1,0:T(8,128)S(1)}, f32[80,128]{1,0:T(8,128)S(1)}, u32[]{:S(2)}, u32[]{:S(2)}) collective-permute-start(f32[80,128]{1,0:T(8,128)S(1)} %get-tuple-element.28), channel_id=1, source_target_pairs={{0,8},{8,0},{16,24},{24,16},{32,40},{40,32},{48,56},{56,48},{64,72... | collective-permute-start | bytes 122888 | tf_op jit(solution)/shard_map/ppermute | solution.py:556
  43.7 4.3 %shard_map.121 = (f32[62,8,128]{2,1,0:T(8,128)}, f32[62,8,128]{2,1,0:T(8,128)}, f32[62,8,128]{2,1,0:T(8,128)}, f32[62,8,128]{2,1,0:T(8,128)}) custom-call(s32[2]{0:T(128)S(1)} %pad_add_fusion.parity, f32[4,66,8,128]{3,2,1,0:T(8,128)S(1)} %get-tuple-element.17.masked, f32[536,128]{1,0:T(8,128)S(1)} %get-tuple-element.18.own_lon.own_odd, ...), custom_call_target="tpu_custom_call" | custom-call | flops 10000000 | bytes 3047424 | tf_op jit(solution)/shard_map/pallas_call | solution.py:517
  48.1 0.0 collective-permute-done.4.odd_b
  48.1 0.0 collective-permute-done.5.even_b
  48.1 2.3 %shard_map.123 = f32[8,128]{1,0:T(8,128)} custom-call(s32[2]{0:T(128)S(1)} %pad_add_fusion.parity, f32[80,128]{1,0:T(8,128)S(1)} %collective-permute-done.4.odd_b, f32[80,128]{1,0:T(8,128)S(1)} %collective-permute-done.5.even_b, f32[80,128]{1,0:T(8,128)S(1)} %get-tuple-element.27.own_b, f32[536,128]{1,0:T(8,128)S(1)} %get-tuple-element.18.own_lon.own_odd, ...), custom_call_target="tpu_custom_call" | custom-call | flops 1000000 | bytes 1000000 | tf_op jit(solution)/shard_map/pallas_call | solution.py:529
Async XLA Ops:
  2.8 34.1 %collective-permute-start = (f32[536,128]{1,0:T(8,128)S(1)}, f32[536,128]{1,0:T(8,128)S(1)}, u32[]{:S(2)}, u32[]{:S(2)}) collective-permute-start(f32[536,128]{1,0:T(8,128)S(1)} %get-tuple-element.18.own_lon.own_odd), channel_id=1, source_target_pairs={{0,1016},{8,16},{16,8},{24,32},{32,24},{40,48},{48,40},{56,64},{64... | collective-permute-start | bytes 823304 | tf_op jit(solution)/shard_map/ppermute | solution.py:546
  25.3 11.6 %collective-permute-start.1 = (f32[536,128]{1,0:T(8,128)S(1)}, f32[536,128]{1,0:T(8,128)S(1)}, u32[]{:S(2)}, u32[]{:S(2)}) collective-permute-start(f32[536,128]{1,0:T(8,128)S(1)} %get-tuple-element.19.own_even), channel_id=1, source_target_pairs={{0,8},{8,0},{16,24},{24,16},{32,40},{40,32},{48,56},{56,48},{64,72... | collective-permute-start | bytes 823304 | tf_op jit(solution)/shard_map/ppermute | solution.py:545
  28.9 6.9 %collective-permute-start.2 = (f32[136,128]{1,0:T(8,128)S(1)}, f32[136,128]{1,0:T(8,128)S(1)}, u32[]{:S(2)}, u32[]{:S(2)}) collective-permute-start(f32[136,128]{1,0:T(8,128)S(1)} %get-tuple-element.20.own_odd_lat), channel_id=1, source_target_pairs={{1,2},{2,1},{3,4},{4,3},{5,6},{6,5},{9,10},{10,9},{11,12},{12,11},... | collective-permute-start | bytes 208904 | tf_op jit(solution)/shard_map/ppermute | solution.py:548
  33.8 3.2 %collective-permute-start.3 = (f32[136,128]{1,0:T(8,128)S(1)}, f32[136,128]{1,0:T(8,128)S(1)}, u32[]{:S(2)}, u32[]{:S(2)}) collective-permute-start(f32[136,128]{1,0:T(8,128)S(1)} %get-tuple-element.21.own_even_lat), channel_id=1, source_target_pairs={{0,1},{1,0},{2,3},{3,2},{4,5},{5,4},{6,7},{7,6},{8,9},{9,8},{10,11... | collective-permute-start | bytes 208904 | tf_op jit(solution)/shard_map/ppermute | solution.py:549
  38.1 9.9 %collective-permute-start.4 = (f32[80,128]{1,0:T(8,128)S(1)}, f32[80,128]{1,0:T(8,128)S(1)}, u32[]{:S(2)}, u32[]{:S(2)}) collective-permute-start(f32[80,128]{1,0:T(8,128)S(1)} %get-tuple-element.27.own_b), channel_id=1, source_target_pairs={{0,1016},{8,16},{16,8},{24,32},{32,24},{40,48},{48,40},{56,64},{64... | collective-permute-start | bytes 122888 | tf_op jit(solution)/shard_map/ppermute | solution.py:555
  40.1 8.0 %collective-permute-start.5 = (f32[80,128]{1,0:T(8,128)S(1)}, f32[80,128]{1,0:T(8,128)S(1)}, u32[]{:S(2)}, u32[]{:S(2)}) collective-permute-start(f32[80,128]{1,0:T(8,128)S(1)} %get-tuple-element.28), channel_id=1, source_target_pairs={{0,8},{8,0},{16,24},{24,16},{32,40},{40,32},{48,56},{56,48},{64,72... | collective-permute-start | bytes 122888 | tf_op jit(solution)/shard_map/ppermute | solution.py:556

commit v3 on v2

--- a/solution.py
+++ b/solution.py
@@ -15,8 +15,8 @@
 STRIP = 128
 FLAT = 4 * STRIP
 LON_ROWS = FLAT + 3 * ROWS
-LAT_ROWS = 17 * ROWS
-SOLVE_ROWS = 5 * ROWS + 32 + 8
+LAT_ROWS = 18 * ROWS
+SOLVE_ROWS = 5 * ROWS + 5 * ROWS
 VMEM = 12 * 1024 * 1024
 
 F32 = jnp.float32
@@ -49,75 +49,57 @@
     return lax.axis_index(axis) % 2 == 0
 
 
-def pack_lon(
-    u, v, t, s, water, layers, diag, elev, parity, masked, up_first, low_first, held, held_int, held_flat, sems
+def flat_of(ref, base=FLAT):
+    return [ref[base + 8 * i : base + 8 * i + 8, :] for i in range(3)]
+
+
+def prepare(
+    u, v, t, s, water, layers, diag, elev, parity,
+    masked, odd_out, even_out, partial, flat, held, held_int, sems,
 ):
-    copies = [
-        pltpu.make_async_copy(src, held.at[i], sems.at[i]) for i, src in enumerate((u, v, t, s))
+    small = [
+        pltpu.make_async_copy(water, held_int.at[0], sems.at[0]),
+        pltpu.make_async_copy(layers, held_int.at[1], sems.at[1]),
+        pltpu.make_async_copy(elev, flat.at[0:8], sems.at[2]),
+        pltpu.make_async_copy(diag, flat.at[8:16], sems.at[3]),
     ]
-    small = [
-        pltpu.make_async_copy(water, held_int.at[0], sems.at[4]),
-        pltpu.make_async_copy(layers, held_int.at[1], sems.at[5]),
-        pltpu.make_async_copy(elev, held_flat.at[0], sems.at[6]),
-        pltpu.make_async_copy(diag, held_flat.at[1], sems.at[7]),
-    ]
-    for copy in small + copies:
+    chunks = []
+    for a in range(4):
+        at = slice(16 * a, min(16 * a + 16, LEVELS))
+        chunks.append(
+            [
+                pltpu.make_async_copy(src.at[at], held.at[f, at], sems.at[4 + 4 * a + f])
+                for f, src in enumerate((u, v, t, s))
+            ]
+        )
+    for copy in small[:2] + [x for chunk in chunks for x in chunk] + small[2:]:
         copy.start()
-    for copy in small:
+    for copy in small[:2]:
         copy.wait()
-    row = rows_of()
-    group = row >> 1
+    row, lane = rows_of(), lanes_of()
+    high, low = lane >> 4, ((lane - 8) & 127) >> 4
+    in_even = (lane & 8) == 0
     depth = held_int[0] * held_int[1]
-    is_even = parity[0] == 0
-    for ref in (up_first, low_first):
-        ref[FLAT : FLAT + 8, :] = held_flat[0]
-        ref[FLAT + 8 : FLAT + 16, :] = held_flat[1]
-        ref[FLAT + 16 : FLAT + 24, :] = depth.astype(F32)
-
+    flat[16:24, :] = depth.astype(F32)
+    is_even = parity[1] == 0
+    zero = jnp.zeros((ROWS, LANES), F32)
     for f in range(4):
-        masked[f, 0] = jnp.zeros((ROWS, LANES), F32)
-        masked[f, LEVELS + 3] = jnp.zeros((ROWS, LANES), F32)
-        copies[f].wait()
-
-        def body(g, carry, f=f):
-            top = bottom = None
-            for i in range(4):
-                k = 4 * g + i
-                m = jnp.where(k < depth, held[f, jnp.minimum(k, LEVELS - 1)], 0.0)
-                masked[f, k + 1] = m
-                a, b = by_rows(m, 2 * i), by_rows(m, 2 * i - 6)
-                top = a if i == 0 else jnp.where(group == i, a, top)
-                bottom = b if i == 0 else jnp.where(group == i, b, bottom)
-            at = pl.ds(pl.multiple_of(f * STRIP + 8 * g, 8), 8)
-            up_first[at, :] = jnp.where(is_even, top, bottom)
-            low_first[at, :] = jnp.where(is_even, bottom, top)
-            return carry
-
-        lax.fori_loop(0, 16, body, 0, unroll=4)
-
-
-def flat_of(ref):
-    return [ref[FLAT + 8 * i : FLAT + 8 * i + 8, :] for i in range(3)]
-
-
-def pack_lat(masked, own_lon, parity, odd_out, even_out, partial):
-    row, lane = rows_of(), lanes_of()
-    slot = lane >> 3
-    elev, diag, depth = flat_of(own_lon)
-    levels = depth.astype(jnp.int32)
-    is_even = parity[1] == 0
-
-    def body(a, acc):
-        left = [None] * 4
-        right = [None] * 4
-        for i in range(16):
+        for i in (0, LEVELS + 1, LEVELS + 2):
+            masked[f, i] = zero
+
+    def tile(a, sums, count=16):
+        whole, inner, sides, flux = sums
+        first, second = [zero] * 4, [zero] * 4
+        for i in range(count):
             k = 16 * a + i
-            wet = k < levels
-            m = [masked[f, k + 1] for f in range(4)]
+            wet = k < depth
+            m = [jnp.where(wet, held[f, k], 0.0) for f in range(4)]
             for f in range(4):
-                x, y = by_lanes(m[f], 8 * i), by_lanes(m[f], 8 * i - 120)
-                left[f] = x if i == 0 else jnp.where(slot == i, x, left[f])
-                right[f] = y if i == 0 else jnp.where(slot == i, y, right[f])
+                masked[f, k + 1] = m[f]
+                if i < 8:
+                    first[f] = jnp.where(high == i, by_lanes(m[f], 16 * i - 120), first[f])
+                else:
+                    second[f] = jnp.where(low == i - 8, by_lanes(m[f], 16 * i - 240), second[f])
             w = scalar_mix(m[2], m[3])
             n1 = jnp.where(row < 7, by_rows(w, -1), 0.0)
             p1 = jnp.where(row > 0, by_rows(w, 1), 0.0)
@@ -129,27 +111,66 @@
             q2 = jnp.where(lane > 1, by_lanes(w, 2), 0.0)
             gx = 8.0 * (n1 - p1) - (n2 - p2)
             gy = 8.0 * (e1 - q1) - (e2 - q2)
-            around = jnp.where(wet, (n1 + p1) + (e1 + q1), 0.0)
-            column = jnp.where(k > 0, w, 0.0) + jnp.where(k + 1 < levels, w, 0.0)
-            acc = acc + (
-                0.94 * w + 0.02 * column + 0.005 * around - ADV * (m[0] * gx + m[1] * gy)
-            )
+            whole = whole + w
+            inner = inner + jnp.where(k + 1 < depth, w, 0.0)
+            sides = sides + jnp.where(wet, (n1 + p1) + (e1 + q1), 0.0)
+            flux = flux + (m[0] * gx + m[1] * gy)
         for f in range(4):
+            right = jnp.where(in_even, first[f], second[f])
+            left = by_lanes(jnp.where(in_even, second[f], first[f]), -8)
             where = pl.ds(pl.multiple_of(f * 32 + 8 * a, 8), 8)
-            odd_out[where, :] = jnp.where(is_even, left[f], right[f])
-            even_out[where, :] = jnp.where(is_even, right[f], left[f])
-        return acc
-
-    acc = 0.1 * lax.fori_loop(0, 4, body, jnp.zeros((ROWS, LANES), F32))
+            odd_out[where, :] = jnp.where(is_even, left, right)
+            even_out[where, :] = jnp.where(is_even, right, left)
+        return whole, inner, sides, flux
+
+    def body(a, sums):
+        for f, src in enumerate((u, v, t, s)):
+            at = pl.ds(16 * a, 16)
+            pltpu.make_async_copy(src.at[at], held.at[f, at], sems.at[4 + 4 * a + f]).wait()
+        return tile(a, sums)
+
+    sums = lax.fori_loop(0, 3, body, (zero,) * 4)
+    for copy in chunks[3]:
+        copy.wait()
+    whole, inner, sides, flux = tile(3, sums, LEVELS - 48)
+    top = scalar_mix(masked[2, 1], masked[3, 1])
+    acc = 0.1 * (0.94 * whole + 0.02 * (whole - top + inner) + 0.005 * sides - ADV * flux)
     partial[...] = acc
-    flat = (acc, elev, diag, depth)
-    left = right = None
-    for i, x in enumerate(flat):
-        a, b = by_lanes(x, 8 * i), by_lanes(x, 8 * i - 120)
-        left = a if i == 0 else jnp.where(slot == i, a, left)
-        right = b if i == 0 else jnp.where(slot == i, b, right)
+    for copy in small[2:]:
+        copy.wait()
+    slot = lane >> 3
+    depth = depth.astype(F32)
+    left = right = zero
+    for i, x in enumerate((acc, flat[0:8, :], flat[8:16, :], depth)):
+        left = jnp.where(slot == i, by_lanes(x, 8 * i), left)
+        right = jnp.where(slot == i, by_lanes(x, 8 * i - 120), right)
     odd_out[128:136, :] = jnp.where(is_even, left, right)
     even_out[128:136, :] = jnp.where(is_even, right, left)
+    left, right = tile_lanes(depth), tile_lanes(by_lanes(depth, 8))
+    odd_out[136:144, :] = jnp.where(is_even, left, right)
+    even_out[136:144, :] = jnp.where(is_even, right, left)
+
+
+def pack_lon(masked, flat, after, parity, odd_out, even_out):
+    group = rows_of() >> 1
+    is_even = parity[0] == 0
+    for ref in (odd_out, even_out):
+        ref[FLAT : FLAT + 24, :] = flat[...]
+
+    def body(g, carry):
+        for f in range(4):
+            top = bottom = None
+            for i in range(4):
+                m = masked[f, 4 * g + i + 1]
+                a, b = by_rows(m, 2 * i), by_rows(m, 2 * i - 6)
+                top = a if i == 0 else jnp.where(group == i, a, top)
+                bottom = b if i == 0 else jnp.where(group == i, b, bottom)
+            at = pl.ds(pl.multiple_of(f * STRIP + 8 * g, 8), 8)
+            odd_out[at, :] = jnp.where(is_even, top, bottom)
+            even_out[at, :] = jnp.where(is_even, bottom, top)
+        return carry
+
+    lax.fori_loop(0, 16, body, 0, unroll=2)
 
 
 def tile_lanes(x):
@@ -166,7 +187,8 @@
 
 
 def wet_pack(depth, a):
-    return (16 * a + (lanes_of() >> 3)).astype(F32) < depth
+    slot = lanes_of() >> 3
+    return (16 * a + (slot >> 1) + 8 * (slot & 1)).astype(F32) < depth
 
 
 def lat_rims(a_v, a_w, a_depth, b_v, b_w, b_depth):
@@ -240,18 +262,20 @@
     ext_l = [four(got_odd_lat, f * 32, lat_even, got_even_lat) for f in range(4)]
     flat_r = jnp.where(lat_even, got_even_lat[128:136, :], got_odd_lat[128:136, :])
     flat_l = jnp.where(lat_even, got_odd_lat[128:136, :], got_even_lat[128:136, :])
+    depth_r = jnp.where(lat_even, got_even_lat[136:144, :], got_odd_lat[136:144, :])
+    depth_l = jnp.where(lat_even, got_odd_lat[136:144, :], got_even_lat[136:144, :])
+    own_depth_r = jnp.where(lat_even, own_even_lat[136:144, :], own_odd_lat[136:144, :])
+    own_depth_l = jnp.where(lat_even, own_odd_lat[136:144, :], own_even_lat[136:144, :])
 
     def mixed(pair):
         return [scalar_mix(x, y) for x, y in zip(*pair, strict=True)]
 
     w_r, w_l = mixed(ext_r[2:]), mixed(ext_l[2:])
     miss_own_r, miss_ext_r = lat_rims(
-        own_r[0], mixed(own_r[1:]), tile_lanes(by_lanes(depth, 8)),
-        ext_r[1], w_r, tile_lanes(by_lanes(flat_r, -24)),
+        own_r[0], mixed(own_r[1:]), own_depth_r, ext_r[1], w_r, depth_r
     )
     miss_ext_l, miss_own_l = lat_rims(
-        ext_l[1], w_l, tile_lanes(by_lanes(flat_l, -24)),
-        own_l[0], mixed(own_l[1:]), tile_lanes(depth),
+        ext_l[1], w_l, depth_l, own_l[0], mixed(own_l[1:]), own_depth_l
     )
     total = total + jnp.where(lane >= 126, miss_own_r, 0.0) + jnp.where(lane < 2, miss_own_l, 0.0)
 
@@ -269,16 +293,13 @@
     for ref in (odd_out, even_out):
         for i, x in enumerate((total, total_side, elev_side, side(2), side(3))):
             ref[8 * i : 8 * i + 8, :] = x
-        ref[SOLVE_ROWS - 8 : SOLVE_ROWS, :] = jnp.zeros((8, LANES), F32)
-    packs = ext_r[0] + ext_l[0] + w_r + w_l
+    packs = ext_r[0] + ext_l[0] + w_r + w_l + [depth_r, depth_l]
     group = row >> 1
-    for i in range(4):
-        top = bottom = None
-        for j in range(4):
-            x = packs[4 * i + j]
-            a, b = by_rows(x, 2 * j), by_rows(x, 2 * j - 6)
-            top = a if j == 0 else jnp.where(group == j, a, top)
-            bottom = b if j == 0 else jnp.where(group == j, b, bottom)
+    for i in range(5):
+        top = bottom = jnp.zeros((ROWS, LANES), F32)
+        for j, x in enumerate(packs[4 * i : 4 * i + 4]):
+            top = jnp.where(group == j, by_rows(x, 2 * j), top)
+            bottom = jnp.where(group == j, by_rows(x, 2 * j - 6), bottom)
         at = slice(40 + 8 * i, 48 + 8 * i)
         odd_out[at, :] = jnp.where(lon_even, top, bottom)
         even_out[at, :] = jnp.where(lon_even, bottom, top)
@@ -295,15 +316,19 @@
     lon_even, lat_even = parity[0] == 0, parity[1] == 0
     outs = (o1, o2, o3, o4)
 
+    in_even = (lane & 8) == 0
+
     def unpack(a, carry):
         for f in range(4):
             at = pl.ds(pl.multiple_of(f * 32 + 8 * a, 8), 8)
             x, y = odd_lat[at, :], even_lat[at, :]
-            west, east = jnp.where(lat_even, x, y), jnp.where(lat_even, y, x)
-            for i in range(16):
-                rims[f, 16 * a + i] = jnp.where(
-                    lane < 64, by_lanes(east, -8 * i), by_lanes(west, 120 - 8 * i)
-                )
+            west = jnp.where(lat_even, x, y)
+            east = by_lanes(jnp.where(lat_even, y, x), 8)
+            first = jnp.where(in_even, west, east)
+            second = jnp.where(in_even, east, west)
+            for i in range(8):
+                rims[f, 16 * a + i] = by_lanes(first, -16 * i - 8)
+                rims[f, 16 * a + 8 + i] = by_lanes(second, -16 * i - 16)
         return carry
 
     lax.fori_loop(0, 4, unpack, 0)
@@ -384,6 +409,9 @@
     def rim_rows(tile, q, first):
         return by_rows(tile[5 + q // 4], first - 2 * (q % 4))
 
+    def near_rows(q):
+        return jnp.where(row < 4, rim_rows(upper, q, 0), rim_rows(lower, q, 6))
+
     def side_parts(ext, base, own_depth, near_depth):
         mine = theirs = jnp.zeros((ROWS, LANES), F32)
         for i in range(4):
@@ -394,15 +422,13 @@
             mine = mine + lon_part(vel, wet_pack(own_depth, i), x1, x2)
             y2 = jnp.where(row < 4, by_rows(w, 2), by_rows(w, -2))
             y1 = jnp.where(row < 4, by_rows(w, 1), by_rows(w, -1))
-            other = jnp.where(row < 4, rim_rows(upper, qu, 0), rim_rows(lower, qu, 6))
-            theirs = theirs + lon_part(other, wet_pack(near_depth, i), y1, y2)
+            theirs = theirs + lon_part(near_rows(qu), wet_pack(near_depth, i), y1, y2)
         return 0.1 * sum_slots(mine), 0.1 * sum_slots(theirs)
 
-    near_side = jnp.where(row < 4, upper[4], lower[4])
-    mine_r, theirs_r = side_parts(ext_r, 0, tile_lanes(own[4]), tile_lanes(near_side))
-    mine_l, theirs_l = side_parts(
-        ext_l, 4, tile_lanes(by_lanes(own[4], 8)), tile_lanes(by_lanes(near_side, 8))
-    )
+    depth_r = jnp.where(lat_even, even_lat[136:144, :], odd_lat[136:144, :])
+    depth_l = jnp.where(lat_even, odd_lat[136:144, :], even_lat[136:144, :])
+    mine_r, theirs_r = side_parts(ext_r, 0, depth_r, near_rows(16))
+    mine_l, theirs_l = side_parts(ext_l, 4, depth_l, near_rows(17))
     in_r, in_l = lane < 8, lane >= 120
     mine = jnp.where(in_r, mine_r, jnp.where(in_l, mine_l, 0.0))
     theirs = jnp.where(in_r, theirs_r, jnp.where(in_l, theirs_l, 0.0))
@@ -485,25 +511,27 @@
 BLOCK = 4 * LEVELS * ROWS * LANES * 4
 
 
-def call_pack_lon(*args):
+def call_prepare(*args):
     return call(
-        pack_lon,
-        (shaped(4, LEVELS + 4, ROWS, LANES), shaped(LON_ROWS, LANES), shaped(LON_ROWS, LANES)),
-        [HERE] * 8 + [SMEM], 10**6, 2 * BLOCK,
-        out_specs=(WHOLE,) * 3,
+        prepare,
+        (
+            shaped(4, LEVELS + 3, ROWS, LANES), shaped(LAT_ROWS, LANES), shaped(LAT_ROWS, LANES),
+            shaped(ROWS, LANES), shaped(3 * ROWS, LANES),
+        ),
+        [HERE] * 8 + [SMEM], 10**7, BLOCK,
+        out_specs=(WHOLE,) * 5,
         scratch_shapes=[
             pltpu.VMEM((4, LEVELS, ROWS, LANES), F32),
             pltpu.VMEM((2, ROWS, LANES), jnp.int32),
-            pltpu.VMEM((2, ROWS, LANES), F32),
-            pltpu.SemaphoreType.DMA((8,)),
+            pltpu.SemaphoreType.DMA((20,)),
         ],
     )(*args)
 
 
-def call_pack_lat(*args):
+def call_pack_lon(*args):
     return call(
-        pack_lat, (shaped(LAT_ROWS, LANES), shaped(LAT_ROWS, LANES), shaped(ROWS, LANES)),
-        [WHOLE] * 2 + [SMEM], 4 * 10**6, BLOCK,
+        pack_lon, (shaped(LON_ROWS, LANES),) * 2,
+        [WHOLE, WHOLE, pl.BlockSpec(memory_space=pl.ANY), SMEM], 10**6, 10**6,
     )(*args)
 
 
@@ -529,31 +557,60 @@
     return call(solve, shaped(ROWS, LANES), [SMEM] + [WHOLE] * 8, 10**6, 10**6)(*args)
 
 
+def exchanges(lon, lat):
+    def pairs(size, first, around):
+        last = size if around else size - 1
+        return [(i, (i + 1) % size) for i in range(first, last, 2)]
+
+    def over_lon(first):
+        return [
+            (x * lat + j, y * lat + j)
+            for a, b in pairs(lon, first, True)
+            for x, y in ((a, b), (b, a))
+            for j in range(lat)
+        ]
+
+    def over_lat(first, rows):
+        return [
+            (i * lat + x, i * lat + y)
+            for i in rows
+            for a, b in pairs(lat, first, False)
+            for x, y in ((a, b), (b, a))
+        ]
+
+    return over_lon, over_lat
+
+
+RUN, EARLY = 8, 4
+
+
 def on_device(u, v, t, s, water, layers, diag, elev):
     lon, lat = lax.axis_size("lon"), lax.axis_size("lat")
-    lon_even = [(i, i ^ 1) for i in range(lon)]
-    lon_odd = [(i, (((i + 1) ^ 1) - 1) % lon) for i in range(lon)]
-    lat_even = [(i, i ^ 1) for i in range(lat)]
-    lat_odd = [(i, ((i + 1) ^ 1) - 1) for i in range(1, lat - 1)]
+    over_lon, over_lat = exchanges(lon, lat)
+    early = [i for i in range(lon) if i % RUN < EARLY]
+    late = [i for i in range(lon) if i % RUN >= EARLY]
+    both = ("lon", "lat")
     parity = jnp.stack([lax.axis_index("lon") & 1, lax.axis_index("lat") & 1]).astype(jnp.int32)
 
     raw = [
         pltpu.with_memory_space_constraint(x, pltpu.HBM)
         for x in (u, v, t, s, water, layers, diag, elev)
     ]
-    masked, own_odd, own_even = call_pack_lon(*raw, parity)
-    got_even = lax.ppermute(own_even, "lon", lon_even)
-    got_odd = lax.ppermute(own_odd, "lon", lon_odd)
-    lat_own_odd, lat_own_even, partial = call_pack_lat(masked, own_odd, parity)
-    lat_got_odd = lax.ppermute(lat_own_odd, "lat", lat_odd)
-    lat_got_even = lax.ppermute(lat_own_even, "lat", lat_even)
+    masked, lat_own_odd, lat_own_even, partial, flat = call_prepare(*raw, parity)
+    lat_early = lax.ppermute(lat_own_odd, both, over_lat(1, early))
+    own_odd, own_even = call_pack_lon(masked, flat, lat_early, parity)
+    got_even = lax.ppermute(own_even, both, over_lon(0))
+    got_odd = lax.ppermute(own_odd, both, over_lon(1))
+    lat_got_even = lax.ppermute(lat_own_even, both, over_lat(0, range(lon)))
+    lat_late = lax.ppermute(lat_own_odd, both, over_lat(1, late))
+    lat_got_odd = lat_early + lat_late
 
     b_odd, b_even = call_forcing(
         parity, got_even, got_odd, own_odd, own_even,
         lat_own_odd, lat_own_even, lat_got_odd, lat_got_even, partial,
     )
-    b_got_odd = lax.ppermute(b_odd, "lon", lon_odd)
-    b_got_even = lax.ppermute(b_even, "lon", lon_even)
+    b_got_odd = lax.ppermute(b_odd, both, over_lon(1))
+    b_got_even = lax.ppermute(b_even, both, over_lon(0))
 
     fresh = call_fields(parity, masked, own_odd, got_odd, got_even, lat_got_odd, lat_got_even)
     height = call_solve(

time: 50.7 us -> 51 us (level)
  the two profiles are of different devices: /device:TPU:1 before, /device:TPU:4 now
where the time goes in v3:
time: 51 us; the launch traced here: 50.7 us
  starting transfers between devices  28.7 us (56%)
  Pallas kernels  10.9 us (21%)
  waiting for transfers between devices  10.2 us (20%)
  between operations  0.75 us (1%)
    ppermute x1, starting transfers between devices, on_device(): got_odd = lax.ppermute(own_odd, both, over_lon(1))  15.8 us
    ppermute x1, waiting for transfers between devices, on_device(): lat_early = lax.ppermute(lat_own_odd, both, over_lat(1, early))  4.87 us
    ppermute x1, starting transfers between devices, on_device(): b_got_odd = lax.ppermute(b_odd, both, over_lon(1))  4.5 us
    pallas_call x1, Pallas kernels, call_fields(): call(fields, (shaped(LEVELS, ROWS, LANES),) * 4, [SMEM] + [WHOLE] * 6, 10...  4.35 us
    ppermute x1, waiting for transfers between devices, on_device(): got_even = lax.ppermute(own_even, both, over_lon(0))  3.37 us
    pallas_call x1, Pallas kernels, call_prepare(): call(prepare, (shaped(4, LEVELS + 3, ROWS, LANES), shaped(LAT_ROWS, LANES...  2.97 us
    pallas_call x1, Pallas kernels, call_solve(): call(solve, shaped(ROWS, LANES), [SMEM] + [WHOLE] * 8, 10 ** 6, 10 ** 6)  2.01 us
    ppermute x1, starting transfers between devices, on_device(): lat_early = lax.ppermute(lat_own_odd, both, over_lat(1, early))  1.92 us
  transfers between devices with their start and end apart: 7, of which 4 were waited for; matrix products, arithmetic and copies ran while one was open for 0% of the time, Pallas kernels for 9%

profile of v3, /device:TPU:4, one launch (start us, length us, event | category | flops | bytes accessed | tf_op | source)
XLA Modules:
  0.0 50.7 jit_solution(655965308003828331)
XLA Ops:
  0.6 0.1 pad_add_fusion.parity
  0.7 3.0 %shard_map.119 = (f32[4,65,8,128]{3,2,1,0:T(8,128)S(1)}, f32[144,128]{1,0:T(8,128)S(1)}, f32[144,128]{1,0:T(8,128)S(1)}, f32[8,128]{1,0:T(8,128)S(1)}, f32[24,128]{1,0:T(8,128)S(1)}) custom-call(f32[62,8,128]{2,1,0:T(8,128)} %u.1, f32[62,8,128]{2,1,0:T(8,128)} %v.1, f32[62,8,128]{2,1,0:T(8,128)} %t.1, f32[62,8,128]{2,1,0:T(8,128)} %s.1, s32[8,128]{1,0:T(8,128)} %water.1, ...), custom_call_target="tpu_custom_call" | custom-call | flops 10000000 | bytes 1015808 | tf_op jit(solution)/shard_map/pallas_call | solution.py:515
  3.7 1.9 %collective-permute-start = (f32[144,128]{1,0:T(8,128)S(1)}, f32[144,128]{1,0:T(8,128)S(1)}, u32[]{:S(2)}, u32[]{:S(2)}) collective-permute-start(f32[144,128]{1,0:T(8,128)S(1)} %get-tuple-element.20.own_odd_lat), channel_id=1, source_target_pairs={{1,2},{2,1},{3,4},{4,3},{5,6},{6,5},{9,10},{10,9},{11,12},{12,11},... | collective-permute-start | bytes 221192 | tf_op jit(solution)/shard_map/ppermute | solution.py:600
  5.6 4.9 %collective-permute-done.after = f32[144,128]{1,0:T(8,128)S(1)} collective-permute-done((f32[144,128]{1,0:T(8,128)S(1)}, f32[144,128]{1,0:T(8,128)S(1)}, u32[]{:S(2)}, u32[]{:S(2)}) %collective-permute-start) | collective-permute-done | bytes 73760 | tf_op jit(solution)/shard_map/ppermute | solution.py:600
  10.5 0.7 %shard_map.120 = (f32[536,128]{1,0:T(8,128)S(1)}, f32[536,128]{1,0:T(8,128)S(1)}) custom-call(f32[4,65,8,128]{3,2,1,0:T(8,128)S(1)} %get-tuple-element.18.masked, f32[24,128]{1,0:T(8,128)S(1)} %get-tuple-element.19.flat, f32[144,128]{1,0:T(8,128)S(1)} %collective-permute-done.after, s32[2]{0:T(128)S(1)} %pad_add_fusion.parity), custom_call_target="tpu_custom_call" | custom-call | flops 1000000 | bytes 1000000 | tf_op jit(solution)/shard_map/pallas_call | solution.py:532
  11.2 15.8 %collective-permute-start.1 = (f32[536,128]{1,0:T(8,128)S(1)}, f32[536,128]{1,0:T(8,128)S(1)}, u32[]{:S(2)}, u32[]{:S(2)}) collective-permute-start(f32[536,128]{1,0:T(8,128)S(1)} %get-tuple-element.21.own_lon.own_odd), channel_id=1, source_target_pairs={{8,16},{9,17},{10,18},{11,19},{12,20},{13,21},{14,22},{15,23},{16,... | collective-permute-start | bytes 823304 | tf_op jit(solution)/shard_map/ppermute | solution.py:603
  27.0 1.9 %collective-permute-start.2 = (f32[536,128]{1,0:T(8,128)S(1)}, f32[536,128]{1,0:T(8,128)S(1)}, u32[]{:S(2)}, u32[]{:S(2)}) collective-permute-start(f32[536,128]{1,0:T(8,128)S(1)} %get-tuple-element.22.own_even), channel_id=1, source_target_pairs={{0,8},{1,9},{2,10},{3,11},{4,12},{5,13},{6,14},{7,15},{8,0},{9,1},... | collective-permute-start | bytes 823304 | tf_op jit(solution)/shard_map/ppermute | solution.py:602
  28.9 0.7 %collective-permute-start.3 = (f32[144,128]{1,0:T(8,128)S(1)}, f32[144,128]{1,0:T(8,128)S(1)}, u32[]{:S(2)}, u32[]{:S(2)}) collective-permute-start(f32[144,128]{1,0:T(8,128)S(1)} %get-tuple-element.20.own_odd_lat), channel_id=1, source_target_pairs={{33,34},{34,33},{35,36},{36,35},{37,38},{38,37},{41,42},{42,41},{4... | collective-permute-start | bytes 221192 | tf_op jit(solution)/shard_map/ppermute | solution.py:605
  29.6 1.9 %collective-permute-start.4 = (f32[144,128]{1,0:T(8,128)S(1)}, f32[144,128]{1,0:T(8,128)S(1)}, u32[]{:S(2)}, u32[]{:S(2)}) collective-permute-start(f32[144,128]{1,0:T(8,128)S(1)} %get-tuple-element.23.own_even_lat), channel_id=1, source_target_pairs={{0,1},{1,0},{2,3},{3,2},{4,5},{5,4},{6,7},{7,6},{8,9},{9,8},{10,11... | collective-permute-start | bytes 221192 | tf_op jit(solution)/shard_map/ppermute | solution.py:604
  31.5 0.0 collective-permute-done.3
  31.6 1.2 %collective-permute-done.4.even_lat.got_even_lat = f32[144,128]{1,0:T(8,128)S(1)} collective-permute-done((f32[144,128]{1,0:T(8,128)S(1)}, f32[144,128]{1,0:T(8,128)S(1)}, u32[]{:S(2)}, u32[]{:S(2)}) %collective-permute-start.4) | collective-permute-done | bytes 73760 | tf_op jit(solution)/shard_map/ppermute | solution.py:604
  32.8 0.8 %collective-permute-done.1.odd_lon.got_odd = f32[536,128]{1,0:T(8,128)S(1)} collective-permute-done((f32[536,128]{1,0:T(8,128)S(1)}, f32[536,128]{1,0:T(8,128)S(1)}, u32[]{:S(2)}, u32[]{:S(2)}) %collective-permute-start.1) | collective-permute-done | bytes 274464 | tf_op jit(solution)/shard_map/ppermute | solution.py:603
  33.6 3.4 %collective-permute-done.2.even_lon.got_even = f32[536,128]{1,0:T(8,128)S(1)} collective-permute-done((f32[536,128]{1,0:T(8,128)S(1)}, f32[536,128]{1,0:T(8,128)S(1)}, u32[]{:S(2)}, u32[]{:S(2)}) %collective-permute-start.2) | collective-permute-done | bytes 274464 | tf_op jit(solution)/shard_map/ppermute | solution.py:602
  36.9 0.9 %shard_map.122 = (f32[80,128]{1,0:T(8,128)S(1)}, f32[80,128]{1,0:T(8,128)S(1)}) custom-call(s32[2]{0:T(128)S(1)} %pad_add_fusion.parity, f32[536,128]{1,0:T(8,128)S(1)} %collective-permute-done.2.even_lon.got_even, f32[536,128]{1,0:T(8,128)S(1)} %collective-permute-done.1.odd_lon.got_odd, f32[536,128]{1,0:T(8,128)S(1)} %get-tuple-element.21.own_lon.own_odd, ...), custom_call_target="tpu_custom_call" | custom-call | flops 1000000 | bytes 1000000 | tf_op jit(solution)/shard_map/pallas_call | solution.py:539
  37.9 4.5 %collective-permute-start.5 = (f32[80,128]{1,0:T(8,128)S(1)}, f32[80,128]{1,0:T(8,128)S(1)}, u32[]{:S(2)}, u32[]{:S(2)}) collective-permute-start(f32[80,128]{1,0:T(8,128)S(1)} %get-tuple-element.29.own_b), channel_id=1, source_target_pairs={{8,16},{9,17},{10,18},{11,19},{12,20},{13,21},{14,22},{15,23},{16,... | collective-permute-start | bytes 122888 | tf_op jit(solution)/shard_map/ppermute | solution.py:612
  42.4 1.9 %collective-permute-start.6 = (f32[80,128]{1,0:T(8,128)S(1)}, f32[80,128]{1,0:T(8,128)S(1)}, u32[]{:S(2)}, u32[]{:S(2)}) collective-permute-start(f32[80,128]{1,0:T(8,128)S(1)} %get-tuple-element.30), channel_id=1, source_target_pairs={{0,8},{1,9},{2,10},{3,11},{4,12},{5,13},{6,14},{7,15},{8,0},{9,1},... | collective-permute-start | bytes 122888 | tf_op jit(solution)/shard_map/ppermute | solution.py:613
  44.3 4.3 %shard_map.121 = (f32[62,8,128]{2,1,0:T(8,128)}, f32[62,8,128]{2,1,0:T(8,128)}, f32[62,8,128]{2,1,0:T(8,128)}, f32[62,8,128]{2,1,0:T(8,128)}) custom-call(s32[2]{0:T(128)S(1)} %pad_add_fusion.parity, f32[4,65,8,128]{3,2,1,0:T(8,128)S(1)} %get-tuple-element.18.masked, f32[536,128]{1,0:T(8,128)S(1)} %get-tuple-element.21.own_lon.own_odd, ...), custom_call_target="tpu_custom_call" | custom-call | flops 10000000 | bytes 3047424 | tf_op jit(solution)/shard_map/pallas_call | solution.py:545
  48.7 0.0 collective-permute-done.5.odd_b
  48.7 0.0 collective-permute-done.6.even_b
  48.7 2.0 %shard_map.123 = f32[8,128]{1,0:T(8,128)} custom-call(s32[2]{0:T(128)S(1)} %pad_add_fusion.parity, f32[80,128]{1,0:T(8,128)S(1)} %collective-permute-done.5.odd_b, f32[80,128]{1,0:T(8,128)S(1)} %collective-permute-done.6.even_b, f32[80,128]{1,0:T(8,128)S(1)} %get-tuple-element.29.own_b, f32[536,128]{1,0:T(8,128)S(1)} %get-tuple-element.21.own_lon.own_odd, ...), custom_call_target="tpu_custom_call" | custom-call | flops 1000000 | bytes 1000000 | tf_op jit(solution)/shard_map/pallas_call | solution.py:557
  (1 shorter events, 0.0 us)
Async XLA Ops:
  3.7 6.8 %collective-permute-start = (f32[144,128]{1,0:T(8,128)S(1)}, f32[144,128]{1,0:T(8,128)S(1)}, u32[]{:S(2)}, u32[]{:S(2)}) collective-permute-start(f32[144,128]{1,0:T(8,128)S(1)} %get-tuple-element.20.own_odd_lat), channel_id=1, source_target_pairs={{1,2},{2,1},{3,4},{4,3},{5,6},{6,5},{9,10},{10,9},{11,12},{12,11},... | collective-permute-start | bytes 221192 | tf_op jit(solution)/shard_map/ppermute | solution.py:600
  11.2 22.4 %collective-permute-start.1 = (f32[536,128]{1,0:T(8,128)S(1)}, f32[536,128]{1,0:T(8,128)S(1)}, u32[]{:S(2)}, u32[]{:S(2)}) collective-permute-start(f32[536,128]{1,0:T(8,128)S(1)} %get-tuple-element.21.own_lon.own_odd), channel_id=1, source_target_pairs={{8,16},{9,17},{10,18},{11,19},{12,20},{13,21},{14,22},{15,23},{16,... | collective-permute-start | bytes 823304 | tf_op jit(solution)/shard_map/ppermute | solution.py:603
  27.0 9.9 %collective-permute-start.2 = (f32[536,128]{1,0:T(8,128)S(1)}, f32[536,128]{1,0:T(8,128)S(1)}, u32[]{:S(2)}, u32[]{:S(2)}) collective-permute-start(f32[536,128]{1,0:T(8,128)S(1)} %get-tuple-element.22.own_even), channel_id=1, source_target_pairs={{0,8},{1,9},{2,10},{3,11},{4,12},{5,13},{6,14},{7,15},{8,0},{9,1},... | collective-permute-start | bytes 823304 | tf_op jit(solution)/shard_map/ppermute | solution.py:602
  28.9 2.6 %collective-permute-start.3 = (f32[144,128]{1,0:T(8,128)S(1)}, f32[144,128]{1,0:T(8,128)S(1)}, u32[]{:S(2)}, u32[]{:S(2)}) collective-permute-start(f32[144,128]{1,0:T(8,128)S(1)} %get-tuple-element.20.own_odd_lat), channel_id=1, source_target_pairs={{33,34},{34,33},{35,36},{36,35},{37,38},{38,37},{41,42},{42,41},{4... | collective-permute-start | bytes 221192 | tf_op jit(solution)/shard_map/ppermute | solution.py:605
  29.6 3.2 %collective-permute-start.4 = (f32[144,128]{1,0:T(8,128)S(1)}, f32[144,128]{1,0:T(8,128)S(1)}, u32[]{:S(2)}, u32[]{:S(2)}) collective-permute-start(f32[144,128]{1,0:T(8,128)S(1)} %get-tuple-element.23.own_even_lat), channel_id=1, source_target_pairs={{0,1},{1,0},{2,3},{3,2},{4,5},{5,4},{6,7},{7,6},{8,9},{9,8},{10,11... | collective-permute-start | bytes 221192 | tf_op jit(solution)/shard_map/ppermute | solution.py:604
  37.9 10.8 %collective-permute-start.5 = (f32[80,128]{1,0:T(8,128)S(1)}, f32[80,128]{1,0:T(8,128)S(1)}, u32[]{:S(2)}, u32[]{:S(2)}) collective-permute-start(f32[80,128]{1,0:T(8,128)S(1)} %get-tuple-element.29.own_b), channel_id=1, source_target_pairs={{8,16},{9,17},{10,18},{11,19},{12,20},{13,21},{14,22},{15,23},{16,... | collective-permute-start | bytes 122888 | tf_op jit(solution)/shard_map/ppermute | solution.py:612
  42.4 6.3 %collective-permute-start.6 = (f32[80,128]{1,0:T(8,128)S(1)}, f32[80,128]{1,0:T(8,128)S(1)}, u32[]{:S(2)}, u32[]{:S(2)}) collective-permute-start(f32[80,128]{1,0:T(8,128)S(1)} %get-tuple-element.30), channel_id=1, source_target_pairs={{0,8},{1,9},{2,10},{3,11},{4,12},{5,13},{6,14},{7,15},{8,0},{9,1},... | collective-permute-start | bytes 122888 | tf_op jit(solution)/shard_map/ppermute | solution.py:613

commit v4 on v2

--- a/solution.py
+++ b/solution.py
@@ -15,8 +15,8 @@
 STRIP = 128
 FLAT = 4 * STRIP
 LON_ROWS = FLAT + 3 * ROWS
-LAT_ROWS = 17 * ROWS
-SOLVE_ROWS = 5 * ROWS + 32 + 8
+LAT_ROWS = 18 * ROWS
+SOLVE_ROWS = 5 * ROWS + 5 * ROWS
 VMEM = 12 * 1024 * 1024
 
 F32 = jnp.float32
@@ -47,6 +47,10 @@
 
 def even(axis):
     return lax.axis_index(axis) % 2 == 0
+
+
+def flat_of(ref, base=FLAT):
+    return [ref[base + 8 * i : base + 8 * i + 8, :] for i in range(3)]
 
 
 def pack_lon(
@@ -61,18 +65,14 @@
         pltpu.make_async_copy(elev, held_flat.at[0], sems.at[6]),
         pltpu.make_async_copy(diag, held_flat.at[1], sems.at[7]),
     ]
-    for copy in small + copies:
+    for copy in small[:2] + copies + small[2:]:
         copy.start()
-    for copy in small:
+    for copy in small[:2]:
         copy.wait()
     row = rows_of()
     group = row >> 1
     depth = held_int[0] * held_int[1]
     is_even = parity[0] == 0
-    for ref in (up_first, low_first):
-        ref[FLAT : FLAT + 8, :] = held_flat[0]
-        ref[FLAT + 8 : FLAT + 16, :] = held_flat[1]
-        ref[FLAT + 16 : FLAT + 24, :] = depth.astype(F32)
 
     for f in range(4):
         masked[f, 0] = jnp.zeros((ROWS, LANES), F32)
@@ -95,29 +95,34 @@
 
         lax.fori_loop(0, 16, body, 0, unroll=4)
 
-
-def flat_of(ref):
-    return [ref[FLAT + 8 * i : FLAT + 8 * i + 8, :] for i in range(3)]
+    for copy in small[2:]:
+        copy.wait()
+    for ref in (up_first, low_first):
+        ref[FLAT : FLAT + 8, :] = held_flat[0]
+        ref[FLAT + 8 : FLAT + 16, :] = held_flat[1]
+        ref[FLAT + 16 : FLAT + 24, :] = depth.astype(F32)
 
 
 def pack_lat(masked, own_lon, parity, odd_out, even_out, partial):
     row, lane = rows_of(), lanes_of()
-    slot = lane >> 3
+    high, low = lane >> 4, ((lane - 8) & 127) >> 4
+    in_even = (lane & 8) == 0
     elev, diag, depth = flat_of(own_lon)
     levels = depth.astype(jnp.int32)
     is_even = parity[1] == 0
-
-    def body(a, acc):
-        left = [None] * 4
-        right = [None] * 4
+    zero = jnp.zeros((ROWS, LANES), F32)
+
+    def tile(a, sums):
+        whole, inner, sides, flux = sums
+        first, second = [zero] * 4, [zero] * 4
         for i in range(16):
             k = 16 * a + i
-            wet = k < levels
             m = [masked[f, k + 1] for f in range(4)]
             for f in range(4):
-                x, y = by_lanes(m[f], 8 * i), by_lanes(m[f], 8 * i - 120)
-                left[f] = x if i == 0 else jnp.where(slot == i, x, left[f])
-                right[f] = y if i == 0 else jnp.where(slot == i, y, right[f])
+                if i < 8:
+                    first[f] = jnp.where(high == i, by_lanes(m[f], 16 * i - 120), first[f])
+                else:
+                    second[f] = jnp.where(low == i - 8, by_lanes(m[f], 16 * i - 240), second[f])
             w = scalar_mix(m[2], m[3])
             n1 = jnp.where(row < 7, by_rows(w, -1), 0.0)
             p1 = jnp.where(row > 0, by_rows(w, 1), 0.0)
@@ -129,27 +134,32 @@
             q2 = jnp.where(lane > 1, by_lanes(w, 2), 0.0)
             gx = 8.0 * (n1 - p1) - (n2 - p2)
             gy = 8.0 * (e1 - q1) - (e2 - q2)
-            around = jnp.where(wet, (n1 + p1) + (e1 + q1), 0.0)
-            column = jnp.where(k > 0, w, 0.0) + jnp.where(k + 1 < levels, w, 0.0)
-            acc = acc + (
-                0.94 * w + 0.02 * column + 0.005 * around - ADV * (m[0] * gx + m[1] * gy)
-            )
+            whole = whole + w
+            inner = inner + jnp.where(k + 1 < levels, w, 0.0)
+            sides = sides + jnp.where(k < levels, (n1 + p1) + (e1 + q1), 0.0)
+            flux = flux + (m[0] * gx + m[1] * gy)
         for f in range(4):
+            right = jnp.where(in_even, first[f], second[f])
+            left = by_lanes(jnp.where(in_even, second[f], first[f]), -8)
             where = pl.ds(pl.multiple_of(f * 32 + 8 * a, 8), 8)
-            odd_out[where, :] = jnp.where(is_even, left[f], right[f])
-            even_out[where, :] = jnp.where(is_even, right[f], left[f])
-        return acc
-
-    acc = 0.1 * lax.fori_loop(0, 4, body, jnp.zeros((ROWS, LANES), F32))
+            odd_out[where, :] = jnp.where(is_even, left, right)
+            even_out[where, :] = jnp.where(is_even, right, left)
+        return whole, inner, sides, flux
+
+    whole, inner, sides, flux = lax.fori_loop(0, 4, tile, (zero,) * 4)
+    top = scalar_mix(masked[2, 1], masked[3, 1])
+    acc = 0.1 * (0.94 * whole + 0.02 * (whole - top + inner) + 0.005 * sides - ADV * flux)
     partial[...] = acc
-    flat = (acc, elev, diag, depth)
-    left = right = None
-    for i, x in enumerate(flat):
-        a, b = by_lanes(x, 8 * i), by_lanes(x, 8 * i - 120)
-        left = a if i == 0 else jnp.where(slot == i, a, left)
-        right = b if i == 0 else jnp.where(slot == i, b, right)
+    slot = lane >> 3
+    left = right = zero
+    for i, x in enumerate((acc, elev, diag, depth)):
+        left = jnp.where(slot == i, by_lanes(x, 8 * i), left)
+        right = jnp.where(slot == i, by_lanes(x, 8 * i - 120), right)
     odd_out[128:136, :] = jnp.where(is_even, left, right)
     even_out[128:136, :] = jnp.where(is_even, right, left)
+    left, right = tile_lanes(depth), tile_lanes(by_lanes(depth, 8))
+    odd_out[136:144, :] = jnp.where(is_even, left, right)
+    even_out[136:144, :] = jnp.where(is_even, right, left)
 
 
 def tile_lanes(x):
@@ -166,7 +176,8 @@
 
 
 def wet_pack(depth, a):
-    return (16 * a + (lanes_of() >> 3)).astype(F32) < depth
+    slot = lanes_of() >> 3
+    return (16 * a + (slot >> 1) + 8 * (slot & 1)).astype(F32) < depth
 
 
 def lat_rims(a_v, a_w, a_depth, b_v, b_w, b_depth):
@@ -240,18 +251,20 @@
     ext_l = [four(got_odd_lat, f * 32, lat_even, got_even_lat) for f in range(4)]
     flat_r = jnp.where(lat_even, got_even_lat[128:136, :], got_odd_lat[128:136, :])
     flat_l = jnp.where(lat_even, got_odd_lat[128:136, :], got_even_lat[128:136, :])
+    depth_r = jnp.where(lat_even, got_even_lat[136:144, :], got_odd_lat[136:144, :])
+    depth_l = jnp.where(lat_even, got_odd_lat[136:144, :], got_even_lat[136:144, :])
+    own_depth_r = jnp.where(lat_even, own_even_lat[136:144, :], own_odd_lat[136:144, :])
+    own_depth_l = jnp.where(lat_even, own_odd_lat[136:144, :], own_even_lat[136:144, :])
 
     def mixed(pair):
         return [scalar_mix(x, y) for x, y in zip(*pair, strict=True)]
 
     w_r, w_l = mixed(ext_r[2:]), mixed(ext_l[2:])
     miss_own_r, miss_ext_r = lat_rims(
-        own_r[0], mixed(own_r[1:]), tile_lanes(by_lanes(depth, 8)),
-        ext_r[1], w_r, tile_lanes(by_lanes(flat_r, -24)),
+        own_r[0], mixed(own_r[1:]), own_depth_r, ext_r[1], w_r, depth_r
     )
     miss_ext_l, miss_own_l = lat_rims(
-        ext_l[1], w_l, tile_lanes(by_lanes(flat_l, -24)),
-        own_l[0], mixed(own_l[1:]), tile_lanes(depth),
+        ext_l[1], w_l, depth_l, own_l[0], mixed(own_l[1:]), own_depth_l
     )
     total = total + jnp.where(lane >= 126, miss_own_r, 0.0) + jnp.where(lane < 2, miss_own_l, 0.0)
 
@@ -269,16 +282,13 @@
     for ref in (odd_out, even_out):
         for i, x in enumerate((total, total_side, elev_side, side(2), side(3))):
             ref[8 * i : 8 * i + 8, :] = x
-        ref[SOLVE_ROWS - 8 : SOLVE_ROWS, :] = jnp.zeros((8, LANES), F32)
-    packs = ext_r[0] + ext_l[0] + w_r + w_l
+    packs = ext_r[0] + ext_l[0] + w_r + w_l + [depth_r, depth_l]
     group = row >> 1
-    for i in range(4):
-        top = bottom = None
-        for j in range(4):
-            x = packs[4 * i + j]
-            a, b = by_rows(x, 2 * j), by_rows(x, 2 * j - 6)
-            top = a if j == 0 else jnp.where(group == j, a, top)
-            bottom = b if j == 0 else jnp.where(group == j, b, bottom)
+    for i in range(5):
+        top = bottom = jnp.zeros((ROWS, LANES), F32)
+        for j, x in enumerate(packs[4 * i : 4 * i + 4]):
+            top = jnp.where(group == j, by_rows(x, 2 * j), top)
+            bottom = jnp.where(group == j, by_rows(x, 2 * j - 6), bottom)
         at = slice(40 + 8 * i, 48 + 8 * i)
         odd_out[at, :] = jnp.where(lon_even, top, bottom)
         even_out[at, :] = jnp.where(lon_even, bottom, top)
@@ -295,15 +305,19 @@
     lon_even, lat_even = parity[0] == 0, parity[1] == 0
     outs = (o1, o2, o3, o4)
 
+    in_even = (lane & 8) == 0
+
     def unpack(a, carry):
         for f in range(4):
             at = pl.ds(pl.multiple_of(f * 32 + 8 * a, 8), 8)
             x, y = odd_lat[at, :], even_lat[at, :]
-            west, east = jnp.where(lat_even, x, y), jnp.where(lat_even, y, x)
-            for i in range(16):
-                rims[f, 16 * a + i] = jnp.where(
-                    lane < 64, by_lanes(east, -8 * i), by_lanes(west, 120 - 8 * i)
-                )
+            west = jnp.where(lat_even, x, y)
+            east = by_lanes(jnp.where(lat_even, y, x), 8)
+            first = jnp.where(in_even, west, east)
+            second = jnp.where(in_even, east, west)
+            for i in range(8):
+                rims[f, 16 * a + i] = by_lanes(first, -16 * i - 8)
+                rims[f, 16 * a + 8 + i] = by_lanes(second, -16 * i - 16)
         return carry
 
     lax.fori_loop(0, 4, unpack, 0)
@@ -384,6 +398,9 @@
     def rim_rows(tile, q, first):
         return by_rows(tile[5 + q // 4], first - 2 * (q % 4))
 
+    def near_rows(q):
+        return jnp.where(row < 4, rim_rows(upper, q, 0), rim_rows(lower, q, 6))
+
     def side_parts(ext, base, own_depth, near_depth):
         mine = theirs = jnp.zeros((ROWS, LANES), F32)
         for i in range(4):
@@ -394,15 +411,13 @@
             mine = mine + lon_part(vel, wet_pack(own_depth, i), x1, x2)
             y2 = jnp.where(row < 4, by_rows(w, 2), by_rows(w, -2))
             y1 = jnp.where(row < 4, by_rows(w, 1), by_rows(w, -1))
-            other = jnp.where(row < 4, rim_rows(upper, qu, 0), rim_rows(lower, qu, 6))
-            theirs = theirs + lon_part(other, wet_pack(near_depth, i), y1, y2)
+            theirs = theirs + lon_part(near_rows(qu), wet_pack(near_depth, i), y1, y2)
         return 0.1 * sum_slots(mine), 0.1 * sum_slots(theirs)
 
-    near_side = jnp.where(row < 4, upper[4], lower[4])
-    mine_r, theirs_r = side_parts(ext_r, 0, tile_lanes(own[4]), tile_lanes(near_side))
-    mine_l, theirs_l = side_parts(
-        ext_l, 4, tile_lanes(by_lanes(own[4], 8)), tile_lanes(by_lanes(near_side, 8))
-    )
+    depth_r = jnp.where(lat_even, even_lat[136:144, :], odd_lat[136:144, :])
+    depth_l = jnp.where(lat_even, odd_lat[136:144, :], even_lat[136:144, :])
+    mine_r, theirs_r = side_parts(ext_r, 0, depth_r, near_rows(16))
+    mine_l, theirs_l = side_parts(ext_l, 4, depth_l, near_rows(17))
     in_r, in_l = lane < 8, lane >= 120
     mine = jnp.where(in_r, mine_r, jnp.where(in_l, mine_l, 0.0))
     theirs = jnp.where(in_r, theirs_r, jnp.where(in_l, theirs_l, 0.0))

time: 50.7 us -> 50.3 us (level)
  transfers between devices with their start and end apart: 6 -> 6, of which waited for: 1 -> 2; matrix products, arithmetic and copies ran while one was open for 0% -> 0% of each run, Pallas kernels for 12% -> 12%
where the time goes in v4:
time: 50.3 us; the launch traced here: 50 us
  starting transfers between devices  36.8 us (73%)
  Pallas kernels  11.1 us (22%)
  waiting for transfers between devices  1.24 us (2%)
  between operations  0.72 us (1%)
    ppermute x1, starting transfers between devices, on_device(): got_odd = lax.ppermute(own_odd, 'lon', lon_odd)  22.5 us
    ppermute x1, starting transfers between devices, on_device(): lat_got_odd = lax.ppermute(lat_own_odd, 'lat', lat_odd)  4.89 us
    pallas_call x1, Pallas kernels, call_fields(): call(fields, (shaped(LEVELS, ROWS, LANES),) * 4, [SMEM] + [WHOLE] * 6, 10...  4.35 us
    ppermute x1, starting transfers between devices, on_device(): b_got_even = lax.ppermute(b_even, 'lon', lon_even)  3.64 us
    pallas_call x1, Pallas kernels, call_pack_lon(): call(pack_lon, (shaped(4, LEVELS + 4, ROWS, LANES), shaped(LON_ROWS, LANE...  2.07 us
    pallas_call x1, Pallas kernels, call_solve(): call(solve, shaped(ROWS, LANES), [SMEM] + [WHOLE] * 8, 10 ** 6, 10 ** 6)  2.01 us
    ppermute x1, starting transfers between devices, on_device(): lat_got_even = lax.ppermute(lat_own_even, 'lat', lat_even)  1.92 us
    ppermute x1, starting transfers between devices, on_device(): got_even = lax.ppermute(own_even, 'lon', lon_even)  1.92 us
  transfers between devices with their start and end apart: 6, of which 2 were waited for; matrix products, arithmetic and copies ran while one was open for 0% of the time, Pallas kernels for 12%

profile of v4, /device:TPU:1, one launch (start us, length us, event | category | flops | bytes accessed | tf_op | source)
XLA Modules:
  0.0 50.0 jit_solution(8856587763088098609)
XLA Ops:
  0.6 0.1 pad_add_fusion.parity
  0.7 2.1 %shard_map.119 = (f32[4,66,8,128]{3,2,1,0:T(8,128)S(1)}, f32[536,128]{1,0:T(8,128)S(1)}, f32[536,128]{1,0:T(8,128)S(1)}) custom-call(f32[62,8,128]{2,1,0:T(8,128)} %u.1, f32[62,8,128]{2,1,0:T(8,128)} %v.1, f32[62,8,128]{2,1,0:T(8,128)} %t.1, f32[62,8,128]{2,1,0:T(8,128)} %s.1, s32[8,128]{1,0:T(8,128)} %water.1, s32[8,128]{1,0:T(8,128)} %layers.1, ...), custom_call_target="tpu_custom_call" | custom-call | flops 1000000 | bytes 2031616 | tf_op jit(solution)/shard_map/pallas_call | solution.py:504
  2.8 22.5 %collective-permute-start = (f32[536,128]{1,0:T(8,128)S(1)}, f32[536,128]{1,0:T(8,128)S(1)}, u32[]{:S(2)}, u32[]{:S(2)}) collective-permute-start(f32[536,128]{1,0:T(8,128)S(1)} %get-tuple-element.18.own_lon.own_odd), channel_id=1, source_target_pairs={{0,1016},{8,16},{16,8},{24,32},{32,24},{40,48},{48,40},{56,64},{64... | collective-permute-start | bytes 823304 | tf_op jit(solution)/shard_map/ppermute | solution.py:561
  25.3 1.9 %collective-permute-start.1 = (f32[536,128]{1,0:T(8,128)S(1)}, f32[536,128]{1,0:T(8,128)S(1)}, u32[]{:S(2)}, u32[]{:S(2)}) collective-permute-start(f32[536,128]{1,0:T(8,128)S(1)} %get-tuple-element.19.own_even), channel_id=1, source_target_pairs={{0,8},{8,0},{16,24},{24,16},{32,40},{40,32},{48,56},{56,48},{64,72... | collective-permute-start | bytes 823304 | tf_op jit(solution)/shard_map/ppermute | solution.py:560
  27.2 1.8 %shard_map.120 = (f32[144,128]{1,0:T(8,128)S(1)}, f32[144,128]{1,0:T(8,128)S(1)}, f32[8,128]{1,0:T(8,128)S(1)}) custom-call(f32[4,66,8,128]{3,2,1,0:T(8,128)S(1)} %get-tuple-element.17.masked, f32[536,128]{1,0:T(8,128)S(1)} %get-tuple-element.18.own_lon.own_odd, s32[2]{0:T(128)S(1)} %pad_add_fusion.parity), custom_call_target="tpu_custom_call" | custom-call | flops 4000000 | bytes 1015808 | tf_op jit(solution)/shard_map/pallas_call | solution.py:519
  29.0 4.9 %collective-permute-start.2 = (f32[144,128]{1,0:T(8,128)S(1)}, f32[144,128]{1,0:T(8,128)S(1)}, u32[]{:S(2)}, u32[]{:S(2)}) collective-permute-start(f32[144,128]{1,0:T(8,128)S(1)} %get-tuple-element.20.own_odd_lat), channel_id=1, source_target_pairs={{1,2},{2,1},{3,4},{4,3},{5,6},{6,5},{9,10},{10,9},{11,12},{12,11},... | collective-permute-start | bytes 221192 | tf_op jit(solution)/shard_map/ppermute | solution.py:563
  33.9 1.9 %collective-permute-start.3 = (f32[144,128]{1,0:T(8,128)S(1)}, f32[144,128]{1,0:T(8,128)S(1)}, u32[]{:S(2)}, u32[]{:S(2)}) collective-permute-start(f32[144,128]{1,0:T(8,128)S(1)} %get-tuple-element.21.own_even_lat), channel_id=1, source_target_pairs={{0,1},{1,0},{2,3},{3,2},{4,5},{5,4},{6,7},{7,6},{8,9},{9,8},{10,11... | collective-permute-start | bytes 221192 | tf_op jit(solution)/shard_map/ppermute | solution.py:564
  35.8 0.1 collective-permute-done.2.odd_lat.got_odd_lat
  35.9 1.1 %collective-permute-done.3.even_lat.got_even_lat = f32[144,128]{1,0:T(8,128)S(1)} collective-permute-done((f32[144,128]{1,0:T(8,128)S(1)}, f32[144,128]{1,0:T(8,128)S(1)}, u32[]{:S(2)}, u32[]{:S(2)}) %collective-permute-start.3) | collective-permute-done | bytes 73760 | tf_op jit(solution)/shard_map/ppermute | solution.py:564
  37.0 0.0 collective-permute-done.odd_lon.got_odd
  37.0 0.0 collective-permute-done.1.even_lon.got_even
  37.0 0.9 %shard_map.122 = (f32[80,128]{1,0:T(8,128)S(1)}, f32[80,128]{1,0:T(8,128)S(1)}) custom-call(s32[2]{0:T(128)S(1)} %pad_add_fusion.parity, f32[536,128]{1,0:T(8,128)S(1)} %collective-permute-done.1.even_lon.got_even, f32[536,128]{1,0:T(8,128)S(1)} %collective-permute-done.odd_lon.got_odd, f32[536,128]{1,0:T(8,128)S(1)} %get-tuple-element.18.own_lon.own_odd, ...), custom_call_target="tpu_custom_call" | custom-call | flops 1000000 | bytes 1000000 | tf_op jit(solution)/shard_map/pallas_call | solution.py:526
  38.0 1.9 %collective-permute-start.4 = (f32[80,128]{1,0:T(8,128)S(1)}, f32[80,128]{1,0:T(8,128)S(1)}, u32[]{:S(2)}, u32[]{:S(2)}) collective-permute-start(f32[80,128]{1,0:T(8,128)S(1)} %get-tuple-element.27.own_b), channel_id=1, source_target_pairs={{0,1016},{8,16},{16,8},{24,32},{32,24},{40,48},{48,40},{56,64},{64... | collective-permute-start | bytes 122888 | tf_op jit(solution)/shard_map/ppermute | solution.py:570
  39.9 3.6 %collective-permute-start.5 = (f32[80,128]{1,0:T(8,128)S(1)}, f32[80,128]{1,0:T(8,128)S(1)}, u32[]{:S(2)}, u32[]{:S(2)}) collective-permute-start(f32[80,128]{1,0:T(8,128)S(1)} %get-tuple-element.28), channel_id=1, source_target_pairs={{0,8},{8,0},{16,24},{24,16},{32,40},{40,32},{48,56},{56,48},{64,72... | collective-permute-start | bytes 122888 | tf_op jit(solution)/shard_map/ppermute | solution.py:571
  43.6 4.4 %shard_map.121 = (f32[62,8,128]{2,1,0:T(8,128)}, f32[62,8,128]{2,1,0:T(8,128)}, f32[62,8,128]{2,1,0:T(8,128)}, f32[62,8,128]{2,1,0:T(8,128)}) custom-call(s32[2]{0:T(128)S(1)} %pad_add_fusion.parity, f32[4,66,8,128]{3,2,1,0:T(8,128)S(1)} %get-tuple-element.17.masked, f32[536,128]{1,0:T(8,128)S(1)} %get-tuple-element.18.own_lon.own_odd, ...), custom_call_target="tpu_custom_call" | custom-call | flops 10000000 | bytes 3047424 | tf_op jit(solution)/shard_map/pallas_call | solution.py:532
  47.9 0.0 collective-permute-done.4.odd_b
  47.9 0.0 collective-permute-done.5.even_b
  47.9 2.0 %shard_map.123 = f32[8,128]{1,0:T(8,128)} custom-call(s32[2]{0:T(128)S(1)} %pad_add_fusion.parity, f32[80,128]{1,0:T(8,128)S(1)} %collective-permute-done.4.odd_b, f32[80,128]{1,0:T(8,128)S(1)} %collective-permute-done.5.even_b, f32[80,128]{1,0:T(8,128)S(1)} %get-tuple-element.27.own_b, f32[536,128]{1,0:T(8,128)S(1)} %get-tuple-element.18.own_lon.own_odd, ...), custom_call_target="tpu_custom_call" | custom-call | flops 1000000 | bytes 1000000 | tf_op jit(solution)/shard_map/pallas_call | solution.py:544
Async XLA Ops:
  2.8 34.3 %collective-permute-start = (f32[536,128]{1,0:T(8,128)S(1)}, f32[536,128]{1,0:T(8,128)S(1)}, u32[]{:S(2)}, u32[]{:S(2)}) collective-permute-start(f32[536,128]{1,0:T(8,128)S(1)} %get-tuple-element.18.own_lon.own_odd), channel_id=1, source_target_pairs={{0,1016},{8,16},{16,8},{24,32},{32,24},{40,48},{48,40},{56,64},{64... | collective-permute-start | bytes 823304 | tf_op jit(solution)/shard_map/ppermute | solution.py:561
  25.3 11.8 %collective-permute-start.1 = (f32[536,128]{1,0:T(8,128)S(1)}, f32[536,128]{1,0:T(8,128)S(1)}, u32[]{:S(2)}, u32[]{:S(2)}) collective-permute-start(f32[536,128]{1,0:T(8,128)S(1)} %get-tuple-element.19.own_even), channel_id=1, source_target_pairs={{0,8},{8,0},{16,24},{24,16},{32,40},{40,32},{48,56},{56,48},{64,72... | collective-permute-start | bytes 823304 | tf_op jit(solution)/shard_map/ppermute | solution.py:560
  29.0 6.9 %collective-permute-start.2 = (f32[144,128]{1,0:T(8,128)S(1)}, f32[144,128]{1,0:T(8,128)S(1)}, u32[]{:S(2)}, u32[]{:S(2)}) collective-permute-start(f32[144,128]{1,0:T(8,128)S(1)} %get-tuple-element.20.own_odd_lat), channel_id=1, source_target_pairs={{1,2},{2,1},{3,4},{4,3},{5,6},{6,5},{9,10},{10,9},{11,12},{12,11},... | collective-permute-start | bytes 221192 | tf_op jit(solution)/shard_map/ppermute | solution.py:563
  33.9 3.2 %collective-permute-start.3 = (f32[144,128]{1,0:T(8,128)S(1)}, f32[144,128]{1,0:T(8,128)S(1)}, u32[]{:S(2)}, u32[]{:S(2)}) collective-permute-start(f32[144,128]{1,0:T(8,128)S(1)} %get-tuple-element.21.own_even_lat), channel_id=1, source_target_pairs={{0,1},{1,0},{2,3},{3,2},{4,5},{5,4},{6,7},{7,6},{8,9},{9,8},{10,11... | collective-permute-start | bytes 221192 | tf_op jit(solution)/shard_map/ppermute | solution.py:564
  38.0 9.9 %collective-permute-start.4 = (f32[80,128]{1,0:T(8,128)S(1)}, f32[80,128]{1,0:T(8,128)S(1)}, u32[]{:S(2)}, u32[]{:S(2)}) collective-permute-start(f32[80,128]{1,0:T(8,128)S(1)} %get-tuple-element.27.own_b), channel_id=1, source_target_pairs={{0,1016},{8,16},{16,8},{24,32},{32,24},{40,48},{48,40},{56,64},{64... | collective-permute-start | bytes 122888 | tf_op jit(solution)/shard_map/ppermute | solution.py:570
  39.9 8.0 %collective-permute-start.5 = (f32[80,128]{1,0:T(8,128)S(1)}, f32[80,128]{1,0:T(8,128)S(1)}, u32[]{:S(2)}, u32[]{:S(2)}) collective-permute-start(f32[80,128]{1,0:T(8,128)S(1)} %get-tuple-element.28), channel_id=1, source_target_pairs={{0,8},{8,0},{16,24},{24,16},{32,40},{40,32},{48,56},{56,48},{64,72... | collective-permute-start | bytes 122888 | tf_op jit(solution)/shard_map/ppermute | solution.py:571

commit v5 on v4

--- a/solution.py
+++ b/solution.py
@@ -93,7 +93,7 @@
             low_first[at, :] = jnp.where(is_even, bottom, top)
             return carry
 
-        lax.fori_loop(0, 16, body, 0, unroll=4)
+        lax.fori_loop(0, 16, body, 0, unroll=True)
 
     for copy in small[2:]:
         copy.wait()
@@ -101,6 +101,26 @@
         ref[FLAT : FLAT + 8, :] = held_flat[0]
         ref[FLAT + 8 : FLAT + 16, :] = held_flat[1]
         ref[FLAT + 16 : FLAT + 24, :] = depth.astype(F32)
+
+
+BF16 = jnp.bfloat16
+
+
+def lat_matrix():
+    shape = (2 * LANES, 2 * LANES)
+    source = rows_of(shape) & 127
+    target = lanes_of(shape)
+    d = source - (target & 127)
+    slope = jnp.where(d == 1, 8.0, jnp.where(d == -1, -8.0, 0.0))
+    slope = slope + jnp.where(d == 2, -1.0, jnp.where(d == -2, 1.0, 0.0))
+    near = jnp.where(jnp.abs(d) == 1, 1.0, 0.0)
+    return jnp.where(target < LANES, slope, near).astype(BF16)
+
+
+def lat_terms(x, matrix):
+    high = x.astype(BF16)
+    rest = (x - high.astype(F32)).astype(BF16)
+    return jnp.dot(jnp.concatenate([high, rest], axis=1), matrix, preferred_element_type=F32)
 
 
 def pack_lat(masked, own_lon, parity, odd_out, even_out, partial):
@@ -111,10 +131,18 @@
     levels = depth.astype(jnp.int32)
     is_even = parity[1] == 0
     zero = jnp.zeros((ROWS, LANES), F32)
+    matrix = lat_matrix()
+    left, right = tile_lanes(depth), tile_lanes(by_lanes(depth, 8))
+    odd_out[136:144, :] = jnp.where(is_even, left, right)
+    even_out[136:144, :] = jnp.where(is_even, right, left)
 
     def tile(a, sums):
         whole, inner, sides, flux = sums
         first, second = [zero] * 4, [zero] * 4
+        tracer = [
+            scalar_mix(masked[2, 16 * a + i + 1], masked[3, 16 * a + i + 1]) for i in range(16)
+        ]
+        terms = lat_terms(jnp.concatenate(tracer, axis=0), matrix)
         for i in range(16):
             k = 16 * a + i
             m = [masked[f, k + 1] for f in range(4)]
@@ -123,20 +151,17 @@
                     first[f] = jnp.where(high == i, by_lanes(m[f], 16 * i - 120), first[f])
                 else:
                     second[f] = jnp.where(low == i - 8, by_lanes(m[f], 16 * i - 240), second[f])
-            w = scalar_mix(m[2], m[3])
+            w = tracer[i]
             n1 = jnp.where(row < 7, by_rows(w, -1), 0.0)
             p1 = jnp.where(row > 0, by_rows(w, 1), 0.0)
             n2 = jnp.where(row < 6, by_rows(w, -2), 0.0)
             p2 = jnp.where(row > 1, by_rows(w, 2), 0.0)
-            e1 = jnp.where(lane < 127, by_lanes(w, -1), 0.0)
-            q1 = jnp.where(lane > 0, by_lanes(w, 1), 0.0)
-            e2 = jnp.where(lane < 126, by_lanes(w, -2), 0.0)
-            q2 = jnp.where(lane > 1, by_lanes(w, 2), 0.0)
             gx = 8.0 * (n1 - p1) - (n2 - p2)
-            gy = 8.0 * (e1 - q1) - (e2 - q2)
+            gy = terms[8 * i : 8 * i + 8, :LANES]
+            around = (n1 + p1) + terms[8 * i : 8 * i + 8, LANES:]
             whole = whole + w
             inner = inner + jnp.where(k + 1 < levels, w, 0.0)
-            sides = sides + jnp.where(k < levels, (n1 + p1) + (e1 + q1), 0.0)
+            sides = sides + jnp.where(k < levels, around, 0.0)
             flux = flux + (m[0] * gx + m[1] * gy)
         for f in range(4):
             right = jnp.where(in_even, first[f], second[f])
@@ -146,7 +171,7 @@
             even_out[where, :] = jnp.where(is_even, right, left)
         return whole, inner, sides, flux
 
-    whole, inner, sides, flux = lax.fori_loop(0, 4, tile, (zero,) * 4)
+    whole, inner, sides, flux = lax.fori_loop(0, 4, tile, (zero,) * 4, unroll=True)
     top = scalar_mix(masked[2, 1], masked[3, 1])
     acc = 0.1 * (0.94 * whole + 0.02 * (whole - top + inner) + 0.005 * sides - ADV * flux)
     partial[...] = acc
@@ -157,21 +182,15 @@
         right = jnp.where(slot == i, by_lanes(x, 8 * i - 120), right)
     odd_out[128:136, :] = jnp.where(is_even, left, right)
     even_out[128:136, :] = jnp.where(is_even, right, left)
-    left, right = tile_lanes(depth), tile_lanes(by_lanes(depth, 8))
-    odd_out[136:144, :] = jnp.where(is_even, left, right)
-    even_out[136:144, :] = jnp.where(is_even, right, left)
 
 
 def tile_lanes(x):
-    x = jnp.where(lanes_of() < 8, x, 0.0)
-    for d in (8, 16, 32, 64):
-        x = x + by_lanes(x, d)
-    return x
+    return sum_slots(jnp.where(lanes_of() < 8, x, 0.0))
 
 
 def sum_slots(x):
-    for d in (8, 16, 32, 64):
-        x = x + by_lanes(x, d)
+    for d in (8, 32):
+        x = (x + by_lanes(x, d)) + (by_lanes(x, 2 * d) + by_lanes(x, 3 * d))
     return x
 
 
@@ -180,25 +199,26 @@
     return (16 * a + (slot >> 1) + 8 * (slot & 1)).astype(F32) < depth
 
 
+def west_part(vel, depth, east, i):
+    column = lanes_of() & 7
+    y1 = jnp.where(column == 7, by_lanes(east, 7), 0.0)
+    y2 = jnp.where(column >= 6, by_lanes(east, 6), 0.0)
+    return 0.005 * jnp.where(wet_pack(depth, i), y1, 0.0) - ADV * vel * (8.0 * y1 - y2)
+
+
+def east_part(vel, depth, west, i):
+    column = lanes_of() & 7
+    z1 = jnp.where(column == 0, by_lanes(west, -7), 0.0)
+    z2 = jnp.where(column <= 1, by_lanes(west, -6), 0.0)
+    return 0.005 * jnp.where(wet_pack(depth, i), z1, 0.0) - ADV * vel * (z2 - 8.0 * z1)
+
+
 def lat_rims(a_v, a_w, a_depth, b_v, b_w, b_depth):
-    column = lanes_of() & 7
     a_sum = b_sum = jnp.zeros((ROWS, LANES), F32)
     for i in range(4):
-        y1, y2 = by_lanes(b_w[i], 7), by_lanes(b_w[i], 6)
-        y1 = jnp.where(column == 7, y1, 0.0)
-        y2 = jnp.where(column >= 6, y2, 0.0)
-        a_sum = a_sum - ADV * a_v[i] * (8.0 * y1 - y2)
-        a_sum = a_sum + 0.005 * jnp.where(wet_pack(a_depth, i), y1, 0.0)
-        z1, z2 = by_lanes(a_w[i], -7), by_lanes(a_w[i], -6)
-        z1 = jnp.where(column == 0, z1, 0.0)
-        z2 = jnp.where(column <= 1, z2, 0.0)
-        b_sum = b_sum - ADV * b_v[i] * (z2 - 8.0 * z1)
-        b_sum = b_sum + 0.005 * jnp.where(wet_pack(b_depth, i), z1, 0.0)
+        a_sum = a_sum + west_part(a_v[i], a_depth, b_w[i], i)
+        b_sum = b_sum + east_part(b_v[i], b_depth, a_w[i], i)
     return 0.1 * sum_slots(a_sum), 0.1 * sum_slots(b_sum)
-
-
-def pick(flag, a, b):
-    return jnp.where(flag, a, b)
 
 
 def four(ref, base, flag, other):
@@ -298,29 +318,40 @@
 
 
 def fields(
-    parity, masked, own_lon, odd_lon, even_lon, odd_lat, even_lat, o1, o2, o3, o4, rims, fresh, sems
+    parity, masked, own_lon, own_odd_lat, own_even_lat, odd_lon, even_lon, odd_lat, even_lat,
+    o1, o2, o3, o4, terms, rims, fresh, sems,
 ):
     row, lane = rows_of(), lanes_of()
     levels = flat_of(own_lon)[2].astype(jnp.int32)
     lon_even, lat_even = parity[0] == 0, parity[1] == 0
     outs = (o1, o2, o3, o4)
+    at_edge = (lane < 2) | (lane >= 126)
+
+    matrix = lat_matrix()
+    for f in range(4):
+        for first in range(0, LEVELS, 16):
+            count = min(16, LEVELS - first)
+            x = masked[f, first + 1 : first + 1 + count].reshape(count * ROWS, LANES)
+            terms[f, ROWS * first : ROWS * (first + count), :] = lat_terms(x, matrix)
 
     in_even = (lane & 8) == 0
 
-    def unpack(a, carry):
+    def west_east(odd, even, base):
+        x, y = odd[base : base + 8, :], even[base : base + 8, :]
+        return jnp.where(lat_even, x, y), jnp.where(lat_even, y, x)
+
+    depth_west, depth_east = west_east(own_odd_lat, own_even_lat, 136)
+    for a in range(4):
+        vel_west, vel_east = west_east(own_odd_lat, own_even_lat, 32 + 8 * a)
         for f in range(4):
-            at = pl.ds(pl.multiple_of(f * 32 + 8 * a, 8), 8)
-            x, y = odd_lat[at, :], even_lat[at, :]
-            west = jnp.where(lat_even, x, y)
-            east = by_lanes(jnp.where(lat_even, y, x), 8)
-            first = jnp.where(in_even, west, east)
-            second = jnp.where(in_even, east, west)
+            west, east = west_east(odd_lat, even_lat, f * 32 + 8 * a)
+            right = west_part(vel_east, depth_east, east, a)
+            left = by_lanes(east_part(vel_west, depth_west, west, a), 8)
+            first = jnp.where(in_even, right, left)
+            second = jnp.where(in_even, left, right)
             for i in range(8):
                 rims[f, 16 * a + i] = by_lanes(first, -16 * i - 8)
                 rims[f, 16 * a + 8 + i] = by_lanes(second, -16 * i - 16)
-        return carry
-
-    lax.fori_loop(0, 4, unpack, 0)
 
     def group(g, count):
         strips = []
@@ -333,6 +364,7 @@
             wet = k < levels
             center = [masked[f, k + 1] for f in range(4)]
             zonal, merid = ADV * center[0], ADV * center[1]
+            at = pl.ds(pl.multiple_of(ROWS * k, ROWS), ROWS)
             for f in range(4):
                 m = center[f]
                 upper, lower = strips[f]
@@ -341,17 +373,12 @@
                 n2 = by_rows(jnp.where(row < 2, rim, m), -2)
                 p1 = by_rows(jnp.where(row > 6, rim, m), 1)
                 p2 = by_rows(jnp.where(row > 5, rim, m), 2)
-                beside = rims[f, k]
-                e1 = by_lanes(jnp.where(lane < 1, beside, m), -1)
-                e2 = by_lanes(jnp.where(lane < 2, beside, m), -2)
-                q1 = by_lanes(jnp.where(lane > 126, beside, m), 1)
-                q2 = by_lanes(jnp.where(lane > 125, beside, m), 2)
                 gx = 8.0 * (n1 - p1) - (n2 - p2)
-                gy = 8.0 * (e1 - q1) - (e2 - q2)
-                around = (n1 + p1) + (e1 + q1)
+                gy = terms[f, at, :LANES]
+                around = (n1 + p1) + terms[f, at, LANES:]
                 column = masked[f, k] + masked[f, k + 2]
                 value = 0.94 * m + 0.02 * column + 0.005 * around - (zonal * gx + merid * gy)
-                fresh[f, k] = jnp.where(wet, value, 0.0)
+                fresh[f, k] = jnp.where(wet, value, 0.0) + jnp.where(at_edge, rims[f, k], 0.0)
 
     def body(g, carry):
         group(g, 4)
@@ -369,7 +396,7 @@
             copies[-1].start()
 
     for first, last in CHUNKS:
-        lax.fori_loop(first, last, body, 0)
+        lax.fori_loop(first, last, body, 0, unroll=True)
         send(4 * first, 4 * last)
     group(15, LEVELS - 60)
     send(60, LEVELS)
@@ -530,9 +557,10 @@
 
 def call_fields(*args):
     return call(
-        fields, (shaped(LEVELS, ROWS, LANES),) * 4, [SMEM] + [WHOLE] * 6, 10**7, 3 * BLOCK,
+        fields, (shaped(LEVELS, ROWS, LANES),) * 4, [SMEM] + [WHOLE] * 8, 10**7, 3 * BLOCK,
         out_specs=(HERE,) * 4,
         scratch_shapes=[
+            pltpu.VMEM((4, LEVELS * ROWS, 2 * LANES), F32),
             pltpu.VMEM((4, LEVELS + 2, ROWS, LANES), F32),
             pltpu.VMEM((4, LEVELS, ROWS, LANES), F32),
             pltpu.SemaphoreType.DMA((16,)),
@@ -570,7 +598,9 @@
     b_got_odd = lax.ppermute(b_odd, "lon", lon_odd)
     b_got_even = lax.ppermute(b_even, "lon", lon_even)
 
-    fresh = call_fields(parity, masked, own_odd, got_odd, got_even, lat_got_odd, lat_got_even)
+    fresh = call_fields(
+        parity, masked, own_odd, lat_own_odd, lat_own_even, got_odd, got_even, lat_got_odd, lat_got_even
+    )
     height = call_solve(
         parity, b_got_odd, b_got_even, b_odd, own_odd, got_odd, got_even, lat_got_odd, lat_got_even
     )

time: 50.3 us -> 48.8 us (0.970)
  the two profiles are of different devices: /device:TPU:1 before, /device:TPU:4 now
where the time goes in v5:
time: 48.8 us; the launch traced here: 48.5 us
  starting transfers between devices  36.9 us (76%)
  Pallas kernels  9.19 us (19%)
  waiting for transfers between devices  1.55 us (3%)
  between operations  0.72 us (1%)
    ppermute x1, starting transfers between devices, on_device(): got_odd = lax.ppermute(own_odd, 'lon', lon_odd)  21.9 us
    ppermute x1, starting transfers between devices, on_device(): lat_got_even = lax.ppermute(lat_own_even, 'lat', lat_even)  4.74 us
    ppermute x1, starting transfers between devices, on_device(): b_got_odd = lax.ppermute(b_odd, 'lon', lon_odd)  4.48 us
    pallas_call x1, Pallas kernels, call_fields(): call(fields, (shaped(LEVELS, ROWS, LANES),) * 4, [SMEM] + [WHOLE] * 8, 10...  3.3 us
    pallas_call x1, Pallas kernels, call_pack_lon(): call(pack_lon, (shaped(4, LEVELS + 4, ROWS, LANES), shaped(LON_ROWS, LANE...  2.01 us
    ppermute x1, starting transfers between devices, on_device(): got_even = lax.ppermute(own_even, 'lon', lon_even)  1.92 us
    ppermute x1, starting transfers between devices, on_device(): lat_got_odd = lax.ppermute(lat_own_odd, 'lat', lat_odd)  1.92 us
    ppermute x1, starting transfers between devices, on_device(): b_got_even = lax.ppermute(b_even, 'lon', lon_even)  1.92 us
  transfers between devices with their start and end apart: 6, of which 3 were waited for; matrix products, arithmetic and copies ran while one was open for 0% of the time, Pallas kernels for 9%

profile of v5, /device:TPU:4, one launch (start us, length us, event | category | flops | bytes accessed | tf_op | source)
XLA Modules:
  0.0 48.5 jit_solution(15465474436368323139)
XLA Ops:
  0.6 0.1 pad_add_fusion.parity
  0.7 2.0 %shard_map.119 = (f32[4,66,8,128]{3,2,1,0:T(8,128)S(1)}, f32[536,128]{1,0:T(8,128)S(1)}, f32[536,128]{1,0:T(8,128)S(1)}) custom-call(f32[62,8,128]{2,1,0:T(8,128)} %u.1, f32[62,8,128]{2,1,0:T(8,128)} %v.1, f32[62,8,128]{2,1,0:T(8,128)} %t.1, f32[62,8,128]{2,1,0:T(8,128)} %s.1, s32[8,128]{1,0:T(8,128)} %water.1, s32[8,128]{1,0:T(8,128)} %layers.1, ...), custom_call_target="tpu_custom_call" | custom-call | flops 1000000 | bytes 2031616 | tf_op jit(solution)/shard_map/pallas_call | solution.py:531
  2.7 21.9 %collective-permute-start = (f32[536,128]{1,0:T(8,128)S(1)}, f32[536,128]{1,0:T(8,128)S(1)}, u32[]{:S(2)}, u32[]{:S(2)}) collective-permute-start(f32[536,128]{1,0:T(8,128)S(1)} %get-tuple-element.18.own_lon.own_odd), channel_id=1, source_target_pairs={{0,1016},{8,16},{16,8},{24,32},{32,24},{40,48},{48,40},{56,64},{64... | collective-permute-start | bytes 823304 | tf_op jit(solution)/shard_map/ppermute | solution.py:589
  24.7 1.9 %collective-permute-start.1 = (f32[536,128]{1,0:T(8,128)S(1)}, f32[536,128]{1,0:T(8,128)S(1)}, u32[]{:S(2)}, u32[]{:S(2)}) collective-permute-start(f32[536,128]{1,0:T(8,128)S(1)} %get-tuple-element.21.own_even), channel_id=1, source_target_pairs={{0,8},{8,0},{16,24},{24,16},{32,40},{40,32},{48,56},{56,48},{64,72... | collective-permute-start | bytes 823304 | tf_op jit(solution)/shard_map/ppermute | solution.py:588
  26.6 1.2 %shard_map.120 = (f32[144,128]{1,0:T(8,128)S(1)}, f32[144,128]{1,0:T(8,128)S(1)}, f32[8,128]{1,0:T(8,128)S(1)}) custom-call(f32[4,66,8,128]{3,2,1,0:T(8,128)S(1)} %get-tuple-element.17.masked, f32[536,128]{1,0:T(8,128)S(1)} %get-tuple-element.18.own_lon.own_odd, s32[2]{0:T(128)S(1)} %pad_add_fusion.parity), custom_call_target="tpu_custom_call" | custom-call | flops 4000000 | bytes 1015808 | tf_op jit(solution)/shard_map/pallas_call | solution.py:546
  27.8 1.9 %collective-permute-start.2 = (f32[144,128]{1,0:T(8,128)S(1)}, f32[144,128]{1,0:T(8,128)S(1)}, u32[]{:S(2)}, u32[]{:S(2)}) collective-permute-start(f32[144,128]{1,0:T(8,128)S(1)} %get-tuple-element.19.own_odd_lat), channel_id=1, source_target_pairs={{1,2},{2,1},{3,4},{4,3},{5,6},{6,5},{9,10},{10,9},{11,12},{12,11},... | collective-permute-start | bytes 221192 | tf_op jit(solution)/shard_map/ppermute | solution.py:591
  29.8 4.7 %collective-permute-start.3 = (f32[144,128]{1,0:T(8,128)S(1)}, f32[144,128]{1,0:T(8,128)S(1)}, u32[]{:S(2)}, u32[]{:S(2)}) collective-permute-start(f32[144,128]{1,0:T(8,128)S(1)} %get-tuple-element.20.own_even_lat), channel_id=1, source_target_pairs={{0,1},{1,0},{2,3},{3,2},{4,5},{5,4},{6,7},{7,6},{8,9},{9,8},{10,11... | collective-permute-start | bytes 221192 | tf_op jit(solution)/shard_map/ppermute | solution.py:592
  34.5 0.0 collective-permute-done.2.odd_lat.got_odd_lat
  34.5 0.9 %collective-permute-done.3.even_lat.got_even_lat = f32[144,128]{1,0:T(8,128)S(1)} collective-permute-done((f32[144,128]{1,0:T(8,128)S(1)}, f32[144,128]{1,0:T(8,128)S(1)}, u32[]{:S(2)}, u32[]{:S(2)}) %collective-permute-start.3) | collective-permute-done | bytes 73760 | tf_op jit(solution)/shard_map/ppermute | solution.py:592
  35.4 0.0 collective-permute-done.odd_lon.got_odd
  35.4 0.0 collective-permute-done.1.even_lon.got_even
  35.4 0.8 %shard_map.122 = (f32[80,128]{1,0:T(8,128)S(1)}, f32[80,128]{1,0:T(8,128)S(1)}) custom-call(s32[2]{0:T(128)S(1)} %pad_add_fusion.parity, f32[536,128]{1,0:T(8,128)S(1)} %collective-permute-done.1.even_lon.got_even, f32[536,128]{1,0:T(8,128)S(1)} %collective-permute-done.odd_lon.got_odd, f32[536,128]{1,0:T(8,128)S(1)} %get-tuple-element.18.own_lon.own_odd, ...), custom_call_target="tpu_custom_call" | custom-call | flops 1000000 | bytes 1000000 | tf_op jit(solution)/shard_map/pallas_call | solution.py:553
  36.2 4.5 %collective-permute-start.4 = (f32[80,128]{1,0:T(8,128)S(1)}, f32[80,128]{1,0:T(8,128)S(1)}, u32[]{:S(2)}, u32[]{:S(2)}) collective-permute-start(f32[80,128]{1,0:T(8,128)S(1)} %get-tuple-element.27.own_b), channel_id=1, source_target_pairs={{0,1016},{8,16},{16,8},{24,32},{32,24},{40,48},{48,40},{56,64},{64... | collective-permute-start | bytes 122888 | tf_op jit(solution)/shard_map/ppermute | solution.py:598
  40.7 1.9 %collective-permute-start.5 = (f32[80,128]{1,0:T(8,128)S(1)}, f32[80,128]{1,0:T(8,128)S(1)}, u32[]{:S(2)}, u32[]{:S(2)}) collective-permute-start(f32[80,128]{1,0:T(8,128)S(1)} %get-tuple-element.28), channel_id=1, source_target_pairs={{0,8},{8,0},{16,24},{24,16},{32,40},{40,32},{48,56},{56,48},{64,72... | collective-permute-start | bytes 122888 | tf_op jit(solution)/shard_map/ppermute | solution.py:599
  42.6 3.3 %shard_map.121 = (f32[62,8,128]{2,1,0:T(8,128)}, f32[62,8,128]{2,1,0:T(8,128)}, f32[62,8,128]{2,1,0:T(8,128)}, f32[62,8,128]{2,1,0:T(8,128)}) custom-call(s32[2]{0:T(128)S(1)} %pad_add_fusion.parity, f32[4,66,8,128]{3,2,1,0:T(8,128)S(1)} %get-tuple-element.17.masked, f32[536,128]{1,0:T(8,128)S(1)} %get-tuple-element.18.own_lon.own_odd, ...), custom_call_target="tpu_custom_call" | custom-call | flops 10000000 | bytes 3047424 | tf_op jit(solution)/shard_map/pallas_call | solution.py:559
  45.9 0.4 collective-permute-done.4.odd_b
  46.3 0.3 collective-permute-done.5.even_b
  46.6 1.9 %shard_map.123 = f32[8,128]{1,0:T(8,128)} custom-call(s32[2]{0:T(128)S(1)} %pad_add_fusion.parity, f32[80,128]{1,0:T(8,128)S(1)} %collective-permute-done.4.odd_b, f32[80,128]{1,0:T(8,128)S(1)} %collective-permute-done.5.even_b, f32[80,128]{1,0:T(8,128)S(1)} %get-tuple-element.27.own_b, f32[536,128]{1,0:T(8,128)S(1)} %get-tuple-element.18.own_lon.own_odd, ...), custom_call_target="tpu_custom_call" | custom-call | flops 1000000 | bytes 1000000 | tf_op jit(solution)/shard_map/pallas_call | solution.py:572
Async XLA Ops:
  2.7 32.7 %collective-permute-start = (f32[536,128]{1,0:T(8,128)S(1)}, f32[536,128]{1,0:T(8,128)S(1)}, u32[]{:S(2)}, u32[]{:S(2)}) collective-permute-start(f32[536,128]{1,0:T(8,128)S(1)} %get-tuple-element.18.own_lon.own_odd), channel_id=1, source_target_pairs={{0,1016},{8,16},{16,8},{24,32},{32,24},{40,48},{48,40},{56,64},{64... | collective-permute-start | bytes 823304 | tf_op jit(solution)/shard_map/ppermute | solution.py:589
  24.7 10.7 %collective-permute-start.1 = (f32[536,128]{1,0:T(8,128)S(1)}, f32[536,128]{1,0:T(8,128)S(1)}, u32[]{:S(2)}, u32[]{:S(2)}) collective-permute-start(f32[536,128]{1,0:T(8,128)S(1)} %get-tuple-element.21.own_even), channel_id=1, source_target_pairs={{0,8},{8,0},{16,24},{24,16},{32,40},{40,32},{48,56},{56,48},{64,72... | collective-permute-start | bytes 823304 | tf_op jit(solution)/shard_map/ppermute | solution.py:588
  27.8 6.7 %collective-permute-start.2 = (f32[144,128]{1,0:T(8,128)S(1)}, f32[144,128]{1,0:T(8,128)S(1)}, u32[]{:S(2)}, u32[]{:S(2)}) collective-permute-start(f32[144,128]{1,0:T(8,128)S(1)} %get-tuple-element.19.own_odd_lat), channel_id=1, source_target_pairs={{1,2},{2,1},{3,4},{4,3},{5,6},{6,5},{9,10},{10,9},{11,12},{12,11},... | collective-permute-start | bytes 221192 | tf_op jit(solution)/shard_map/ppermute | solution.py:591
  29.8 5.6 %collective-permute-start.3 = (f32[144,128]{1,0:T(8,128)S(1)}, f32[144,128]{1,0:T(8,128)S(1)}, u32[]{:S(2)}, u32[]{:S(2)}) collective-permute-start(f32[144,128]{1,0:T(8,128)S(1)} %get-tuple-element.20.own_even_lat), channel_id=1, source_target_pairs={{0,1},{1,0},{2,3},{3,2},{4,5},{5,4},{6,7},{7,6},{8,9},{9,8},{10,11... | collective-permute-start | bytes 221192 | tf_op jit(solution)/shard_map/ppermute | solution.py:592
  36.2 10.1 %collective-permute-start.4 = (f32[80,128]{1,0:T(8,128)S(1)}, f32[80,128]{1,0:T(8,128)S(1)}, u32[]{:S(2)}, u32[]{:S(2)}) collective-permute-start(f32[80,128]{1,0:T(8,128)S(1)} %get-tuple-element.27.own_b), channel_id=1, source_target_pairs={{0,1016},{8,16},{16,8},{24,32},{32,24},{40,48},{48,40},{56,64},{64... | collective-permute-start | bytes 122888 | tf_op jit(solution)/shard_map/ppermute | solution.py:598
  40.7 5.9 %collective-permute-start.5 = (f32[80,128]{1,0:T(8,128)S(1)}, f32[80,128]{1,0:T(8,128)S(1)}, u32[]{:S(2)}, u32[]{:S(2)}) collective-permute-start(f32[80,128]{1,0:T(8,128)S(1)} %get-tuple-element.28), channel_id=1, source_target_pairs={{0,8},{8,0},{16,24},{24,16},{32,40},{40,32},{48,56},{56,48},{64,72... | collective-permute-start | bytes 122888 | tf_op jit(solution)/shard_map/ppermute | solution.py:599

commit v6 on v5

--- a/solution.py
+++ b/solution.py
@@ -54,7 +54,7 @@
 
 
 def pack_lon(
-    u, v, t, s, water, layers, diag, elev, parity, masked, up_first, low_first, held, held_int, held_flat, sems
+    u, v, t, s, water, layers, diag, elev, after, parity, masked, up_first, low_first, held, held_int, held_flat, sems
 ):
     copies = [
         pltpu.make_async_copy(src, held.at[i], sems.at[i]) for i, src in enumerate((u, v, t, s))
@@ -123,11 +123,11 @@
     return jnp.dot(jnp.concatenate([high, rest], axis=1), matrix, preferred_element_type=F32)
 
 
-def pack_lat(masked, own_lon, parity, odd_out, even_out, partial):
+def lat_packs(masked, flat, parity, odd_out, even_out, partial):
     row, lane = rows_of(), lanes_of()
     high, low = lane >> 4, ((lane - 8) & 127) >> 4
     in_even = (lane & 8) == 0
-    elev, diag, depth = flat_of(own_lon)
+    elev, diag, depth = flat
     levels = depth.astype(jnp.int32)
     is_even = parity[1] == 0
     zero = jnp.zeros((ROWS, LANES), F32)
@@ -184,6 +184,50 @@
     even_out[128:136, :] = jnp.where(is_even, right, left)
 
 
+def pack_lat_early(
+    u, v, t, s, water, layers, diag, elev, parity, odd_out, even_out, partial, masked, held, held_int, held_flat, sems
+):
+    @pl.when(parity[2] == 1)
+    def _():
+        copies = [
+            pltpu.make_async_copy(src, dst, sems.at[i])
+            for i, (src, dst) in enumerate(
+                [(x, held.at[f]) for f, x in enumerate((u, v, t, s))]
+                + [(water, held_int.at[0]), (layers, held_int.at[1])]
+                + [(elev, held_flat.at[0]), (diag, held_flat.at[1])]
+            )
+        ]
+        for copy in copies:
+            copy.start()
+        for copy in copies:
+            copy.wait()
+        depth = held_int[0] * held_int[1]
+        for f in range(4):
+            for i in (0, LEVELS + 1, LEVELS + 2, LEVELS + 3):
+                masked[f, i] = jnp.zeros((ROWS, LANES), F32)
+
+        def body(k, carry):
+            for f in range(4):
+                masked[f, k + 1] = jnp.where(k < depth, held[f, k], 0.0)
+            return carry
+
+        lax.fori_loop(0, LEVELS, body, 0)
+        flat = (held_flat[0], held_flat[1], depth.astype(F32))
+        lat_packs(masked, flat, parity, odd_out, even_out, partial)
+
+
+def pack_lat_late(masked, own_lon, odd, even, before, parity, odd_out, even_out, partial):
+    @pl.when(parity[2] == 1)
+    def _():
+        odd_out[...] = odd[...]
+        even_out[...] = even[...]
+        partial[...] = before[...]
+
+    @pl.when(parity[2] == 0)
+    def _():
+        lat_packs(masked, flat_of(own_lon), parity, odd_out, even_out, partial)
+
+
 def tile_lanes(x):
     return sum_slots(jnp.where(lanes_of() < 8, x, 0.0))
 
@@ -531,7 +575,7 @@
     return call(
         pack_lon,
         (shaped(4, LEVELS + 4, ROWS, LANES), shaped(LON_ROWS, LANES), shaped(LON_ROWS, LANES)),
-        [HERE] * 8 + [SMEM], 10**6, 2 * BLOCK,
+        [HERE] * 8 + [pl.BlockSpec(memory_space=pl.ANY), SMEM], 10**6, 2 * BLOCK,
         out_specs=(WHOLE,) * 3,
         scratch_shapes=[
             pltpu.VMEM((4, LEVELS, ROWS, LANES), F32),
@@ -542,11 +586,24 @@
     )(*args)
 
 
-def call_pack_lat(*args):
+LAT_OUT = (shaped(LAT_ROWS, LANES), shaped(LAT_ROWS, LANES), shaped(ROWS, LANES))
+
+
+def call_pack_lat_early(*args):
     return call(
-        pack_lat, (shaped(LAT_ROWS, LANES), shaped(LAT_ROWS, LANES), shaped(ROWS, LANES)),
-        [WHOLE] * 2 + [SMEM], 4 * 10**6, BLOCK,
+        pack_lat_early, LAT_OUT, [HERE] * 8 + [SMEM], 4 * 10**6, BLOCK,
+        scratch_shapes=[
+            pltpu.VMEM((4, LEVELS + 4, ROWS, LANES), F32),
+            pltpu.VMEM((4, LEVELS, ROWS, LANES), F32),
+            pltpu.VMEM((2, ROWS, LANES), jnp.int32),
+            pltpu.VMEM((2, ROWS, LANES), F32),
+            pltpu.SemaphoreType.DMA((8,)),
+        ],
     )(*args)
+
+
+def call_pack_lat_late(*args):
+    return call(pack_lat_late, LAT_OUT, [WHOLE] * 5 + [SMEM], 4 * 10**6, BLOCK)(*args)
 
 
 def call_forcing(*args):
@@ -572,24 +629,37 @@
     return call(solve, shaped(ROWS, LANES), [SMEM] + [WHOLE] * 8, 10**6, 10**6)(*args)
 
 
+RUN, EARLY = 8, 4
+
+
 def on_device(u, v, t, s, water, layers, diag, elev):
     lon, lat = lax.axis_size("lon"), lax.axis_size("lat")
     lon_even = [(i, i ^ 1) for i in range(lon)]
     lon_odd = [(i, (((i + 1) ^ 1) - 1) % lon) for i in range(lon)]
     lat_even = [(i, i ^ 1) for i in range(lat)]
     lat_odd = [(i, ((i + 1) ^ 1) - 1) for i in range(1, lat - 1)]
-    parity = jnp.stack([lax.axis_index("lon") & 1, lax.axis_index("lat") & 1]).astype(jnp.int32)
+
+    def odd_of(early):
+        rows = [i for i in range(lon) if (i % RUN < EARLY) == early]
+        return [(i * lat + a, i * lat + b) for i in rows for a, b in lat_odd]
+
+    at = lax.axis_index("lon")
+    parity = jnp.stack([at & 1, lax.axis_index("lat") & 1, at % RUN < EARLY]).astype(jnp.int32)
 
     raw = [
         pltpu.with_memory_space_constraint(x, pltpu.HBM)
         for x in (u, v, t, s, water, layers, diag, elev)
     ]
-    masked, own_odd, own_even = call_pack_lon(*raw, parity)
+    first_odd, first_even, first_partial = call_pack_lat_early(*raw, parity)
+    lat_early = lax.ppermute(first_odd, ("lon", "lat"), odd_of(True))
+    masked, own_odd, own_even = call_pack_lon(*raw, lat_early, parity)
     got_even = lax.ppermute(own_even, "lon", lon_even)
     got_odd = lax.ppermute(own_odd, "lon", lon_odd)
-    lat_own_odd, lat_own_even, partial = call_pack_lat(masked, own_odd, parity)
-    lat_got_odd = lax.ppermute(lat_own_odd, "lat", lat_odd)
+    lat_own_odd, lat_own_even, partial = call_pack_lat_late(
+        masked, own_odd, first_odd, first_even, first_partial, parity
+    )
     lat_got_even = lax.ppermute(lat_own_even, "lat", lat_even)
+    lat_got_odd = lat_early + lax.ppermute(lat_own_odd, ("lon", "lat"), odd_of(False))
 
     b_odd, b_even = call_forcing(
         parity, got_even, got_odd, own_odd, own_even,

time: 48.8 us -> 49.3 us (1.010)
  starting transfers between devices: 36.9 us -> 26.3 us
  waiting for transfers between devices: 1.55 us -> 10.3 us
  Pallas kernels: 9.19 us -> 11.5 us
    ppermute x1, starting transfers between devices: 21.9 us -> 13.4 us  [on_device(): got_odd = lax.ppermute(own_odd, 'lon', lon_odd)]
    ppermute x1 -> x2, waiting for transfers between devices: 0.01 us -> 4.89 us  [the longest x1 4.89 us: on_device(): lat_early = lax.ppermute(first_odd, ('lon', 'lat'), odd_of(True))]
    ppermute x1, waiting for transfers between devices: 0.01 us -> 3.37 us  [on_device(): got_even = lax.ppermute(own_even, 'lon', lon_even)]
    ppermute x1, starting transfers between devices: 4.74 us -> 1.92 us  [on_device(): lat_got_even = lax.ppermute(lat_own_even, 'lat', lat_even)]
    pallas_call x1 -> x2, Pallas kernels: 1.22 us -> 3.57 us  [the longest x1 3 us: call_pack_lat_early(): call(pack_lat_early, LAT_OUT, [HERE] * 8 + [SMEM], 4 * 10 ** 6, BLOCK, sc...]
    ppermute x1 -> x2, starting transfers between devices: 1.92 us -> 2.59 us  [the longest x1 1.92 us: on_device(): lat_early = lax.ppermute(first_odd, ('lon', 'lat'), odd_of(True))]
  transfers between devices with their start and end apart: 6 -> 7, of which waited for: 3 -> 6; matrix products, arithmetic and copies ran while one was open for 0% -> 0% of each run, Pallas kernels for 9% -> 8%
where the time goes in v6:
time: 49.3 us; the launch traced here: 49 us
  starting transfers between devices  26.3 us (53%)
  Pallas kernels  11.5 us (23%)
  waiting for transfers between devices  10.3 us (21%)
  between operations  0.75 us (2%)
    ppermute x1, starting transfers between devices, on_device(): got_odd = lax.ppermute(own_odd, 'lon', lon_odd)  13.4 us
    ppermute x1, waiting for transfers between devices, on_device(): lat_early = lax.ppermute(first_odd, ('lon', 'lat'), odd_of(True))  4.89 us
    ppermute x1, starting transfers between devices, on_device(): b_got_odd = lax.ppermute(b_odd, 'lon', lon_odd)  4.5 us
    ppermute x1, waiting for transfers between devices, on_device(): got_even = lax.ppermute(own_even, 'lon', lon_even)  3.37 us
    pallas_call x1, Pallas kernels, call_fields(): call(fields, (shaped(LEVELS, ROWS, LANES),) * 4, [SMEM] + [WHOLE] * 8, 10...  3.3 us
    pallas_call x1, Pallas kernels, call_pack_lat_early(): call(pack_lat_early, LAT_OUT, [HERE] * 8 + [SMEM], 4 * 10 ** 6, BLOCK, sc...  3 us
    pallas_call x1, Pallas kernels, call_pack_lon(): call(pack_lon, (shaped(4, LEVELS + 4, ROWS, LANES), shaped(LON_ROWS, LANE...  2.01 us
    ppermute x1, starting transfers between devices, on_device(): lat_got_even = lax.ppermute(lat_own_even, 'lat', lat_even)  1.92 us
  transfers between devices with their start and end apart: 7, of which 6 were waited for; matrix products, arithmetic and copies ran while one was open for 0% of the time, Pallas kernels for 8%

profile of v6, /device:TPU:4, one launch (start us, length us, event | category | flops | bytes accessed | tf_op | source)
XLA Modules:
  0.0 49.0 jit_solution(4640811804844905529)
XLA Ops:
  0.6 0.1 pad_add_fusion.parity
  0.7 3.0 %shard_map.119 = (f32[144,128]{1,0:T(8,128)S(1)}, f32[144,128]{1,0:T(8,128)S(1)}, f32[8,128]{1,0:T(8,128)S(1)}) custom-call(f32[62,8,128]{2,1,0:T(8,128)} %u.3, f32[62,8,128]{2,1,0:T(8,128)} %v.3, f32[62,8,128]{2,1,0:T(8,128)} %t.3, f32[62,8,128]{2,1,0:T(8,128)} %s.3, s32[8,128]{1,0:T(8,128)} %water.3, s32[8,128]{1,0:T(8,128)} %layers.3, f32[8,128]{1,0:T(8,128)} %diag.3, ...), custom_call_target="tpu_custom_call" | custom-call | flops 4000000 | bytes 1015808 | tf_op jit(solution)/shard_map/pallas_call | solution.py:593
  3.7 1.9 %collective-permute-start = (f32[144,128]{1,0:T(8,128)S(1)}, f32[144,128]{1,0:T(8,128)S(1)}, u32[]{:S(2)}, u32[]{:S(2)}) collective-permute-start(f32[144,128]{1,0:T(8,128)S(1)} %get-tuple-element.20.odd), channel_id=1, source_target_pairs={{1,2},{2,1},{3,4},{4,3},{5,6},{6,5},{9,10},{10,9},{11,12},{12,11},... | collective-permute-start | bytes 221192 | tf_op jit(solution)/shard_map/ppermute | solution.py:654
  5.7 4.9 %collective-permute-done.after = f32[144,128]{1,0:T(8,128)S(1)} collective-permute-done((f32[144,128]{1,0:T(8,128)S(1)}, f32[144,128]{1,0:T(8,128)S(1)}, u32[]{:S(2)}, u32[]{:S(2)}) %collective-permute-start) | collective-permute-done | bytes 73760 | tf_op jit(solution)/shard_map/ppermute | solution.py:654
  10.6 2.0 %shard_map.120 = (f32[4,66,8,128]{3,2,1,0:T(8,128)S(1)}, f32[536,128]{1,0:T(8,128)S(1)}, f32[536,128]{1,0:T(8,128)S(1)}) custom-call(f32[62,8,128]{2,1,0:T(8,128)} %u.3, f32[62,8,128]{2,1,0:T(8,128)} %v.3, f32[62,8,128]{2,1,0:T(8,128)} %t.3, f32[62,8,128]{2,1,0:T(8,128)} %s.3, s32[8,128]{1,0:T(8,128)} %water.3, s32[8,128]{1,0:T(8,128)} %layers.3, ...), custom_call_target="tpu_custom_call" | custom-call | flops 1000000 | bytes 2031616 | tf_op jit(solution)/shard_map/pallas_call | solution.py:575
  12.6 13.4 %collective-permute-start.1 = (f32[536,128]{1,0:T(8,128)S(1)}, f32[536,128]{1,0:T(8,128)S(1)}, u32[]{:S(2)}, u32[]{:S(2)}) collective-permute-start(f32[536,128]{1,0:T(8,128)S(1)} %get-tuple-element.22.own_lon.own_odd), channel_id=1, source_target_pairs={{0,1016},{8,16},{16,8},{24,32},{32,24},{40,48},{48,40},{56,64},{64... | collective-permute-start | bytes 823304 | tf_op jit(solution)/shard_map/ppermute | solution.py:657
  26.0 1.9 %collective-permute-start.2 = (f32[536,128]{1,0:T(8,128)S(1)}, f32[536,128]{1,0:T(8,128)S(1)}, u32[]{:S(2)}, u32[]{:S(2)}) collective-permute-start(f32[536,128]{1,0:T(8,128)S(1)} %get-tuple-element.27.own_even), channel_id=1, source_target_pairs={{0,8},{8,0},{16,24},{24,16},{32,40},{40,32},{48,56},{56,48},{64,72... | collective-permute-start | bytes 823304 | tf_op jit(solution)/shard_map/ppermute | solution.py:656
  27.9 0.6 %shard_map.121 = (f32[144,128]{1,0:T(8,128)S(1)}, f32[144,128]{1,0:T(8,128)S(1)}, f32[8,128]{1,0:T(8,128)S(1)}) custom-call(f32[4,66,8,128]{3,2,1,0:T(8,128)S(1)} %get-tuple-element.21.masked, f32[536,128]{1,0:T(8,128)S(1)} %get-tuple-element.22.own_lon.own_odd, f32[144,128]{1,0:T(8,128)S(1)} %get-tuple-element.20.odd, ...), custom_call_target="tpu_custom_call" | custom-call | flops 4000000 | bytes 1015808 | tf_op jit(solution)/shard_map/pallas_call | solution.py:606
  28.5 0.7 %collective-permute-start.3 = (f32[144,128]{1,0:T(8,128)S(1)}, f32[144,128]{1,0:T(8,128)S(1)}, u32[]{:S(2)}, u32[]{:S(2)}) collective-permute-start(f32[144,128]{1,0:T(8,128)S(1)} %get-tuple-element.25.own_odd_lat), channel_id=1, source_target_pairs={{33,34},{34,33},{35,36},{36,35},{37,38},{38,37},{41,42},{42,41},{4... | collective-permute-start | bytes 221192 | tf_op jit(solution)/shard_map/ppermute | solution.py:662
  29.2 1.9 %collective-permute-start.4 = (f32[144,128]{1,0:T(8,128)S(1)}, f32[144,128]{1,0:T(8,128)S(1)}, u32[]{:S(2)}, u32[]{:S(2)}) collective-permute-start(f32[144,128]{1,0:T(8,128)S(1)} %get-tuple-element.26.own_even_lat), channel_id=1, source_target_pairs={{0,1},{1,0},{2,3},{3,2},{4,5},{5,4},{6,7},{7,6},{8,9},{9,8},{10,11... | collective-permute-start | bytes 221192 | tf_op jit(solution)/shard_map/ppermute | solution.py:661
  31.1 0.0 collective-permute-done.3
  31.1 1.2 %collective-permute-done.4.even_lat.got_even_lat = f32[144,128]{1,0:T(8,128)S(1)} collective-permute-done((f32[144,128]{1,0:T(8,128)S(1)}, f32[144,128]{1,0:T(8,128)S(1)}, u32[]{:S(2)}, u32[]{:S(2)}) %collective-permute-start.4) | collective-permute-done | bytes 73760 | tf_op jit(solution)/shard_map/ppermute | solution.py:661
  32.3 0.2 collective-permute-done.1.odd_lon.got_odd
  32.6 3.4 %collective-permute-done.2.even_lon.got_even = f32[536,128]{1,0:T(8,128)S(1)} collective-permute-done((f32[536,128]{1,0:T(8,128)S(1)}, f32[536,128]{1,0:T(8,128)S(1)}, u32[]{:S(2)}, u32[]{:S(2)}) %collective-permute-start.2) | collective-permute-done | bytes 274464 | tf_op jit(solution)/shard_map/ppermute | solution.py:656
  35.9 0.8 %shard_map.123 = (f32[80,128]{1,0:T(8,128)S(1)}, f32[80,128]{1,0:T(8,128)S(1)}) custom-call(s32[3]{0:T(128)S(1)} %pad_add_fusion.parity, f32[536,128]{1,0:T(8,128)S(1)} %collective-permute-done.2.even_lon.got_even, f32[536,128]{1,0:T(8,128)S(1)} %collective-permute-done.1.odd_lon.got_odd, f32[536,128]{1,0:T(8,128)S(1)} %get-tuple-element.22.own_lon.own_odd, ...), custom_call_target="tpu_custom_call" | custom-call | flops 1000000 | bytes 1000000 | tf_op jit(solution)/shard_map/pallas_call | solution.py:610
  36.7 4.5 %collective-permute-start.5 = (f32[80,128]{1,0:T(8,128)S(1)}, f32[80,128]{1,0:T(8,128)S(1)}, u32[]{:S(2)}, u32[]{:S(2)}) collective-permute-start(f32[80,128]{1,0:T(8,128)S(1)} %get-tuple-element.33.own_b), channel_id=1, source_target_pairs={{0,1016},{8,16},{16,8},{24,32},{32,24},{40,48},{48,40},{56,64},{64... | collective-permute-start | bytes 122888 | tf_op jit(solution)/shard_map/ppermute | solution.py:668
  41.2 1.9 %collective-permute-start.6 = (f32[80,128]{1,0:T(8,128)S(1)}, f32[80,128]{1,0:T(8,128)S(1)}, u32[]{:S(2)}, u32[]{:S(2)}) collective-permute-start(f32[80,128]{1,0:T(8,128)S(1)} %get-tuple-element.34), channel_id=1, source_target_pairs={{0,8},{8,0},{16,24},{24,16},{32,40},{40,32},{48,56},{56,48},{64,72... | collective-permute-start | bytes 122888 | tf_op jit(solution)/shard_map/ppermute | solution.py:669
  43.2 3.3 %shard_map.122 = (f32[62,8,128]{2,1,0:T(8,128)}, f32[62,8,128]{2,1,0:T(8,128)}, f32[62,8,128]{2,1,0:T(8,128)}, f32[62,8,128]{2,1,0:T(8,128)}) custom-call(s32[3]{0:T(128)S(1)} %pad_add_fusion.parity, f32[4,66,8,128]{3,2,1,0:T(8,128)S(1)} %get-tuple-element.21.masked, f32[536,128]{1,0:T(8,128)S(1)} %get-tuple-element.22.own_lon.own_odd, ...), custom_call_target="tpu_custom_call" | custom-call | flops 10000000 | bytes 3047424 | tf_op jit(solution)/shard_map/pallas_call | solution.py:616
  46.5 0.4 collective-permute-done.5.odd_b
  46.9 0.3 collective-permute-done.6.even_b
  47.1 1.9 %shard_map.124 = f32[8,128]{1,0:T(8,128)} custom-call(s32[3]{0:T(128)S(1)} %pad_add_fusion.parity, f32[80,128]{1,0:T(8,128)S(1)} %collective-permute-done.5.odd_b, f32[80,128]{1,0:T(8,128)S(1)} %collective-permute-done.6.even_b, f32[80,128]{1,0:T(8,128)S(1)} %get-tuple-element.33.own_b, f32[536,128]{1,0:T(8,128)S(1)} %get-tuple-element.22.own_lon.own_odd, ...), custom_call_target="tpu_custom_call" | custom-call | flops 1000000 | bytes 1000000 | tf_op jit(solution)/shard_map/pallas_call | solution.py:629
  (1 shorter events, 0.0 us)
Async XLA Ops:
  3.7 6.8 %collective-permute-start = (f32[144,128]{1,0:T(8,128)S(1)}, f32[144,128]{1,0:T(8,128)S(1)}, u32[]{:S(2)}, u32[]{:S(2)}) collective-permute-start(f32[144,128]{1,0:T(8,128)S(1)} %get-tuple-element.20.odd), channel_id=1, source_target_pairs={{1,2},{2,1},{3,4},{4,3},{5,6},{6,5},{9,10},{10,9},{11,12},{12,11},... | collective-permute-start | bytes 221192 | tf_op jit(solution)/shard_map/ppermute | solution.py:654
  12.6 20.0 %collective-permute-start.1 = (f32[536,128]{1,0:T(8,128)S(1)}, f32[536,128]{1,0:T(8,128)S(1)}, u32[]{:S(2)}, u32[]{:S(2)}) collective-permute-start(f32[536,128]{1,0:T(8,128)S(1)} %get-tuple-element.22.own_lon.own_odd), channel_id=1, source_target_pairs={{0,1016},{8,16},{16,8},{24,32},{32,24},{40,48},{48,40},{56,64},{64... | collective-permute-start | bytes 823304 | tf_op jit(solution)/shard_map/ppermute | solution.py:657
  26.0 9.9 %collective-permute-start.2 = (f32[536,128]{1,0:T(8,128)S(1)}, f32[536,128]{1,0:T(8,128)S(1)}, u32[]{:S(2)}, u32[]{:S(2)}) collective-permute-start(f32[536,128]{1,0:T(8,128)S(1)} %get-tuple-element.27.own_even), channel_id=1, source_target_pairs={{0,8},{8,0},{16,24},{24,16},{32,40},{40,32},{48,56},{56,48},{64,72... | collective-permute-start | bytes 823304 | tf_op jit(solution)/shard_map/ppermute | solution.py:656
  28.5 2.6 %collective-permute-start.3 = (f32[144,128]{1,0:T(8,128)S(1)}, f32[144,128]{1,0:T(8,128)S(1)}, u32[]{:S(2)}, u32[]{:S(2)}) collective-permute-start(f32[144,128]{1,0:T(8,128)S(1)} %get-tuple-element.25.own_odd_lat), channel_id=1, source_target_pairs={{33,34},{34,33},{35,36},{36,35},{37,38},{38,37},{41,42},{42,41},{4... | collective-permute-start | bytes 221192 | tf_op jit(solution)/shard_map/ppermute | solution.py:662
  29.2 3.2 %collective-permute-start.4 = (f32[144,128]{1,0:T(8,128)S(1)}, f32[144,128]{1,0:T(8,128)S(1)}, u32[]{:S(2)}, u32[]{:S(2)}) collective-permute-start(f32[144,128]{1,0:T(8,128)S(1)} %get-tuple-element.26.own_even_lat), channel_id=1, source_target_pairs={{0,1},{1,0},{2,3},{3,2},{4,5},{5,4},{6,7},{7,6},{8,9},{9,8},{10,11... | collective-permute-start | bytes 221192 | tf_op jit(solution)/shard_map/ppermute | solution.py:661
  36.7 10.1 %collective-permute-start.5 = (f32[80,128]{1,0:T(8,128)S(1)}, f32[80,128]{1,0:T(8,128)S(1)}, u32[]{:S(2)}, u32[]{:S(2)}) collective-permute-start(f32[80,128]{1,0:T(8,128)S(1)} %get-tuple-element.33.own_b), channel_id=1, source_target_pairs={{0,1016},{8,16},{16,8},{24,32},{32,24},{40,48},{48,40},{56,64},{64... | collective-permute-start | bytes 122888 | tf_op jit(solution)/shard_map/ppermute | solution.py:668
  41.2 5.9 %collective-permute-start.6 = (f32[80,128]{1,0:T(8,128)S(1)}, f32[80,128]{1,0:T(8,128)S(1)}, u32[]{:S(2)}, u32[]{:S(2)}) collective-permute-start(f32[80,128]{1,0:T(8,128)S(1)} %get-tuple-element.34), channel_id=1, source_target_pairs={{0,8},{8,0},{16,24},{24,16},{32,40},{40,32},{48,56},{56,48},{64,72... | collective-permute-start | bytes 122888 | tf_op jit(solution)/shard_map/ppermute | solution.py:669

commit v7 on v5

--- a/solution.py
+++ b/solution.py
@@ -14,7 +14,8 @@
 LANES = 128
 STRIP = 128
 FLAT = 4 * STRIP
-LON_ROWS = FLAT + 3 * ROWS
+TIED = FLAT + 3 * ROWS
+LON_ROWS = TIED + ROWS
 LAT_ROWS = 18 * ROWS
 SOLVE_ROWS = 5 * ROWS + 5 * ROWS
 VMEM = 12 * 1024 * 1024
@@ -101,6 +102,7 @@
         ref[FLAT : FLAT + 8, :] = held_flat[0]
         ref[FLAT + 8 : FLAT + 16, :] = held_flat[1]
         ref[FLAT + 16 : FLAT + 24, :] = depth.astype(F32)
+        ref[TIED:LON_ROWS, :] = jnp.zeros((ROWS, LANES), F32)
 
 
 BF16 = jnp.bfloat16
@@ -221,16 +223,26 @@
     return 0.1 * sum_slots(a_sum), 0.1 * sum_slots(b_sum)
 
 
+class Either:
+    def __init__(self, first, second):
+        self.refs = (first, second)
+
+    def __getitem__(self, at):
+        first, second = self.refs
+        return first[at] + second[at]
+
+
 def four(ref, base, flag, other):
     at = [slice(base + 8 * i, base + 8 * i + 8) for i in range(4)]
     return [jnp.where(flag, ref[x, :], other[x, :]) for x in at]
 
 
 def forcing(
-    parity, got_even, got_odd, own_odd, own_even,
+    parity, got_late, got_odd, got_early, own_odd, own_even,
     own_odd_lat, own_even_lat, got_odd_lat, got_even_lat, partial,
     odd_out, even_out,
 ):
+    got_even = Either(got_early, got_late)
     row, lane = rows_of(), lanes_of()
     lon_even, lat_even = parity[0] == 0, parity[1] == 0
     elev, diag, depth = flat_of(own_odd)
@@ -318,9 +330,10 @@
 
 
 def fields(
-    parity, masked, own_lon, own_odd_lat, own_even_lat, odd_lon, even_lon, odd_lat, even_lat,
+    parity, masked, own_lon, own_odd_lat, own_even_lat, late_lon, odd_lon, early_lon, odd_lat, even_lat,
     o1, o2, o3, o4, terms, rims, fresh, sems,
 ):
+    even_lon = Either(early_lon, late_lon)
     row, lane = rows_of(), lanes_of()
     levels = flat_of(own_lon)[2].astype(jnp.int32)
     lon_even, lat_even = parity[0] == 0, parity[1] == 0
@@ -405,8 +418,9 @@
 
 
 def solve(
-    parity, odd_b, even_b, own_b, own_lon, odd_lon, even_lon, odd_lat, even_lat, height
+    parity, odd_b, even_b, own_b, own_lon, late_lon, odd_lon, early_lon, odd_lat, even_lat, height
 ):
+    even_lon = Either(early_lon, late_lon)
     row, lane = rows_of(), lanes_of()
     lon_even, lat_even = parity[0] == 0, parity[1] == 0
     lower = [jnp.where(lon_even, odd_b[8 * i : 8 * i + 8, :], even_b[8 * i : 8 * i + 8, :]) for i in range(10)]
@@ -551,13 +565,13 @@
 
 def call_forcing(*args):
     return call(
-        forcing, (shaped(SOLVE_ROWS, LANES),) * 2, [SMEM] + [WHOLE] * 9, 10**6, 10**6
+        forcing, (shaped(SOLVE_ROWS, LANES),) * 2, [SMEM] + [WHOLE] * 10, 10**6, 10**6
     )(*args)
 
 
 def call_fields(*args):
     return call(
-        fields, (shaped(LEVELS, ROWS, LANES),) * 4, [SMEM] + [WHOLE] * 8, 10**7, 3 * BLOCK,
+        fields, (shaped(LEVELS, ROWS, LANES),) * 4, [SMEM] + [WHOLE] * 9, 10**7, 3 * BLOCK,
         out_specs=(HERE,) * 4,
         scratch_shapes=[
             pltpu.VMEM((4, LEVELS * ROWS, 2 * LANES), F32),
@@ -569,7 +583,10 @@
 
 
 def call_solve(*args):
-    return call(solve, shaped(ROWS, LANES), [SMEM] + [WHOLE] * 8, 10**6, 10**6)(*args)
+    return call(solve, shaped(ROWS, LANES), [SMEM] + [WHOLE] * 9, 10**6, 10**6)(*args)
+
+
+RUN, EARLY = 8, 2
 
 
 def on_device(u, v, t, s, water, layers, diag, elev):
@@ -578,6 +595,8 @@
     lon_odd = [(i, (((i + 1) ^ 1) - 1) % lon) for i in range(lon)]
     lat_even = [(i, i ^ 1) for i in range(lat)]
     lat_odd = [(i, ((i + 1) ^ 1) - 1) for i in range(1, lat - 1)]
+    early = [(a, b) for a, b in lon_even if a % RUN < EARLY]
+    late = [(a, b) for a, b in lon_even if a % RUN >= EARLY]
     parity = jnp.stack([lax.axis_index("lon") & 1, lax.axis_index("lat") & 1]).astype(jnp.int32)
 
     raw = [
@@ -585,24 +604,29 @@
         for x in (u, v, t, s, water, layers, diag, elev)
     ]
     masked, own_odd, own_even = call_pack_lon(*raw, parity)
-    got_even = lax.ppermute(own_even, "lon", lon_even)
+    got_early = lax.ppermute(own_even, "lon", early)
+    own_odd = own_odd.at[TIED:].set(got_early[TIED:])
+    own_even = own_even.at[TIED:].set(got_early[TIED:])
     got_odd = lax.ppermute(own_odd, "lon", lon_odd)
+    got_late = lax.ppermute(own_even, "lon", late)
     lat_own_odd, lat_own_even, partial = call_pack_lat(masked, own_odd, parity)
     lat_got_odd = lax.ppermute(lat_own_odd, "lat", lat_odd)
     lat_got_even = lax.ppermute(lat_own_even, "lat", lat_even)
 
     b_odd, b_even = call_forcing(
-        parity, got_even, got_odd, own_odd, own_even,
+        parity, got_late, got_odd, got_early, own_odd, own_even,
         lat_own_odd, lat_own_even, lat_got_odd, lat_got_even, partial,
     )
     b_got_odd = lax.ppermute(b_odd, "lon", lon_odd)
     b_got_even = lax.ppermute(b_even, "lon", lon_even)
 
     fresh = call_fields(
-        parity, masked, own_odd, lat_own_odd, lat_own_even, got_odd, got_even, lat_got_odd, lat_got_even
+        parity, masked, own_odd, lat_own_odd, lat_own_even, got_late, got_odd, got_early,
+        lat_got_odd, lat_got_even,
     )
     height = call_solve(
-        parity, b_got_odd, b_got_even, b_odd, own_odd, got_odd, got_even, lat_got_odd, lat_got_even
+        parity, b_got_odd, b_got_even, b_odd, own_odd, got_late, got_odd, got_early,
+        lat_got_odd, lat_got_even,
     )
     return (*fresh, height)
 

time: 48.8 us -> 50 us (1.025)
  the two profiles are of different devices: /device:TPU:4 before, /device:TPU:1 now
where the time goes in v7:
time: 50 us; the launch traced here: 49.7 us
  starting transfers between devices  34.5 us (69%)
  Pallas kernels  9.21 us (18%)
  waiting for transfers between devices  5.16 us (10%)
  between operations  0.73 us (1%)
    ppermute x1, starting transfers between devices, on_device(): got_odd = lax.ppermute(own_odd, 'lon', lon_odd)  13.5 us
    ppermute x1, starting transfers between devices, on_device(): b_got_odd = lax.ppermute(b_odd, 'lon', lon_odd)  5.83 us
    ppermute x1, starting transfers between devices, on_device(): got_early = lax.ppermute(own_even, 'lon', early)  5.74 us
    ppermute x1, starting transfers between devices, on_device(): lat_got_odd = lax.ppermute(lat_own_odd, 'lat', lat_odd)  4.88 us
    ppermute x1, waiting for transfers between devices, on_device(): got_early = lax.ppermute(own_even, 'lon', early)  3.92 us
    pallas_call x1, Pallas kernels, call_fields(): call(fields, (shaped(LEVELS, ROWS, LANES),) * 4, [SMEM] + [WHOLE] * 9, 10...  3.32 us
    pallas_call x1, Pallas kernels, call_pack_lon(): call(pack_lon, (shaped(4, LEVELS + 4, ROWS, LANES), shaped(LON_ROWS, LANE...  2.01 us
    ppermute x1, starting transfers between devices, on_device(): lat_got_even = lax.ppermute(lat_own_even, 'lat', lat_even)  1.92 us
  transfers between devices with their start and end apart: 7, of which 3 were waited for; matrix products, arithmetic and copies ran while one was open for 0% of the time, Pallas kernels for 9%

profile of v7, /device:TPU:1, one launch (start us, length us, event | category | flops | bytes accessed | tf_op | source)
XLA Modules:
  0.0 49.7 jit_solution(1122473044251232009)
XLA Ops:
  0.6 0.1 pad_add_fusion.parity
  0.7 2.0 %shard_map.119 = (f32[4,66,8,128]{3,2,1,0:T(8,128)S(1)}, f32[544,128]{1,0:T(8,128)S(1)}, f32[544,128]{1,0:T(8,128)S(1)}) custom-call(f32[62,8,128]{2,1,0:T(8,128)} %u.1, f32[62,8,128]{2,1,0:T(8,128)} %v.1, f32[62,8,128]{2,1,0:T(8,128)} %t.1, f32[62,8,128]{2,1,0:T(8,128)} %s.1, s32[8,128]{1,0:T(8,128)} %water.1, s32[8,128]{1,0:T(8,128)} %layers.1, ...), custom_call_target="tpu_custom_call" | custom-call | flops 1000000 | bytes 2031616 | tf_op jit(solution)/shard_map/pallas_call | solution.py:545
  2.7 5.7 %collective-permute-start = (f32[544,128]{1,0:T(8,128)S(1)}, f32[544,128]{1,0:T(8,128)S(1)}, u32[]{:S(2)}, u32[]{:S(2)}) collective-permute-start(f32[544,128]{1,0:T(8,128)S(1)} %get-tuple-element.43), channel_id=1, source_target_pairs={{0,8},{8,0},{64,72},{72,64},{128,136},{136,128},{192,200},{200,192... | collective-permute-start | bytes 835592 | tf_op jit(solution)/shard_map/ppermute | solution.py:607
  8.5 3.9 %collective-permute-done.early_lon.got_early = f32[544,128]{1,0:T(8,128)S(1)} collective-permute-done((f32[544,128]{1,0:T(8,128)S(1)}, f32[544,128]{1,0:T(8,128)S(1)}, u32[]{:S(2)}, u32[]{:S(2)}) %collective-permute-start) | collective-permute-done | bytes 278560 | tf_op jit(solution)/shard_map/ppermute | solution.py:607
  12.4 13.5 %collective-permute-start.2 = (f32[544,128]{1,0:T(8,128)S(1)}, f32[544,128]{1,0:T(8,128)S(1)}, u32[]{:S(2)}, u32[]{:S(2)}) collective-permute-start(f32[544,128]{1,0:T(8,128)S(1)} %get-tuple-element.54.own_lon.own_odd), channel_id=1, source_target_pairs={{0,1016},{8,16},{16,8},{24,32},{32,24},{40,48},{48,40},{56,64},{64... | collective-permute-start | bytes 835592 | tf_op jit(solution)/shard_map/ppermute | solution.py:610
  25.9 0.7 %collective-permute-start.1 = (f32[544,128]{1,0:T(8,128)S(1)}, f32[544,128]{1,0:T(8,128)S(1)}, u32[]{:S(2)}, u32[]{:S(2)}) collective-permute-start(f32[544,128]{1,0:T(8,128)S(1)} %get-tuple-element.53.own_even), channel_id=1, source_target_pairs={{16,24},{24,16},{32,40},{40,32},{48,56},{56,48},{80,88},{88,80},{9... | collective-permute-start | bytes 835592 | tf_op jit(solution)/shard_map/ppermute | solution.py:611
  26.6 1.2 %shard_map.120 = (f32[144,128]{1,0:T(8,128)S(1)}, f32[144,128]{1,0:T(8,128)S(1)}, f32[8,128]{1,0:T(8,128)S(1)}) custom-call(f32[4,66,8,128]{3,2,1,0:T(8,128)S(1)} %get-tuple-element.41.masked, f32[544,128]{1,0:T(8,128)S(1)} %get-tuple-element.54.own_lon.own_odd, s32[2]{0:T(128)S(1)} %pad_add_fusion.parity), custom_call_target="tpu_custom_call" | custom-call | flops 4000000 | bytes 1015808 | tf_op jit(solution)/shard_map/pallas_call | solution.py:560
  27.8 4.9 %collective-permute-start.3 = (f32[144,128]{1,0:T(8,128)S(1)}, f32[144,128]{1,0:T(8,128)S(1)}, u32[]{:S(2)}, u32[]{:S(2)}) collective-permute-start(f32[144,128]{1,0:T(8,128)S(1)} %get-tuple-element.44.own_odd_lat), channel_id=1, source_target_pairs={{1,2},{2,1},{3,4},{4,3},{5,6},{6,5},{9,10},{10,9},{11,12},{12,11},... | collective-permute-start | bytes 221192 | tf_op jit(solution)/shard_map/ppermute | solution.py:613
  32.7 1.9 %collective-permute-start.4 = (f32[144,128]{1,0:T(8,128)S(1)}, f32[144,128]{1,0:T(8,128)S(1)}, u32[]{:S(2)}, u32[]{:S(2)}) collective-permute-start(f32[144,128]{1,0:T(8,128)S(1)} %get-tuple-element.45.own_even_lat), channel_id=1, source_target_pairs={{0,1},{1,0},{2,3},{3,2},{4,5},{5,4},{6,7},{7,6},{8,9},{9,8},{10,11... | collective-permute-start | bytes 221192 | tf_op jit(solution)/shard_map/ppermute | solution.py:614
  34.7 0.4 collective-permute-done.3.odd_lat.got_odd_lat
  35.1 0.8 %collective-permute-done.4.even_lat.got_even_lat = f32[144,128]{1,0:T(8,128)S(1)} collective-permute-done((f32[144,128]{1,0:T(8,128)S(1)}, f32[144,128]{1,0:T(8,128)S(1)}, u32[]{:S(2)}, u32[]{:S(2)}) %collective-permute-start.4) | collective-permute-done | bytes 73760 | tf_op jit(solution)/shard_map/ppermute | solution.py:614
  35.9 0.0 collective-permute-done.2.odd_lon.got_odd
  35.9 0.0 collective-permute-done.1.late_lon.got_late
  35.9 0.8 %shard_map.122 = (f32[80,128]{1,0:T(8,128)S(1)}, f32[80,128]{1,0:T(8,128)S(1)}) custom-call(s32[2]{0:T(128)S(1)} %pad_add_fusion.parity, f32[544,128]{1,0:T(8,128)S(1)} %collective-permute-done.1.late_lon.got_late, f32[544,128]{1,0:T(8,128)S(1)} %collective-permute-done.2.odd_lon.got_odd, f32[544,128]{1,0:T(8,128)S(1)} %collective-permute-done.early_lon.got_early, ...), custom_call_target="tpu_custom_call" | custom-call | flops 1000000 | bytes 1000000 | tf_op jit(solution)/shard_map/pallas_call | solution.py:567
  36.7 5.8 %collective-permute-start.5 = (f32[80,128]{1,0:T(8,128)S(1)}, f32[80,128]{1,0:T(8,128)S(1)}, u32[]{:S(2)}, u32[]{:S(2)}) collective-permute-start(f32[80,128]{1,0:T(8,128)S(1)} %get-tuple-element.51.own_b), channel_id=1, source_target_pairs={{0,1016},{8,16},{16,8},{24,32},{32,24},{40,48},{48,40},{56,64},{64... | collective-permute-start | bytes 122888 | tf_op jit(solution)/shard_map/ppermute | solution.py:620
  42.6 1.9 %collective-permute-start.6 = (f32[80,128]{1,0:T(8,128)S(1)}, f32[80,128]{1,0:T(8,128)S(1)}, u32[]{:S(2)}, u32[]{:S(2)}) collective-permute-start(f32[80,128]{1,0:T(8,128)S(1)} %get-tuple-element.52), channel_id=1, source_target_pairs={{0,8},{8,0},{16,24},{24,16},{32,40},{40,32},{48,56},{56,48},{64,72... | collective-permute-start | bytes 122888 | tf_op jit(solution)/shard_map/ppermute | solution.py:621
  44.5 3.3 %shard_map.121 = (f32[62,8,128]{2,1,0:T(8,128)}, f32[62,8,128]{2,1,0:T(8,128)}, f32[62,8,128]{2,1,0:T(8,128)}, f32[62,8,128]{2,1,0:T(8,128)}) custom-call(s32[2]{0:T(128)S(1)} %pad_add_fusion.parity, f32[4,66,8,128]{3,2,1,0:T(8,128)S(1)} %get-tuple-element.41.masked, f32[544,128]{1,0:T(8,128)S(1)} %get-tuple-element.54.own_lon.own_odd, ...), custom_call_target="tpu_custom_call" | custom-call | flops 10000000 | bytes 3047424 | tf_op jit(solution)/shard_map/pallas_call | solution.py:573
  47.8 0.0 collective-permute-done.5.odd_b
  47.8 0.0 collective-permute-done.6.even_b
  47.8 1.9 %shard_map.123 = f32[8,128]{1,0:T(8,128)} custom-call(s32[2]{0:T(128)S(1)} %pad_add_fusion.parity, f32[80,128]{1,0:T(8,128)S(1)} %collective-permute-done.5.odd_b, f32[80,128]{1,0:T(8,128)S(1)} %collective-permute-done.6.even_b, f32[80,128]{1,0:T(8,128)S(1)} %get-tuple-element.51.own_b, f32[544,128]{1,0:T(8,128)S(1)} %get-tuple-element.54.own_lon.own_odd, ...), custom_call_target="tpu_custom_call" | custom-call | flops 1000000 | bytes 1000000 | tf_op jit(solution)/shard_map/pallas_call | solution.py:586
  (1 shorter events, 0.0 us)
Async XLA Ops:
  2.7 9.7 %collective-permute-start = (f32[544,128]{1,0:T(8,128)S(1)}, f32[544,128]{1,0:T(8,128)S(1)}, u32[]{:S(2)}, u32[]{:S(2)}) collective-permute-start(f32[544,128]{1,0:T(8,128)S(1)} %get-tuple-element.43), channel_id=1, source_target_pairs={{0,8},{8,0},{64,72},{72,64},{128,136},{136,128},{192,200},{200,192... | collective-permute-start | bytes 835592 | tf_op jit(solution)/shard_map/ppermute | solution.py:607
  12.4 23.5 %collective-permute-start.2 = (f32[544,128]{1,0:T(8,128)S(1)}, f32[544,128]{1,0:T(8,128)S(1)}, u32[]{:S(2)}, u32[]{:S(2)}) collective-permute-start(f32[544,128]{1,0:T(8,128)S(1)} %get-tuple-element.54.own_lon.own_odd), channel_id=1, source_target_pairs={{0,1016},{8,16},{16,8},{24,32},{32,24},{40,48},{48,40},{56,64},{64... | collective-permute-start | bytes 835592 | tf_op jit(solution)/shard_map/ppermute | solution.py:610
  25.9 10.0 %collective-permute-start.1 = (f32[544,128]{1,0:T(8,128)S(1)}, f32[544,128]{1,0:T(8,128)S(1)}, u32[]{:S(2)}, u32[]{:S(2)}) collective-permute-start(f32[544,128]{1,0:T(8,128)S(1)} %get-tuple-element.53.own_even), channel_id=1, source_target_pairs={{16,24},{24,16},{32,40},{40,32},{48,56},{56,48},{80,88},{88,80},{9... | collective-permute-start | bytes 835592 | tf_op jit(solution)/shard_map/ppermute | solution.py:611
  27.8 7.2 %collective-permute-start.3 = (f32[144,128]{1,0:T(8,128)S(1)}, f32[144,128]{1,0:T(8,128)S(1)}, u32[]{:S(2)}, u32[]{:S(2)}) collective-permute-start(f32[144,128]{1,0:T(8,128)S(1)} %get-tuple-element.44.own_odd_lat), channel_id=1, source_target_pairs={{1,2},{2,1},{3,4},{4,3},{5,6},{6,5},{9,10},{10,9},{11,12},{12,11},... | collective-permute-start | bytes 221192 | tf_op jit(solution)/shard_map/ppermute | solution.py:613
  32.7 3.2 %collective-permute-start.4 = (f32[144,128]{1,0:T(8,128)S(1)}, f32[144,128]{1,0:T(8,128)S(1)}, u32[]{:S(2)}, u32[]{:S(2)}) collective-permute-start(f32[144,128]{1,0:T(8,128)S(1)} %get-tuple-element.45.own_even_lat), channel_id=1, source_target_pairs={{0,1},{1,0},{2,3},{3,2},{4,5},{5,4},{6,7},{7,6},{8,9},{9,8},{10,11... | collective-permute-start | bytes 221192 | tf_op jit(solution)/shard_map/ppermute | solution.py:614
  36.7 11.1 %collective-permute-start.5 = (f32[80,128]{1,0:T(8,128)S(1)}, f32[80,128]{1,0:T(8,128)S(1)}, u32[]{:S(2)}, u32[]{:S(2)}) collective-permute-start(f32[80,128]{1,0:T(8,128)S(1)} %get-tuple-element.51.own_b), channel_id=1, source_target_pairs={{0,1016},{8,16},{16,8},{24,32},{32,24},{40,48},{48,40},{56,64},{64... | collective-permute-start | bytes 122888 | tf_op jit(solution)/shard_map/ppermute | solution.py:620
  42.6 5.3 %collective-permute-start.6 = (f32[80,128]{1,0:T(8,128)S(1)}, f32[80,128]{1,0:T(8,128)S(1)}, u32[]{:S(2)}, u32[]{:S(2)}) collective-permute-start(f32[80,128]{1,0:T(8,128)S(1)} %get-tuple-element.52), channel_id=1, source_target_pairs={{0,8},{8,0},{16,24},{24,16},{32,40},{40,32},{48,56},{56,48},{64,72... | collective-permute-start | bytes 122888 | tf_op jit(solution)/shard_map/ppermute | solution.py:621

commit v8 on v5

--- a/solution.py
+++ b/solution.py
@@ -521,7 +521,6 @@
     )
 
 
-SMEM = pl.BlockSpec(memory_space=pltpu.SMEM)
 WHOLE = pl.BlockSpec(memory_space=pltpu.VMEM)
 HERE = pl.BlockSpec(memory_space=pltpu.HBM)
 BLOCK = 4 * LEVELS * ROWS * LANES * 4
@@ -531,7 +530,7 @@
     return call(
         pack_lon,
         (shaped(4, LEVELS + 4, ROWS, LANES), shaped(LON_ROWS, LANES), shaped(LON_ROWS, LANES)),
-        [HERE] * 8 + [SMEM], 10**6, 2 * BLOCK,
+        [HERE] * 8 + [WHOLE], 10**6, 2 * BLOCK,
         out_specs=(WHOLE,) * 3,
         scratch_shapes=[
             pltpu.VMEM((4, LEVELS, ROWS, LANES), F32),
@@ -545,19 +544,19 @@
 def call_pack_lat(*args):
     return call(
         pack_lat, (shaped(LAT_ROWS, LANES), shaped(LAT_ROWS, LANES), shaped(ROWS, LANES)),
-        [WHOLE] * 2 + [SMEM], 4 * 10**6, BLOCK,
+        [WHOLE] * 2 + [WHOLE], 4 * 10**6, BLOCK,
     )(*args)
 
 
 def call_forcing(*args):
     return call(
-        forcing, (shaped(SOLVE_ROWS, LANES),) * 2, [SMEM] + [WHOLE] * 9, 10**6, 10**6
+        forcing, (shaped(SOLVE_ROWS, LANES),) * 2, [WHOLE] + [WHOLE] * 9, 10**6, 10**6
     )(*args)
 
 
 def call_fields(*args):
     return call(
-        fields, (shaped(LEVELS, ROWS, LANES),) * 4, [SMEM] + [WHOLE] * 8, 10**7, 3 * BLOCK,
+        fields, (shaped(LEVELS, ROWS, LANES),) * 4, [WHOLE] + [WHOLE] * 8, 10**7, 3 * BLOCK,
         out_specs=(HERE,) * 4,
         scratch_shapes=[
             pltpu.VMEM((4, LEVELS * ROWS, 2 * LANES), F32),
@@ -569,7 +568,7 @@
 
 
 def call_solve(*args):
-    return call(solve, shaped(ROWS, LANES), [SMEM] + [WHOLE] * 8, 10**6, 10**6)(*args)
+    return call(solve, shaped(ROWS, LANES), [WHOLE] + [WHOLE] * 8, 10**6, 10**6)(*args)
 
 
 def on_device(u, v, t, s, water, layers, diag, elev):
@@ -578,7 +577,8 @@
     lon_odd = [(i, (((i + 1) ^ 1) - 1) % lon) for i in range(lon)]
     lat_even = [(i, i ^ 1) for i in range(lat)]
     lat_odd = [(i, ((i + 1) ^ 1) - 1) for i in range(1, lat - 1)]
-    parity = jnp.stack([lax.axis_index("lon") & 1, lax.axis_index("lat") & 1]).astype(jnp.int32)
+    odd = jnp.stack([lax.axis_index("lon") & 1, lax.axis_index("lat") & 1]).astype(jnp.int32)
+    parity = jnp.broadcast_to(odd[:, None, None], (2, ROWS, LANES))
 
     raw = [
         pltpu.with_memory_space_constraint(x, pltpu.HBM)

time: 48.8 us -> 47.2 us (0.967)
  Pallas kernels: 9.19 us -> 6.52 us
  starting transfers between devices: 36.9 us -> 37.5 us
  waiting for transfers between devices: 1.55 us -> 2.06 us
    pallas_call x3, Pallas kernels: 5.96 us -> 4.37 us  [the longest x1 2.79 us: call_fields(): call(fields, (shaped(LEVELS, ROWS, LANES),) * 4, [WHOLE] + [WHOLE] * 8, 1...]
    pallas_call x1, Pallas kernels: 1.22 us -> 0.68 us  [call_pack_lat(): call(pack_lat, (shaped(LAT_ROWS, LANES), shaped(LAT_ROWS, LANES), shaped(...]
    pallas_call x1, Pallas kernels: 2.01 us -> 1.47 us  [call_pack_lon(): call(pack_lon, (shaped(4, LEVELS + 4, ROWS, LANES), shaped(LON_ROWS, LANE...]
    ppermute x1, waiting for transfers between devices: 0.27 us -> 0.81 us  [on_device(): b_got_even = lax.ppermute(b_even, 'lon', lon_even)]
    ppermute x1, starting transfers between devices: 4.48 us -> 5.02 us  [on_device(): b_got_odd = lax.ppermute(b_odd, 'lon', lon_odd)]
  transfers between devices with their start and end apart: 6 -> 6, of which waited for: 3 -> 3; matrix products, arithmetic and copies ran while one was open for 0% -> 0% of each run, Pallas kernels for 9% -> 7%
where the time goes in v8:
time: 47.2 us; the launch traced here: 46.9 us
  starting transfers between devices  37.5 us (79%)
  Pallas kernels  6.52 us (14%)
  waiting for transfers between devices  2.06 us (4%)
  between operations  0.72 us (2%)
    ppermute x1, starting transfers between devices, on_device(): got_odd = lax.ppermute(own_odd, 'lon', lon_odd)  21.9 us
    ppermute x1, starting transfers between devices, on_device(): b_got_odd = lax.ppermute(b_odd, 'lon', lon_odd)  5.02 us
    ppermute x1, starting transfers between devices, on_device(): lat_got_even = lax.ppermute(lat_own_even, 'lat', lat_even)  4.75 us
    pallas_call x1, Pallas kernels, call_fields(): call(fields, (shaped(LEVELS, ROWS, LANES),) * 4, [WHOLE] + [WHOLE] * 8, 1...  2.79 us
    ppermute x1, starting transfers between devices, on_device(): got_even = lax.ppermute(own_even, 'lon', lon_even)  1.92 us
    ppermute x1, starting transfers between devices, on_device(): lat_got_odd = lax.ppermute(lat_own_odd, 'lat', lat_odd)  1.92 us
    ppermute x1, starting transfers between devices, on_device(): b_got_even = lax.ppermute(b_even, 'lon', lon_even)  1.92 us
    pallas_call x1, Pallas kernels, call_pack_lon(): call(pack_lon, (shaped(4, LEVELS + 4, ROWS, LANES), shaped(LON_ROWS, LANE...  1.47 us
  transfers between devices with their start and end apart: 6, of which 3 were waited for; matrix products, arithmetic and copies ran while one was open for 0% of the time, Pallas kernels for 7%

profile of v8, /device:TPU:4, one launch (start us, length us, event | category | flops | bytes accessed | tf_op | source)
XLA Modules:
  0.0 46.9 jit_solution(14302131534590689572)
XLA Ops:
  0.6 0.1 pad_add_fusion
  0.7 0.1 broadcast_in_dim.2.parity
  0.8 1.5 %shard_map.119 = (f32[4,66,8,128]{3,2,1,0:T(8,128)S(1)}, f32[536,128]{1,0:T(8,128)S(1)}, f32[536,128]{1,0:T(8,128)S(1)}) custom-call(f32[62,8,128]{2,1,0:T(8,128)} %u.1, f32[62,8,128]{2,1,0:T(8,128)} %v.1, f32[62,8,128]{2,1,0:T(8,128)} %t.1, f32[62,8,128]{2,1,0:T(8,128)} %s.1, s32[8,128]{1,0:T(8,128)} %water.1, s32[8,128]{1,0:T(8,128)} %layers.1, ...), custom_call_target="tpu_custom_call" | custom-call | flops 1000000 | bytes 2031616 | tf_op jit(solution)/shard_map/pallas_call | solution.py:530
  2.3 21.9 %collective-permute-start = (f32[536,128]{1,0:T(8,128)S(1)}, f32[536,128]{1,0:T(8,128)S(1)}, u32[]{:S(2)}, u32[]{:S(2)}) collective-permute-start(f32[536,128]{1,0:T(8,128)S(1)} %get-tuple-element.18.own_lon.own_odd), channel_id=1, source_target_pairs={{0,1016},{8,16},{16,8},{24,32},{32,24},{40,48},{48,40},{56,64},{64... | collective-permute-start | bytes 823304 | tf_op jit(solution)/shard_map/ppermute | solution.py:589
  24.2 1.9 %collective-permute-start.1 = (f32[536,128]{1,0:T(8,128)S(1)}, f32[536,128]{1,0:T(8,128)S(1)}, u32[]{:S(2)}, u32[]{:S(2)}) collective-permute-start(f32[536,128]{1,0:T(8,128)S(1)} %get-tuple-element.21.own_even), channel_id=1, source_target_pairs={{0,8},{8,0},{16,24},{24,16},{32,40},{40,32},{48,56},{56,48},{64,72... | collective-permute-start | bytes 823304 | tf_op jit(solution)/shard_map/ppermute | solution.py:588
  26.1 0.7 %shard_map.120 = (f32[144,128]{1,0:T(8,128)S(1)}, f32[144,128]{1,0:T(8,128)S(1)}, f32[8,128]{1,0:T(8,128)S(1)}) custom-call(f32[4,66,8,128]{3,2,1,0:T(8,128)S(1)} %get-tuple-element.17.masked, f32[536,128]{1,0:T(8,128)S(1)} %get-tuple-element.18.own_lon.own_odd, s32[2,8,128]{2,1,0:T(8,128)S(1)} %broadcast_in_dim.2.parity), custom_call_target="tpu_custom_call" | custom-call | flops 4000000 | bytes 1015808 | tf_op jit(solution)/shard_map/pallas_call | solution.py:545
  26.8 1.9 %collective-permute-start.2 = (f32[144,128]{1,0:T(8,128)S(1)}, f32[144,128]{1,0:T(8,128)S(1)}, u32[]{:S(2)}, u32[]{:S(2)}) collective-permute-start(f32[144,128]{1,0:T(8,128)S(1)} %get-tuple-element.19.own_odd_lat), channel_id=1, source_target_pairs={{1,2},{2,1},{3,4},{4,3},{5,6},{6,5},{9,10},{10,9},{11,12},{12,11},... | collective-permute-start | bytes 221192 | tf_op jit(solution)/shard_map/ppermute | solution.py:591
  28.8 4.7 %collective-permute-start.3 = (f32[144,128]{1,0:T(8,128)S(1)}, f32[144,128]{1,0:T(8,128)S(1)}, u32[]{:S(2)}, u32[]{:S(2)}) collective-permute-start(f32[144,128]{1,0:T(8,128)S(1)} %get-tuple-element.20.own_even_lat), channel_id=1, source_target_pairs={{0,1},{1,0},{2,3},{3,2},{4,5},{5,4},{6,7},{7,6},{8,9},{9,8},{10,11... | collective-permute-start | bytes 221192 | tf_op jit(solution)/shard_map/ppermute | solution.py:592
  33.5 0.0 collective-permute-done.2.odd_lat.got_odd_lat
  33.5 0.9 %collective-permute-done.3.even_lat.got_even_lat = f32[144,128]{1,0:T(8,128)S(1)} collective-permute-done((f32[144,128]{1,0:T(8,128)S(1)}, f32[144,128]{1,0:T(8,128)S(1)}, u32[]{:S(2)}, u32[]{:S(2)}) %collective-permute-start.3) | collective-permute-done | bytes 73760 | tf_op jit(solution)/shard_map/ppermute | solution.py:592
  34.4 0.0 collective-permute-done.odd_lon.got_odd
  34.4 0.0 collective-permute-done.1.even_lon.got_even
  34.4 0.3 shard_map.122
  34.7 5.0 %collective-permute-start.4 = (f32[80,128]{1,0:T(8,128)S(1)}, f32[80,128]{1,0:T(8,128)S(1)}, u32[]{:S(2)}, u32[]{:S(2)}) collective-permute-start(f32[80,128]{1,0:T(8,128)S(1)} %get-tuple-element.27.own_b), channel_id=1, source_target_pairs={{0,1016},{8,16},{16,8},{24,32},{32,24},{40,48},{48,40},{56,64},{64... | collective-permute-start | bytes 122888 | tf_op jit(solution)/shard_map/ppermute | solution.py:598
  39.7 1.9 %collective-permute-start.5 = (f32[80,128]{1,0:T(8,128)S(1)}, f32[80,128]{1,0:T(8,128)S(1)}, u32[]{:S(2)}, u32[]{:S(2)}) collective-permute-start(f32[80,128]{1,0:T(8,128)S(1)} %get-tuple-element.28), channel_id=1, source_target_pairs={{0,8},{8,0},{16,24},{24,16},{32,40},{40,32},{48,56},{56,48},{64,72... | collective-permute-start | bytes 122888 | tf_op jit(solution)/shard_map/ppermute | solution.py:599
  41.6 2.8 %shard_map.121 = (f32[62,8,128]{2,1,0:T(8,128)}, f32[62,8,128]{2,1,0:T(8,128)}, f32[62,8,128]{2,1,0:T(8,128)}, f32[62,8,128]{2,1,0:T(8,128)}) custom-call(s32[2,8,128]{2,1,0:T(8,128)S(1)} %broadcast_in_dim.2.parity, f32[4,66,8,128]{3,2,1,0:T(8,128)S(1)} %get-tuple-element.17.masked, f32[536,128]{1,0:T(8,128)S(1)} %get-tuple-element.18.own_lon.own_odd, ...), custom_call_target="tpu_custom_call" | custom-call | flops 10000000 | bytes 3047424 | tf_op jit(solution)/shard_map/pallas_call | solution.py:558
  44.4 0.4 collective-permute-done.4.odd_b
  44.8 0.8 %collective-permute-done.5.even_b = f32[80,128]{1,0:T(8,128)S(1)} collective-permute-done((f32[80,128]{1,0:T(8,128)S(1)}, f32[80,128]{1,0:T(8,128)S(1)}, u32[]{:S(2)}, u32[]{:S(2)}) %collective-permute-start.5) | collective-permute-done | bytes 40992 | tf_op jit(solution)/shard_map/ppermute | solution.py:599
  45.6 1.3 %shard_map.123 = f32[8,128]{1,0:T(8,128)} custom-call(s32[2,8,128]{2,1,0:T(8,128)S(1)} %broadcast_in_dim.2.parity, f32[80,128]{1,0:T(8,128)S(1)} %collective-permute-done.4.odd_b, f32[80,128]{1,0:T(8,128)S(1)} %collective-permute-done.5.even_b, f32[80,128]{1,0:T(8,128)S(1)} %get-tuple-element.27.own_b, f32[536,128]{1,0:T(8,128)S(1)} %get-tuple-element.18.own_lon.own_odd, ...), custom_call_target="tpu_custom_call" | custom-call | flops 1000000 | bytes 1000000 | tf_op jit(solution)/shard_map/pallas_call | solution.py:571
Async XLA Ops:
  2.3 32.1 %collective-permute-start = (f32[536,128]{1,0:T(8,128)S(1)}, f32[536,128]{1,0:T(8,128)S(1)}, u32[]{:S(2)}, u32[]{:S(2)}) collective-permute-start(f32[536,128]{1,0:T(8,128)S(1)} %get-tuple-element.18.own_lon.own_odd), channel_id=1, source_target_pairs={{0,1016},{8,16},{16,8},{24,32},{32,24},{40,48},{48,40},{56,64},{64... | collective-permute-start | bytes 823304 | tf_op jit(solution)/shard_map/ppermute | solution.py:589
  24.2 10.2 %collective-permute-start.1 = (f32[536,128]{1,0:T(8,128)S(1)}, f32[536,128]{1,0:T(8,128)S(1)}, u32[]{:S(2)}, u32[]{:S(2)}) collective-permute-start(f32[536,128]{1,0:T(8,128)S(1)} %get-tuple-element.21.own_even), channel_id=1, source_target_pairs={{0,8},{8,0},{16,24},{24,16},{32,40},{40,32},{48,56},{56,48},{64,72... | collective-permute-start | bytes 823304 | tf_op jit(solution)/shard_map/ppermute | solution.py:588
  26.8 6.7 %collective-permute-start.2 = (f32[144,128]{1,0:T(8,128)S(1)}, f32[144,128]{1,0:T(8,128)S(1)}, u32[]{:S(2)}, u32[]{:S(2)}) collective-permute-start(f32[144,128]{1,0:T(8,128)S(1)} %get-tuple-element.19.own_odd_lat), channel_id=1, source_target_pairs={{1,2},{2,1},{3,4},{4,3},{5,6},{6,5},{9,10},{10,9},{11,12},{12,11},... | collective-permute-start | bytes 221192 | tf_op jit(solution)/shard_map/ppermute | solution.py:591
  28.8 5.6 %collective-permute-start.3 = (f32[144,128]{1,0:T(8,128)S(1)}, f32[144,128]{1,0:T(8,128)S(1)}, u32[]{:S(2)}, u32[]{:S(2)}) collective-permute-start(f32[144,128]{1,0:T(8,128)S(1)} %get-tuple-element.20.own_even_lat), channel_id=1, source_target_pairs={{0,1},{1,0},{2,3},{3,2},{4,5},{5,4},{6,7},{7,6},{8,9},{9,8},{10,11... | collective-permute-start | bytes 221192 | tf_op jit(solution)/shard_map/ppermute | solution.py:592
  34.7 10.1 %collective-permute-start.4 = (f32[80,128]{1,0:T(8,128)S(1)}, f32[80,128]{1,0:T(8,128)S(1)}, u32[]{:S(2)}, u32[]{:S(2)}) collective-permute-start(f32[80,128]{1,0:T(8,128)S(1)} %get-tuple-element.27.own_b), channel_id=1, source_target_pairs={{0,1016},{8,16},{16,8},{24,32},{32,24},{40,48},{48,40},{56,64},{64... | collective-permute-start | bytes 122888 | tf_op jit(solution)/shard_map/ppermute | solution.py:598
  39.7 5.9 %collective-permute-start.5 = (f32[80,128]{1,0:T(8,128)S(1)}, f32[80,128]{1,0:T(8,128)S(1)}, u32[]{:S(2)}, u32[]{:S(2)}) collective-permute-start(f32[80,128]{1,0:T(8,128)S(1)} %get-tuple-element.28), channel_id=1, source_target_pairs={{0,8},{8,0},{16,24},{24,16},{32,40},{40,32},{48,56},{56,48},{64,72... | collective-permute-start | bytes 122888 | tf_op jit(solution)/shard_map/ppermute | solution.py:599

commit v9 on v8

--- a/solution.py
+++ b/solution.py
@@ -16,7 +16,7 @@
 FLAT = 4 * STRIP
 LON_ROWS = FLAT + 3 * ROWS
 LAT_ROWS = 18 * ROWS
-SOLVE_ROWS = 5 * ROWS + 5 * ROWS
+SOLVE_ROWS = 3 * ROWS + 5 * ROWS
 VMEM = 12 * 1024 * 1024
 
 F32 = jnp.float32
@@ -45,8 +45,8 @@
     return 0.7 * t - 0.5 * s
 
 
-def even(axis):
-    return lax.axis_index(axis) % 2 == 0
+def is_even_over(axis):
+    return lax.axis_index(axis) & 1 == 0
 
 
 def flat_of(ref, base=FLAT):
@@ -54,7 +54,7 @@
 
 
 def pack_lon(
-    u, v, t, s, water, layers, diag, elev, parity, masked, up_first, low_first, held, held_int, held_flat, sems
+    u, v, t, s, water, layers, diag, elev, masked, up_first, low_first, held, held_int, held_flat, sems
 ):
     copies = [
         pltpu.make_async_copy(src, held.at[i], sems.at[i]) for i, src in enumerate((u, v, t, s))
@@ -72,7 +72,7 @@
     row = rows_of()
     group = row >> 1
     depth = held_int[0] * held_int[1]
-    is_even = parity[0] == 0
+    is_even = is_even_over("lon")
 
     for f in range(4):
         masked[f, 0] = jnp.zeros((ROWS, LANES), F32)
@@ -123,13 +123,13 @@
     return jnp.dot(jnp.concatenate([high, rest], axis=1), matrix, preferred_element_type=F32)
 
 
-def pack_lat(masked, own_lon, parity, odd_out, even_out, partial):
+def pack_lat(masked, own_lon, odd_out, even_out, partial):
     row, lane = rows_of(), lanes_of()
     high, low = lane >> 4, ((lane - 8) & 127) >> 4
     in_even = (lane & 8) == 0
     elev, diag, depth = flat_of(own_lon)
     levels = depth.astype(jnp.int32)
-    is_even = parity[1] == 0
+    is_even = is_even_over("lat")
     zero = jnp.zeros((ROWS, LANES), F32)
     matrix = lat_matrix()
     left, right = tile_lanes(depth), tile_lanes(by_lanes(depth, 8))
@@ -227,12 +227,12 @@
 
 
 def forcing(
-    parity, got_even, got_odd, own_odd, own_even,
+    got_even, got_odd, own_odd, own_even,
     own_odd_lat, own_even_lat, got_odd_lat, got_even_lat, partial,
     odd_out, even_out,
 ):
     row, lane = rows_of(), lanes_of()
-    lon_even, lat_even = parity[0] == 0, parity[1] == 0
+    lon_even, lat_even = is_even_over("lon"), is_even_over("lat")
     elev, diag, depth = flat_of(own_odd)
     total = elev + partial[...]
 
@@ -299,8 +299,13 @@
     total_side = side(0) + elev_side
     total_side = total_side + jnp.where(lane < 2, miss_ext_r, 0.0)
     total_side = total_side + jnp.where(lane >= 126, miss_ext_l, 0.0)
+    slot = lane >> 3
+    sides = jnp.zeros((ROWS, LANES), F32)
+    for i in range(3):
+        sides = jnp.where(slot == 2 * i, by_lanes(flat_r, 8 * i - 8), sides)
+        sides = jnp.where(slot == (2 * i - 1) % 16, by_lanes(flat_l, 8 * i + 112), sides)
     for ref in (odd_out, even_out):
-        for i, x in enumerate((total, total_side, elev_side, side(2), side(3))):
+        for i, x in enumerate((total, total_side, sides)):
             ref[8 * i : 8 * i + 8, :] = x
     packs = ext_r[0] + ext_l[0] + w_r + w_l + [depth_r, depth_l]
     group = row >> 1
@@ -309,7 +314,7 @@
         for j, x in enumerate(packs[4 * i : 4 * i + 4]):
             top = jnp.where(group == j, by_rows(x, 2 * j), top)
             bottom = jnp.where(group == j, by_rows(x, 2 * j - 6), bottom)
-        at = slice(40 + 8 * i, 48 + 8 * i)
+        at = slice(24 + 8 * i, 32 + 8 * i)
         odd_out[at, :] = jnp.where(lon_even, top, bottom)
         even_out[at, :] = jnp.where(lon_even, bottom, top)
 
@@ -318,12 +323,12 @@
 
 
 def fields(
-    parity, masked, own_lon, own_odd_lat, own_even_lat, odd_lon, even_lon, odd_lat, even_lat,
+    masked, own_lon, own_odd_lat, own_even_lat, odd_lon, even_lon, odd_lat, even_lat,
     o1, o2, o3, o4, terms, rims, fresh, sems,
 ):
     row, lane = rows_of(), lanes_of()
     levels = flat_of(own_lon)[2].astype(jnp.int32)
-    lon_even, lat_even = parity[0] == 0, parity[1] == 0
+    lon_even, lat_even = is_even_over("lon"), is_even_over("lat")
     outs = (o1, o2, o3, o4)
     at_edge = (lane < 2) | (lane >= 126)
 
@@ -405,13 +410,13 @@
 
 
 def solve(
-    parity, odd_b, even_b, own_b, own_lon, odd_lon, even_lon, odd_lat, even_lat, height
+    odd_b, even_b, own_b, own_lon, odd_lon, even_lon, odd_lat, even_lat, height
 ):
     row, lane = rows_of(), lanes_of()
-    lon_even, lat_even = parity[0] == 0, parity[1] == 0
-    lower = [jnp.where(lon_even, odd_b[8 * i : 8 * i + 8, :], even_b[8 * i : 8 * i + 8, :]) for i in range(10)]
-    upper = [jnp.where(lon_even, even_b[8 * i : 8 * i + 8, :], odd_b[8 * i : 8 * i + 8, :]) for i in range(10)]
-    own = [own_b[8 * i : 8 * i + 8, :] for i in range(5)]
+    lon_even, lat_even = is_even_over("lon"), is_even_over("lat")
+    lower = [jnp.where(lon_even, odd_b[8 * i : 8 * i + 8, :], even_b[8 * i : 8 * i + 8, :]) for i in range(8)]
+    upper = [jnp.where(lon_even, even_b[8 * i : 8 * i + 8, :], odd_b[8 * i : 8 * i + 8, :]) for i in range(8)]
+    own = [own_b[8 * i : 8 * i + 8, :] for i in range(3)]
 
     ext_r = [four(even_lat, f * 32, lat_even, odd_lat) for f in (0, 2, 3)]
     ext_l = [four(odd_lat, f * 32, lat_even, even_lat) for f in (0, 2, 3)]
@@ -423,7 +428,7 @@
         return 0.005 * jnp.where(wet, near, 0.0) - ADV * vel * slope
 
     def rim_rows(tile, q, first):
-        return by_rows(tile[5 + q // 4], first - 2 * (q % 4))
+        return by_rows(tile[3 + q // 4], first - 2 * (q % 4))
 
     def near_rows(q):
         return jnp.where(row < 4, rim_rows(upper, q, 0), rim_rows(lower, q, 6))
@@ -460,9 +465,13 @@
         own[1] + mine,
         upper[1] + jnp.where(row < 2, theirs, 0.0),
     ]
-    elev = [flat_low[0], flat_own[0], flat_up[0], lower[2], own[2], upper[2]]
-    diag = [flat_low[1], flat_own[1], flat_up[1], lower[3], own[3], upper[3]]
-    wet = [x > 0.0 for x in (flat_low[2], flat_own[2], flat_up[2], lower[4], own[4], upper[4])]
+    sides = [
+        [jnp.where(in_r | in_l, by_lanes(x[2], -16 * i), 0.0) for x in (lower, own, upper)]
+        for i in range(3)
+    ]
+    elev = [flat_low[0], flat_own[0], flat_up[0]] + sides[0]
+    diag = [flat_low[1], flat_own[1], flat_up[1]] + sides[1]
+    wet = [x > 0.0 for x in [flat_low[2], flat_own[2], flat_up[2]] + sides[2]]
     diag = [x + 4.0 for x in diag]
     inverse = [1.0 / x for x in diag]
     coupled = [jnp.where(a, x, 0.0) for a, x in zip(wet, inverse, strict=True)]
@@ -530,7 +539,7 @@
     return call(
         pack_lon,
         (shaped(4, LEVELS + 4, ROWS, LANES), shaped(LON_ROWS, LANES), shaped(LON_ROWS, LANES)),
-        [HERE] * 8 + [WHOLE], 10**6, 2 * BLOCK,
+        [HERE] * 8, 10**6, 2 * BLOCK,
         out_specs=(WHOLE,) * 3,
         scratch_shapes=[
             pltpu.VMEM((4, LEVELS, ROWS, LANES), F32),
@@ -544,19 +553,19 @@
 def call_pack_lat(*args):
     return call(
         pack_lat, (shaped(LAT_ROWS, LANES), shaped(LAT_ROWS, LANES), shaped(ROWS, LANES)),
-        [WHOLE] * 2 + [WHOLE], 4 * 10**6, BLOCK,
+        [WHOLE] * 2, 4 * 10**6, BLOCK,
     )(*args)
 
 
 def call_forcing(*args):
     return call(
-        forcing, (shaped(SOLVE_ROWS, LANES),) * 2, [WHOLE] + [WHOLE] * 9, 10**6, 10**6
+        forcing, (shaped(SOLVE_ROWS, LANES),) * 2, [WHOLE] * 9, 10**6, 10**6
     )(*args)
 
 
 def call_fields(*args):
     return call(
-        fields, (shaped(LEVELS, ROWS, LANES),) * 4, [WHOLE] + [WHOLE] * 8, 10**7, 3 * BLOCK,
+        fields, (shaped(LEVELS, ROWS, LANES),) * 4, [WHOLE] * 8, 10**7, 3 * BLOCK,
         out_specs=(HERE,) * 4,
         scratch_shapes=[
             pltpu.VMEM((4, LEVELS * ROWS, 2 * LANES), F32),
@@ -568,7 +577,7 @@
 
 
 def call_solve(*args):
-    return call(solve, shaped(ROWS, LANES), [WHOLE] + [WHOLE] * 8, 10**6, 10**6)(*args)
+    return call(solve, shaped(ROWS, LANES), [WHOLE] * 8, 10**6, 10**6)(*args)
 
 
 def on_device(u, v, t, s, water, layers, diag, elev):
@@ -577,32 +586,30 @@
     lon_odd = [(i, (((i + 1) ^ 1) - 1) % lon) for i in range(lon)]
     lat_even = [(i, i ^ 1) for i in range(lat)]
     lat_odd = [(i, ((i + 1) ^ 1) - 1) for i in range(1, lat - 1)]
-    odd = jnp.stack([lax.axis_index("lon") & 1, lax.axis_index("lat") & 1]).astype(jnp.int32)
-    parity = jnp.broadcast_to(odd[:, None, None], (2, ROWS, LANES))
 
     raw = [
         pltpu.with_memory_space_constraint(x, pltpu.HBM)
         for x in (u, v, t, s, water, layers, diag, elev)
     ]
-    masked, own_odd, own_even = call_pack_lon(*raw, parity)
+    masked, own_odd, own_even = call_pack_lon(*raw)
     got_even = lax.ppermute(own_even, "lon", lon_even)
     got_odd = lax.ppermute(own_odd, "lon", lon_odd)
-    lat_own_odd, lat_own_even, partial = call_pack_lat(masked, own_odd, parity)
+    lat_own_odd, lat_own_even, partial = call_pack_lat(masked, own_odd)
     lat_got_odd = lax.ppermute(lat_own_odd, "lat", lat_odd)
     lat_got_even = lax.ppermute(lat_own_even, "lat", lat_even)
 
     b_odd, b_even = call_forcing(
-        parity, got_even, got_odd, own_odd, own_even,
+        got_even, got_odd, own_odd, own_even,
         lat_own_odd, lat_own_even, lat_got_odd, lat_got_even, partial,
     )
     b_got_odd = lax.ppermute(b_odd, "lon", lon_odd)
     b_got_even = lax.ppermute(b_even, "lon", lon_even)
 
     fresh = call_fields(
-        parity, masked, own_odd, lat_own_odd, lat_own_even, got_odd, got_even, lat_got_odd, lat_got_even
+        masked, own_odd, lat_own_odd, lat_own_even, got_odd, got_even, lat_got_odd, lat_got_even
     )
     height = call_solve(
-        parity, b_got_odd, b_got_even, b_odd, own_odd, got_odd, got_even, lat_got_odd, lat_got_even
+        b_got_odd, b_got_even, b_odd, own_odd, got_odd, got_even, lat_got_odd, lat_got_even
     )
     return (*fresh, height)
 

time: 47.2 us -> 47 us (level)
  no operation moved by 1% of the time
where the time goes in v9:
time: 47 us; the launch traced here: 46.7 us
  starting transfers between devices  37.5 us (80%)
  Pallas kernels  6.34 us (13%)
  waiting for transfers between devices  2.14 us (5%)
  between operations  0.72 us (2%)
    ppermute x1, starting transfers between devices, on_device(): got_odd = lax.ppermute(own_odd, 'lon', lon_odd)  21.9 us
    ppermute x1, starting transfers between devices, on_device(): b_got_odd = lax.ppermute(b_odd, 'lon', lon_odd)  5.03 us
    ppermute x1, starting transfers between devices, on_device(): lat_got_even = lax.ppermute(lat_own_even, 'lat', lat_even)  4.74 us
    pallas_call x1, Pallas kernels, call_fields(): call(fields, (shaped(LEVELS, ROWS, LANES),) * 4, [WHOLE] * 8, 10 ** 7, 3...  2.62 us
    ppermute x1, starting transfers between devices, on_device(): got_even = lax.ppermute(own_even, 'lon', lon_even)  1.92 us
    ppermute x1, starting transfers between devices, on_device(): lat_got_odd = lax.ppermute(lat_own_odd, 'lat', lat_odd)  1.92 us
    ppermute x1, starting transfers between devices, on_device(): b_got_even = lax.ppermute(b_even, 'lon', lon_even)  1.92 us
    pallas_call x1, Pallas kernels, call_pack_lon(): call(pack_lon, (shaped(4, LEVELS + 4, ROWS, LANES), shaped(LON_ROWS, LANE...  1.47 us
  transfers between devices with their start and end apart: 6, of which 3 were waited for; matrix products, arithmetic and copies ran while one was open for 0% of the time, Pallas kernels for 7%

profile of v9, /device:TPU:4, one launch (start us, length us, event | category | flops | bytes accessed | tf_op | source)
XLA Modules:
  0.0 46.7 jit_solution(2964081822199716776)
XLA Ops:
  0.6 1.5 %shard_map.119 = (f32[4,66,8,128]{3,2,1,0:T(8,128)S(1)}, f32[536,128]{1,0:T(8,128)S(1)}, f32[536,128]{1,0:T(8,128)S(1)}) custom-call(f32[62,8,128]{2,1,0:T(8,128)} %u.1, f32[62,8,128]{2,1,0:T(8,128)} %v.1, f32[62,8,128]{2,1,0:T(8,128)} %t.1, f32[62,8,128]{2,1,0:T(8,128)} %s.1, s32[8,128]{1,0:T(8,128)} %water.1, s32[8,128]{1,0:T(8,128)} %layers.1, ...), custom_call_target="tpu_custom_call" | custom-call | flops 1000000 | bytes 2031616 | tf_op jit(solution)/shard_map/pallas_call | solution.py:539
  2.1 21.9 %collective-permute-start = (f32[536,128]{1,0:T(8,128)S(1)}, f32[536,128]{1,0:T(8,128)S(1)}, u32[]{:S(2)}, u32[]{:S(2)}) collective-permute-start(f32[536,128]{1,0:T(8,128)S(1)} %get-tuple-element.18.own_lon.own_odd), channel_id=1, source_target_pairs={{0,1016},{8,16},{16,8},{24,32},{32,24},{40,48},{48,40},{56,64},{64... | collective-permute-start | bytes 823304 | tf_op jit(solution)/shard_map/ppermute | solution.py:596
  24.1 1.9 %collective-permute-start.1 = (f32[536,128]{1,0:T(8,128)S(1)}, f32[536,128]{1,0:T(8,128)S(1)}, u32[]{:S(2)}, u32[]{:S(2)}) collective-permute-start(f32[536,128]{1,0:T(8,128)S(1)} %get-tuple-element.21.own_even), channel_id=1, source_target_pairs={{0,8},{8,0},{16,24},{24,16},{32,40},{40,32},{48,56},{56,48},{64,72... | collective-permute-start | bytes 823304 | tf_op jit(solution)/shard_map/ppermute | solution.py:595
  26.0 0.7 %shard_map.120 = (f32[144,128]{1,0:T(8,128)S(1)}, f32[144,128]{1,0:T(8,128)S(1)}, f32[8,128]{1,0:T(8,128)S(1)}) custom-call(f32[4,66,8,128]{3,2,1,0:T(8,128)S(1)} %get-tuple-element.17.masked, f32[536,128]{1,0:T(8,128)S(1)} %get-tuple-element.18.own_lon.own_odd), custom_call_target="tpu_custom_call" | custom-call | flops 4000000 | bytes 1015808 | tf_op jit(solution)/shard_map/pallas_call | solution.py:554
  26.7 1.9 %collective-permute-start.2 = (f32[144,128]{1,0:T(8,128)S(1)}, f32[144,128]{1,0:T(8,128)S(1)}, u32[]{:S(2)}, u32[]{:S(2)}) collective-permute-start(f32[144,128]{1,0:T(8,128)S(1)} %get-tuple-element.19.own_odd_lat), channel_id=1, source_target_pairs={{1,2},{2,1},{3,4},{4,3},{5,6},{6,5},{9,10},{10,9},{11,12},{12,11},... | collective-permute-start | bytes 221192 | tf_op jit(solution)/shard_map/ppermute | solution.py:598
  28.6 4.7 %collective-permute-start.3 = (f32[144,128]{1,0:T(8,128)S(1)}, f32[144,128]{1,0:T(8,128)S(1)}, u32[]{:S(2)}, u32[]{:S(2)}) collective-permute-start(f32[144,128]{1,0:T(8,128)S(1)} %get-tuple-element.20.own_even_lat), channel_id=1, source_target_pairs={{0,1},{1,0},{2,3},{3,2},{4,5},{5,4},{6,7},{7,6},{8,9},{9,8},{10,11... | collective-permute-start | bytes 221192 | tf_op jit(solution)/shard_map/ppermute | solution.py:599
  33.3 0.0 collective-permute-done.2.odd_lat.got_odd_lat
  33.3 0.9 %collective-permute-done.3.even_lat.got_even_lat = f32[144,128]{1,0:T(8,128)S(1)} collective-permute-done((f32[144,128]{1,0:T(8,128)S(1)}, f32[144,128]{1,0:T(8,128)S(1)}, u32[]{:S(2)}, u32[]{:S(2)}) %collective-permute-start.3) | collective-permute-done | bytes 73760 | tf_op jit(solution)/shard_map/ppermute | solution.py:599
  34.2 0.0 collective-permute-done.odd_lon.got_odd
  34.2 0.0 collective-permute-done.1.even_lon.got_even
  34.2 0.3 shard_map.122
  34.5 5.0 %collective-permute-start.4 = (f32[64,128]{1,0:T(8,128)S(1)}, f32[64,128]{1,0:T(8,128)S(1)}, u32[]{:S(2)}, u32[]{:S(2)}) collective-permute-start(f32[64,128]{1,0:T(8,128)S(1)} %get-tuple-element.27.own_b), channel_id=1, source_target_pairs={{0,1016},{8,16},{16,8},{24,32},{32,24},{40,48},{48,40},{56,64},{64... | collective-permute-start | bytes 98312 | tf_op jit(solution)/shard_map/ppermute | solution.py:605
  39.5 1.9 %collective-permute-start.5 = (f32[64,128]{1,0:T(8,128)S(1)}, f32[64,128]{1,0:T(8,128)S(1)}, u32[]{:S(2)}, u32[]{:S(2)}) collective-permute-start(f32[64,128]{1,0:T(8,128)S(1)} %get-tuple-element.28), channel_id=1, source_target_pairs={{0,8},{8,0},{16,24},{24,16},{32,40},{40,32},{48,56},{56,48},{64,72... | collective-permute-start | bytes 98312 | tf_op jit(solution)/shard_map/ppermute | solution.py:606
  41.5 2.6 %shard_map.121 = (f32[62,8,128]{2,1,0:T(8,128)}, f32[62,8,128]{2,1,0:T(8,128)}, f32[62,8,128]{2,1,0:T(8,128)}, f32[62,8,128]{2,1,0:T(8,128)}) custom-call(f32[4,66,8,128]{3,2,1,0:T(8,128)S(1)} %get-tuple-element.17.masked, f32[536,128]{1,0:T(8,128)S(1)} %get-tuple-element.18.own_lon.own_odd, f32[144,128]{1,0:T(8,128)S(1)} %get-tuple-element.19.own_odd_lat, ...), custom_call_target="tpu_custom_call" | custom-call | flops 10000000 | bytes 3047424 | tf_op jit(solution)/shard_map/pallas_call | solution.py:567
  44.1 0.4 collective-permute-done.4.odd_b
  44.5 0.8 %collective-permute-done.5.even_b = f32[64,128]{1,0:T(8,128)S(1)} collective-permute-done((f32[64,128]{1,0:T(8,128)S(1)}, f32[64,128]{1,0:T(8,128)S(1)}, u32[]{:S(2)}, u32[]{:S(2)}) %collective-permute-start.5) | collective-permute-done | bytes 32800 | tf_op jit(solution)/shard_map/ppermute | solution.py:606
  45.4 1.3 %shard_map.123 = f32[8,128]{1,0:T(8,128)} custom-call(f32[64,128]{1,0:T(8,128)S(1)} %collective-permute-done.4.odd_b, f32[64,128]{1,0:T(8,128)S(1)} %collective-permute-done.5.even_b, f32[64,128]{1,0:T(8,128)S(1)} %get-tuple-element.27.own_b, f32[536,128]{1,0:T(8,128)S(1)} %get-tuple-element.18.own_lon.own_odd, ...), custom_call_target="tpu_custom_call" | custom-call | flops 1000000 | bytes 1000000 | tf_op jit(solution)/shard_map/pallas_call | solution.py:580
Async XLA Ops:
  2.1 32.1 %collective-permute-start = (f32[536,128]{1,0:T(8,128)S(1)}, f32[536,128]{1,0:T(8,128)S(1)}, u32[]{:S(2)}, u32[]{:S(2)}) collective-permute-start(f32[536,128]{1,0:T(8,128)S(1)} %get-tuple-element.18.own_lon.own_odd), channel_id=1, source_target_pairs={{0,1016},{8,16},{16,8},{24,32},{32,24},{40,48},{48,40},{56,64},{64... | collective-permute-start | bytes 823304 | tf_op jit(solution)/shard_map/ppermute | solution.py:596
  24.1 10.2 %collective-permute-start.1 = (f32[536,128]{1,0:T(8,128)S(1)}, f32[536,128]{1,0:T(8,128)S(1)}, u32[]{:S(2)}, u32[]{:S(2)}) collective-permute-start(f32[536,128]{1,0:T(8,128)S(1)} %get-tuple-element.21.own_even), channel_id=1, source_target_pairs={{0,8},{8,0},{16,24},{24,16},{32,40},{40,32},{48,56},{56,48},{64,72... | collective-permute-start | bytes 823304 | tf_op jit(solution)/shard_map/ppermute | solution.py:595
  26.7 6.7 %collective-permute-start.2 = (f32[144,128]{1,0:T(8,128)S(1)}, f32[144,128]{1,0:T(8,128)S(1)}, u32[]{:S(2)}, u32[]{:S(2)}) collective-permute-start(f32[144,128]{1,0:T(8,128)S(1)} %get-tuple-element.19.own_odd_lat), channel_id=1, source_target_pairs={{1,2},{2,1},{3,4},{4,3},{5,6},{6,5},{9,10},{10,9},{11,12},{12,11},... | collective-permute-start | bytes 221192 | tf_op jit(solution)/shard_map/ppermute | solution.py:598
  28.6 5.6 %collective-permute-start.3 = (f32[144,128]{1,0:T(8,128)S(1)}, f32[144,128]{1,0:T(8,128)S(1)}, u32[]{:S(2)}, u32[]{:S(2)}) collective-permute-start(f32[144,128]{1,0:T(8,128)S(1)} %get-tuple-element.20.own_even_lat), channel_id=1, source_target_pairs={{0,1},{1,0},{2,3},{3,2},{4,5},{5,4},{6,7},{7,6},{8,9},{9,8},{10,11... | collective-permute-start | bytes 221192 | tf_op jit(solution)/shard_map/ppermute | solution.py:599
  34.5 10.0 %collective-permute-start.4 = (f32[64,128]{1,0:T(8,128)S(1)}, f32[64,128]{1,0:T(8,128)S(1)}, u32[]{:S(2)}, u32[]{:S(2)}) collective-permute-start(f32[64,128]{1,0:T(8,128)S(1)} %get-tuple-element.27.own_b), channel_id=1, source_target_pairs={{0,1016},{8,16},{16,8},{24,32},{32,24},{40,48},{48,40},{56,64},{64... | collective-permute-start | bytes 98312 | tf_op jit(solution)/shard_map/ppermute | solution.py:605
  39.5 5.8 %collective-permute-start.5 = (f32[64,128]{1,0:T(8,128)S(1)}, f32[64,128]{1,0:T(8,128)S(1)}, u32[]{:S(2)}, u32[]{:S(2)}) collective-permute-start(f32[64,128]{1,0:T(8,128)S(1)} %get-tuple-element.28), channel_id=1, source_target_pairs={{0,8},{8,0},{16,24},{24,16},{32,40},{40,32},{48,56},{56,48},{64,72... | collective-permute-start | bytes 98312 | tf_op jit(solution)/shard_map/ppermute | solution.py:606

commit v10 on v9

--- a/solution.py
+++ b/solution.py
@@ -476,41 +476,66 @@
     inverse = [1.0 / x for x in diag]
     coupled = [jnp.where(a, x, 0.0) for a, x in zip(wet, inverse, strict=True)]
 
-    def neighbours(x):
-        out = []
+    def over_rows(x):
         up = [by_rows(y, -1) for y in x]
         down = [by_rows(y, 1) for y in x]
-        east = [by_lanes(y, -1) for y in x]
-        west = [by_lanes(y, 1) for y in x]
+        out = []
         for i in range(6):
             h, c = divmod(i, 3)
-            base = 3 * h
-            other = 3 * (1 - h) + c
-            n = jnp.where(row < 7, up[i], up[base + (c + 1) % 3])
-            p = jnp.where(row > 0, down[i], down[base + (c + 2) % 3])
-            e = jnp.where(lane < 127, east[i], east[other])
-            w = jnp.where(lane > 0, west[i], west[other])
-            out.append((n + p) + (e + w))
+            n = jnp.where(row < 7, up[i], up[3 * h + (c + 1) % 3])
+            p = jnp.where(row > 0, down[i], down[3 * h + (c + 2) % 3])
+            out.append(n + p)
         return out
+
+    def moved(x, d):
+        turned = [by_lanes(y, -d) for y in x]
+        inside = lane < LANES - d if d > 0 else lane >= -d
+        return [jnp.where(inside, turned[i], turned[(i + 3) % 6]) for i in range(6)]
+
+    def each(f, *xs):
+        return [f(*x) for x in zip(*xs, strict=True)]
 
     sigma = SPECTRUM_MID / SPECTRUM_HALF
     ratio = 1.0 / sigma
-    scaled = [x * y for x, y in zip(rhs, inverse, strict=True)]
+    factors = [(0.0, 1.0 / SPECTRUM_MID)]
+    for _ in range(ITERS - 1):
+        following = 1.0 / (2.0 * sigma - ratio)
+        factors.append((following * ratio, 2.0 * following / SPECTRUM_HALF))
+        ratio = following
+    scaled = each(lambda x, y: x * y, rhs, inverse)
     previous = elev
     iterate = elev[1]
-    for step in range(ITERS):
-        around = neighbours([jnp.where(a, x, 0.0) for a, x in zip(wet, previous, strict=True)])
-        scaled = [
-            (res - x) + c * n
-            for res, x, c, n in zip(scaled, previous, coupled, around, strict=True)
-        ]
-        if step == 0:
-            previous = [res / SPECTRUM_MID for res in scaled]
+    beside = [moved(coupled, 1), moved(coupled, -1)]
+
+    def masked(x, c):
+        return each(lambda y, k: jnp.where(k > 0.0, y, 0.0), x, c)
+
+    def advance(x, res, c, z, z_next, z_last, factor):
+        keep, gain = factor
+        near = over_rows(z)
+        res = each(
+            lambda r, y, k, n, e, w: (r - y) + k * (n + (e + w)), res, x, c, near, z_next, z_last
+        )
+        if keep:
+            x = each(lambda y, r: keep * y + gain * r, x, res)
         else:
-            following = 1.0 / (2.0 * sigma - ratio)
-            keep, gain = following * ratio, 2.0 * following / SPECTRUM_HALF
-            previous = [keep * x + gain * res for x, res in zip(previous, scaled, strict=True)]
-            ratio = following
+            x = each(lambda r: gain * r, res)
+        return x, res
+
+    for step in range(0, ITERS, 2):
+        z = masked(previous, coupled)
+        east, west = moved(z, 1), moved(z, -1)
+        far = moved(z, 2), moved(z, -2)
+        r_east, r_west = moved(scaled, 1), moved(scaled, -1)
+        first, second = factors[step : step + 2]
+        previous, scaled = advance(previous, scaled, coupled, z, east, west, first)
+        iterate = iterate + previous[1]
+        d_east, _ = advance(east, r_east, beside[0], east, far[0], z, first)
+        d_west, _ = advance(west, r_west, beside[1], west, z, far[1], first)
+        z = masked(previous, coupled)
+        previous, scaled = advance(
+            previous, scaled, coupled, z, masked(d_east, beside[0]), masked(d_west, beside[1]), second
+        )
         iterate = iterate + previous[1]
     height[...] = iterate
 

time: 47 us -> 46.9 us (level)
  no operation moved by 1% of the time
where the time goes in v10:
time: 46.9 us; the launch traced here: 46.6 us
  starting transfers between devices  37.5 us (80%)
  Pallas kernels  6.29 us (13%)
  waiting for transfers between devices  2.14 us (5%)
  between operations  0.72 us (2%)
    ppermute x1, starting transfers between devices, on_device(): got_odd = lax.ppermute(own_odd, 'lon', lon_odd)  21.9 us
    ppermute x1, starting transfers between devices, on_device(): b_got_odd = lax.ppermute(b_odd, 'lon', lon_odd)  5.03 us
    ppermute x1, starting transfers between devices, on_device(): lat_got_even = lax.ppermute(lat_own_even, 'lat', lat_even)  4.74 us
    pallas_call x1, Pallas kernels, call_fields(): call(fields, (shaped(LEVELS, ROWS, LANES),) * 4, [WHOLE] * 8, 10 ** 7, 3...  2.62 us
    ppermute x1, starting transfers between devices, on_device(): got_even = lax.ppermute(own_even, 'lon', lon_even)  1.92 us
    ppermute x1, starting transfers between devices, on_device(): lat_got_odd = lax.ppermute(lat_own_odd, 'lat', lat_odd)  1.92 us
    ppermute x1, starting transfers between devices, on_device(): b_got_even = lax.ppermute(b_even, 'lon', lon_even)  1.92 us
    pallas_call x1, Pallas kernels, call_pack_lon(): call(pack_lon, (shaped(4, LEVELS + 4, ROWS, LANES), shaped(LON_ROWS, LANE...  1.47 us
  transfers between devices with their start and end apart: 6, of which 3 were waited for; matrix products, arithmetic and copies ran while one was open for 0% of the time, Pallas kernels for 7%

profile of v10, /device:TPU:4, one launch (start us, length us, event | category | flops | bytes accessed | tf_op | source)
XLA Modules:
  0.0 46.6 jit_solution(9411221514931435064)
XLA Ops:
  0.6 1.5 %shard_map.119 = (f32[4,66,8,128]{3,2,1,0:T(8,128)S(1)}, f32[536,128]{1,0:T(8,128)S(1)}, f32[536,128]{1,0:T(8,128)S(1)}) custom-call(f32[62,8,128]{2,1,0:T(8,128)} %u.1, f32[62,8,128]{2,1,0:T(8,128)} %v.1, f32[62,8,128]{2,1,0:T(8,128)} %t.1, f32[62,8,128]{2,1,0:T(8,128)} %s.1, s32[8,128]{1,0:T(8,128)} %water.1, s32[8,128]{1,0:T(8,128)} %layers.1, ...), custom_call_target="tpu_custom_call" | custom-call | flops 1000000 | bytes 2031616 | tf_op jit(solution)/shard_map/pallas_call | solution.py:564
  2.1 21.9 %collective-permute-start = (f32[536,128]{1,0:T(8,128)S(1)}, f32[536,128]{1,0:T(8,128)S(1)}, u32[]{:S(2)}, u32[]{:S(2)}) collective-permute-start(f32[536,128]{1,0:T(8,128)S(1)} %get-tuple-element.18.own_lon.own_odd), channel_id=1, source_target_pairs={{0,1016},{8,16},{16,8},{24,32},{32,24},{40,48},{48,40},{56,64},{64... | collective-permute-start | bytes 823304 | tf_op jit(solution)/shard_map/ppermute | solution.py:621
  24.1 1.9 %collective-permute-start.1 = (f32[536,128]{1,0:T(8,128)S(1)}, f32[536,128]{1,0:T(8,128)S(1)}, u32[]{:S(2)}, u32[]{:S(2)}) collective-permute-start(f32[536,128]{1,0:T(8,128)S(1)} %get-tuple-element.21.own_even), channel_id=1, source_target_pairs={{0,8},{8,0},{16,24},{24,16},{32,40},{40,32},{48,56},{56,48},{64,72... | collective-permute-start | bytes 823304 | tf_op jit(solution)/shard_map/ppermute | solution.py:620
  26.0 0.7 %shard_map.120 = (f32[144,128]{1,0:T(8,128)S(1)}, f32[144,128]{1,0:T(8,128)S(1)}, f32[8,128]{1,0:T(8,128)S(1)}) custom-call(f32[4,66,8,128]{3,2,1,0:T(8,128)S(1)} %get-tuple-element.17.masked, f32[536,128]{1,0:T(8,128)S(1)} %get-tuple-element.18.own_lon.own_odd), custom_call_target="tpu_custom_call" | custom-call | flops 4000000 | bytes 1015808 | tf_op jit(solution)/shard_map/pallas_call | solution.py:579
  26.7 1.9 %collective-permute-start.2 = (f32[144,128]{1,0:T(8,128)S(1)}, f32[144,128]{1,0:T(8,128)S(1)}, u32[]{:S(2)}, u32[]{:S(2)}) collective-permute-start(f32[144,128]{1,0:T(8,128)S(1)} %get-tuple-element.19.own_odd_lat), channel_id=1, source_target_pairs={{1,2},{2,1},{3,4},{4,3},{5,6},{6,5},{9,10},{10,9},{11,12},{12,11},... | collective-permute-start | bytes 221192 | tf_op jit(solution)/shard_map/ppermute | solution.py:623
  28.6 4.7 %collective-permute-start.3 = (f32[144,128]{1,0:T(8,128)S(1)}, f32[144,128]{1,0:T(8,128)S(1)}, u32[]{:S(2)}, u32[]{:S(2)}) collective-permute-start(f32[144,128]{1,0:T(8,128)S(1)} %get-tuple-element.20.own_even_lat), channel_id=1, source_target_pairs={{0,1},{1,0},{2,3},{3,2},{4,5},{5,4},{6,7},{7,6},{8,9},{9,8},{10,11... | collective-permute-start | bytes 221192 | tf_op jit(solution)/shard_map/ppermute | solution.py:624
  33.3 0.0 collective-permute-done.2.odd_lat.got_odd_lat
  33.3 0.9 %collective-permute-done.3.even_lat.got_even_lat = f32[144,128]{1,0:T(8,128)S(1)} collective-permute-done((f32[144,128]{1,0:T(8,128)S(1)}, f32[144,128]{1,0:T(8,128)S(1)}, u32[]{:S(2)}, u32[]{:S(2)}) %collective-permute-start.3) | collective-permute-done | bytes 73760 | tf_op jit(solution)/shard_map/ppermute | solution.py:624
  34.2 0.0 collective-permute-done.odd_lon.got_odd
  34.2 0.0 collective-permute-done.1.even_lon.got_even
  34.2 0.3 shard_map.122
  34.5 5.0 %collective-permute-start.4 = (f32[64,128]{1,0:T(8,128)S(1)}, f32[64,128]{1,0:T(8,128)S(1)}, u32[]{:S(2)}, u32[]{:S(2)}) collective-permute-start(f32[64,128]{1,0:T(8,128)S(1)} %get-tuple-element.27.own_b), channel_id=1, source_target_pairs={{0,1016},{8,16},{16,8},{24,32},{32,24},{40,48},{48,40},{56,64},{64... | collective-permute-start | bytes 98312 | tf_op jit(solution)/shard_map/ppermute | solution.py:630
  39.5 1.9 %collective-permute-start.5 = (f32[64,128]{1,0:T(8,128)S(1)}, f32[64,128]{1,0:T(8,128)S(1)}, u32[]{:S(2)}, u32[]{:S(2)}) collective-permute-start(f32[64,128]{1,0:T(8,128)S(1)} %get-tuple-element.28), channel_id=1, source_target_pairs={{0,8},{8,0},{16,24},{24,16},{32,40},{40,32},{48,56},{56,48},{64,72... | collective-permute-start | bytes 98312 | tf_op jit(solution)/shard_map/ppermute | solution.py:631
  41.5 2.6 %shard_map.121 = (f32[62,8,128]{2,1,0:T(8,128)}, f32[62,8,128]{2,1,0:T(8,128)}, f32[62,8,128]{2,1,0:T(8,128)}, f32[62,8,128]{2,1,0:T(8,128)}) custom-call(f32[4,66,8,128]{3,2,1,0:T(8,128)S(1)} %get-tuple-element.17.masked, f32[536,128]{1,0:T(8,128)S(1)} %get-tuple-element.18.own_lon.own_odd, f32[144,128]{1,0:T(8,128)S(1)} %get-tuple-element.19.own_odd_lat, ...), custom_call_target="tpu_custom_call" | custom-call | flops 10000000 | bytes 3047424 | tf_op jit(solution)/shard_map/pallas_call | solution.py:592
  44.1 0.4 collective-permute-done.4.odd_b
  44.5 0.8 %collective-permute-done.5.even_b = f32[64,128]{1,0:T(8,128)S(1)} collective-permute-done((f32[64,128]{1,0:T(8,128)S(1)}, f32[64,128]{1,0:T(8,128)S(1)}, u32[]{:S(2)}, u32[]{:S(2)}) %collective-permute-start.5) | collective-permute-done | bytes 32800 | tf_op jit(solution)/shard_map/ppermute | solution.py:631
  45.4 1.3 %shard_map.123 = f32[8,128]{1,0:T(8,128)} custom-call(f32[64,128]{1,0:T(8,128)S(1)} %collective-permute-done.4.odd_b, f32[64,128]{1,0:T(8,128)S(1)} %collective-permute-done.5.even_b, f32[64,128]{1,0:T(8,128)S(1)} %get-tuple-element.27.own_b, f32[536,128]{1,0:T(8,128)S(1)} %get-tuple-element.18.own_lon.own_odd, ...), custom_call_target="tpu_custom_call" | custom-call | flops 1000000 | bytes 1000000 | tf_op jit(solution)/shard_map/pallas_call | solution.py:605
Async XLA Ops:
  2.1 32.1 %collective-permute-start = (f32[536,128]{1,0:T(8,128)S(1)}, f32[536,128]{1,0:T(8,128)S(1)}, u32[]{:S(2)}, u32[]{:S(2)}) collective-permute-start(f32[536,128]{1,0:T(8,128)S(1)} %get-tuple-element.18.own_lon.own_odd), channel_id=1, source_target_pairs={{0,1016},{8,16},{16,8},{24,32},{32,24},{40,48},{48,40},{56,64},{64... | collective-permute-start | bytes 823304 | tf_op jit(solution)/shard_map/ppermute | solution.py:621
  24.1 10.2 %collective-permute-start.1 = (f32[536,128]{1,0:T(8,128)S(1)}, f32[536,128]{1,0:T(8,128)S(1)}, u32[]{:S(2)}, u32[]{:S(2)}) collective-permute-start(f32[536,128]{1,0:T(8,128)S(1)} %get-tuple-element.21.own_even), channel_id=1, source_target_pairs={{0,8},{8,0},{16,24},{24,16},{32,40},{40,32},{48,56},{56,48},{64,72... | collective-permute-start | bytes 823304 | tf_op jit(solution)/shard_map/ppermute | solution.py:620
  26.7 6.7 %collective-permute-start.2 = (f32[144,128]{1,0:T(8,128)S(1)}, f32[144,128]{1,0:T(8,128)S(1)}, u32[]{:S(2)}, u32[]{:S(2)}) collective-permute-start(f32[144,128]{1,0:T(8,128)S(1)} %get-tuple-element.19.own_odd_lat), channel_id=1, source_target_pairs={{1,2},{2,1},{3,4},{4,3},{5,6},{6,5},{9,10},{10,9},{11,12},{12,11},... | collective-permute-start | bytes 221192 | tf_op jit(solution)/shard_map/ppermute | solution.py:623
  28.6 5.6 %collective-permute-start.3 = (f32[144,128]{1,0:T(8,128)S(1)}, f32[144,128]{1,0:T(8,128)S(1)}, u32[]{:S(2)}, u32[]{:S(2)}) collective-permute-start(f32[144,128]{1,0:T(8,128)S(1)} %get-tuple-element.20.own_even_lat), channel_id=1, source_target_pairs={{0,1},{1,0},{2,3},{3,2},{4,5},{5,4},{6,7},{7,6},{8,9},{9,8},{10,11... | collective-permute-start | bytes 221192 | tf_op jit(solution)/shard_map/ppermute | solution.py:624
  34.5 10.0 %collective-permute-start.4 = (f32[64,128]{1,0:T(8,128)S(1)}, f32[64,128]{1,0:T(8,128)S(1)}, u32[]{:S(2)}, u32[]{:S(2)}) collective-permute-start(f32[64,128]{1,0:T(8,128)S(1)} %get-tuple-element.27.own_b), channel_id=1, source_target_pairs={{0,1016},{8,16},{16,8},{24,32},{32,24},{40,48},{48,40},{56,64},{64... | collective-permute-start | bytes 98312 | tf_op jit(solution)/shard_map/ppermute | solution.py:630
  39.5 5.8 %collective-permute-start.5 = (f32[64,128]{1,0:T(8,128)S(1)}, f32[64,128]{1,0:T(8,128)S(1)}, u32[]{:S(2)}, u32[]{:S(2)}) collective-permute-start(f32[64,128]{1,0:T(8,128)S(1)} %get-tuple-element.28), channel_id=1, source_target_pairs={{0,8},{8,0},{16,24},{24,16},{32,40},{40,32},{48,56},{56,48},{64,72... | collective-permute-start | bytes 98312 | tf_op jit(solution)/shard_map/ppermute | solution.py:631
